TPU v7x, 512 devices: a whole 4x4x16 slice. The times are simulated.
512 devices in a mesh: section: 32 (over z, y_hi), tensor: 16 (over x, y_lo, core).
Axes of the slice: x: 4, y: 4 (y_hi: 2, y_lo: 2; y = y_hi * 2 + y_lo), z: 16, core: 2. Of those that a mesh axis runs over, the one named last changes fastest.
Arguments:
- section_input: bfloat16 [32, 128, 4096], P('section', None, 'tensor'), may hold values from -6 to 6
- section_grad: bfloat16 [32, 128, 4096], P('section', None, 'tensor'), may hold values from -6 to 6
- mirror_store: bfloat16 [32, 2, 128, 4096], P('section', None, None, 'tensor'), may hold values from -6 to 6
- fetch_slot: int32 [32], P('section'), may hold values from 0 to 1
- norm_gain: float32 [32, 4096], P('section'), may hold values from 0.25 to 4
- w_query: bfloat16 [32, 4096, 4096], P('section', None, 'tensor')
- w_keyval: bfloat16 [32, 1024, 4096], P('section', 'tensor')
- w_output: bfloat16 [32, 4096, 4096], P('section', 'tensor'), may hold values from -0.09375 to 0.09375
Outputs:
- forward_next: bfloat16 [32, 128, 4096], P('section', None, 'tensor')
- grad_prev: bfloat16 [32, 128, 4096], P('section', None, 'tensor')
- evicted: bfloat16 [32, 128, 4096], P('section', None, 'tensor')
All inputs are finite; a program needn't handle non-finite values.
Results may differ from a plain program's by a relative error of at most 0.023.
Values may be sent and summed in bfloat16 or wider, within the bound.
No kernel may reach another device: no remote copies, remote signals or barrier semaphores. Data moves between devices by JAX's collectives and lax.ppermute only.
A program may use at most 64 MiB of HBM per device.

v0:
```python
import jax
import jax.numpy as jnp
from jax import lax
from jax.sharding import PartitionSpec as P

HEADS = 32
KV_HEADS = 4
HEAD_DIM = 128


epsilon = 1e-05


def swapped(shard, axis, bit):
    return lax.ppermute(shard, axis, [(i, i ^ 1 << bit) for i in range(lax.axis_size(axis))])


def from_behind(block, axis, distance):
    devices = range(lax.axis_size(axis))
    route = [((i - distance) % len(devices), i) for i in devices]
    return lax.ppermute(block, axis, route)


def combine_terms(partial_value):
    summed = lax.psum(partial_value.astype(jnp.bfloat16), "tensor").astype(jnp.float32)
    return summed


def attend(layer_cols, gain_row, query_w, keyval_w):
    whole = lax.all_gather(layer_cols, "tensor", axis=1, tiled=True)
    count = whole.shape[0]
    per_dev = query_w.shape[1] // HEAD_DIM
    widened = whole.astype(jnp.float32)
    inverse = lax.rsqrt(jnp.mean(widened * widened, axis=-1, keepdims=True) + epsilon)
    normed = (widened * inverse * gain_row).astype(jnp.bfloat16)
    queries = jnp.dot(normed, query_w, preferred_element_type=jnp.float32).astype(jnp.bfloat16)
    kv_part = lax.dot_general(
        normed, keyval_w, (((1,), (1,)), ((), ())), preferred_element_type=jnp.float32
    ).astype(jnp.bfloat16)
    keyvals = lax.all_gather(kv_part, "tensor", axis=1, tiled=True)
    group = lax.axis_index("tensor") * per_dev // (HEADS // KV_HEADS)
    own_keys = lax.dynamic_slice_in_dim(keyvals, group * HEAD_DIM, HEAD_DIM, 1)
    own_values = lax.dynamic_slice_in_dim(
        keyvals, KV_HEADS * HEAD_DIM + group * HEAD_DIM, HEAD_DIM, 1
    )
    query_heads = queries.reshape(count, per_dev, HEAD_DIM)
    scores = jnp.einsum(
        "thd,sd->hts", query_heads, own_keys, preferred_element_type=jnp.float32
    ) * HEAD_DIM ** (-0.5)
    position = jnp.arange(count, dtype=jnp.int32)
    causal = position[:, None] >= position[None, :]
    scores = jnp.where(causal[None], scores, jnp.float32(-1e30))
    row_max = jnp.max(scores, axis=-1, keepdims=True)
    expval = jnp.exp(scores - row_max)
    probs = expval / jnp.sum(expval, axis=-1, keepdims=True)
    return (query_heads, own_keys, own_values, probs, group, widened, inverse)


def body(
    section_input, section_grad, mirror_store, fetch_slot, norm_gain, w_query, w_keyval, w_output
):
    x_cols = section_input[0]
    grad_cols = section_grad[0]
    gain_row = norm_gain[0]
    query_w = w_query[0]
    keyval_w = w_keyval[0]
    output_w = w_output[0]
    col_count = x_cols.shape[1]
    col_start = lax.axis_index("tensor") * col_count
    held_cols = mirror_store[0][fetch_slot[0]]
    stacked = jnp.stack([x_cols, held_cols])
    bit_count = lax.axis_size("section").bit_length() - 1
    for bit_pos in range(bit_count):
        stacked = swapped(stacked, "section", bit_pos)
    evicted_cols = stacked[0]
    fetched_cols = stacked[1]
    query_heads, own_keys, own_values, probs, group, widened, inverse = attend(
        x_cols, gain_row, query_w, keyval_w
    )
    count = probs.shape[1]
    mixed = jnp.einsum(
        "hts,sd->thd", probs.astype(jnp.bfloat16), own_values, preferred_element_type=jnp.float32
    ).astype(jnp.bfloat16)
    partial_value = jnp.dot(mixed.reshape(count, -1), output_w, preferred_element_type=jnp.float32)
    summed = combine_terms(partial_value)
    out_cols = lax.dynamic_slice_in_dim(summed, col_start, col_count, 1)
    layer_out = (x_cols.astype(jnp.float32) + out_cols).astype(jnp.bfloat16)
    forward_next = from_behind(layer_out, "section", 1)
    query_heads, own_keys, own_values, probs, group, widened, inverse = attend(
        fetched_cols, gain_row, query_w, keyval_w
    )
    score_scale = HEAD_DIM ** (-0.5)
    grad_whole = lax.all_gather(grad_cols, "tensor", axis=1, tiled=True)
    dmixed = lax.dot_general(
        grad_whole, output_w, (((1,), (1,)), ((), ())), preferred_element_type=jnp.float32
    ).astype(jnp.bfloat16)
    dmixed = dmixed.reshape(count, -1, HEAD_DIM)
    dprob = jnp.einsum("thd,sd->hts", dmixed, own_values, preferred_element_type=jnp.float32)
    row_dot = jnp.sum(probs * dprob, axis=-1, keepdims=True)
    dscore = (probs * (dprob - row_dot)).astype(jnp.bfloat16)
    dqueries = (
        jnp.einsum("hts,sd->thd", dscore, own_keys, preferred_element_type=jnp.float32)
        * score_scale
    ).astype(jnp.bfloat16)
    dkey = (
        jnp.einsum("hts,thd->sd", dscore, query_heads, preferred_element_type=jnp.float32)
        * score_scale
    )
    dval = jnp.einsum(
        "hts,thd->sd", probs.astype(jnp.bfloat16), dmixed, preferred_element_type=jnp.float32
    )
    columns = keyval_w.shape[0]
    blocks = lax.all_gather(
        jnp.concatenate([dkey, dval], axis=1).astype(jnp.bfloat16), "tensor", axis=1, tiled=True
    )
    ranks = lax.axis_size("tensor")
    grouped = (
        blocks.reshape(count, KV_HEADS, ranks // KV_HEADS, 2, HEAD_DIM)
        .astype(jnp.float32)
        .sum(axis=2)
    )
    layout = jnp.transpose(grouped, (0, 2, 1, 3)).reshape(count, 2 * KV_HEADS * HEAD_DIM)
    own_grads = lax.dynamic_slice_in_dim(
        layout, lax.axis_index("tensor") * columns, columns, 1
    ).astype(jnp.bfloat16)
    dterm = lax.dot_general(
        dqueries.reshape(count, -1),
        query_w,
        (((1,), (1,)), ((), ())),
        preferred_element_type=jnp.float32,
    )
    dterm = dterm + jnp.dot(own_grads, keyval_w, preferred_element_type=jnp.float32)
    dnormed = combine_terms(dterm)
    x_part = fetched_cols.astype(jnp.float32)
    scaled_full = gain_row * dnormed
    stat = jnp.mean(widened * scaled_full, axis=-1, keepdims=True)
    scaled = lax.dynamic_slice_in_dim(scaled_full, col_start, col_count, 1)
    dlayer = inverse * scaled - x_part * inverse**3 * stat
    grad_out = (grad_cols.astype(jnp.float32) + dlayer).astype(jnp.bfloat16)
    grad_prev = from_behind(grad_out, "section", -1)
    return (forward_next[None], grad_prev[None], evicted_cols[None])


def solution(mesh):
    placed = (
        P("section", None, "tensor"),
        P("section", None, "tensor"),
        P("section", None, None, "tensor"),
        P("section"),
        P("section", None),
        P("section", None, "tensor"),
        P("section", "tensor", None),
        P("section", "tensor", None),
    )
    return jax.shard_map(
        body,
        mesh=mesh,
        in_specs=placed,
        out_specs=(
            P("section", None, "tensor"),
            P("section", None, "tensor"),
            P("section", None, "tensor"),
        ),
        check_vma=False,
    )
```

profile of v0, /device:TPU:1, one launch (start us, length us, event | category | flops | bytes accessed | tf_op | source)
XLA Modules:
  0.0 387.0 jit_solution(9360222807303585544)
XLA Ops:
  11.1 5.7 %collective-permute-start.1 = (bf16[2,128,256]{2,1,0:T(8,128)(2,1)S(1)}, bf16[2,128,256]{2,1,0:T(8,128)(2,1)S(1)}, u32[]{:S(2)}, u32[]{:S(2)}) collective-permute-start(bf16[2,128,256]{2,1,0:T(8,128)(2,1)S(1)} %pad_maximum_fusion), channel_id=1, source_target_pairs={{0,16},{16,0},{32,48},{48,32},{64,80},{80,64},{96,112},{112,96},{1... | collective-permute-start | bytes 393224 | tf_op jit(solution)/shard_map/ppermute | solution.py:15
  16.7 2.3 collective-permute-done.1
  19.1 4.1 %collective-permute-start.2 = (bf16[2,128,256]{2,1,0:T(8,128)(2,1)S(1)}, bf16[2,128,256]{2,1,0:T(8,128)(2,1)S(1)}, u32[]{:S(2)}, u32[]{:S(2)}) collective-permute-start(bf16[2,128,256]{2,1,0:T(8,128)(2,1)S(1)} %collective-permute-done.1), channel_id=1, source_target_pairs={{0,32},{16,48},{32,0},{48,16},{64,96},{80,112},{96,64},{112,80},{1... | collective-permute-start | bytes 393224 | tf_op jit(solution)/shard_map/ppermute | solution.py:15
  23.2 2.6 collective-permute-done.2
  25.8 4.6 %collective-permute-start.3 = (bf16[2,128,256]{2,1,0:T(8,128)(2,1)S(1)}, bf16[2,128,256]{2,1,0:T(8,128)(2,1)S(1)}, u32[]{:S(2)}, u32[]{:S(2)}) collective-permute-start(bf16[2,128,256]{2,1,0:T(8,128)(2,1)S(1)} %collective-permute-done.2), channel_id=1, source_target_pairs={{0,64},{16,80},{32,96},{48,112},{64,0},{80,16},{96,32},{112,48},{1... | collective-permute-start | bytes 393224 | tf_op jit(solution)/shard_map/ppermute | solution.py:15
  30.4 3.8 collective-permute-done.3
  34.2 9.1 %collective-permute-start.4 = (bf16[2,128,256]{2,1,0:T(8,128)(2,1)S(1)}, bf16[2,128,256]{2,1,0:T(8,128)(2,1)S(1)}, u32[]{:S(2)}, u32[]{:S(2)}) collective-permute-start(bf16[2,128,256]{2,1,0:T(8,128)(2,1)S(1)} %collective-permute-done.3), channel_id=1, source_target_pairs={{0,128},{16,144},{32,160},{48,176},{64,192},{80,208},{96,224},{112... | collective-permute-start | bytes 393224 | tf_op jit(solution)/shard_map/ppermute | solution.py:15
  43.3 6.6 %collective-permute-done.4 = bf16[2,128,256]{2,1,0:T(8,128)(2,1)S(1)} collective-permute-done((bf16[2,128,256]{2,1,0:T(8,128)(2,1)S(1)}, bf16[2,128,256]{2,1,0:T(8,128)(2,1)S(1)}, u32[]{:S(2)}, u32[]{:S(2)}) %collective-permute-start.4) | collective-permute-done | bytes 131104 | tf_op jit(solution)/shard_map/ppermute | solution.py:15
  49.9 17.7 %collective-permute-start.5 = (bf16[2,128,256]{2,1,0:T(8,128)(2,1)S(1)}, bf16[2,128,256]{2,1,0:T(8,128)(2,1)S(1)}, u32[]{:S(2)}, u32[]{:S(2)}) collective-permute-start(bf16[2,128,256]{2,1,0:T(8,128)(2,1)S(1)} %collective-permute-done.4), channel_id=1, source_target_pairs={{0,256},{16,272},{32,288},{48,304},{64,320},{80,336},{96,352},{112... | collective-permute-start | bytes 393224 | tf_op jit(solution)/shard_map/ppermute | solution.py:15
  67.6 10.6 %collective-permute-done.5 = bf16[2,128,256]{2,1,0:T(8,128)(2,1)S(1)} collective-permute-done((bf16[2,128,256]{2,1,0:T(8,128)(2,1)S(1)}, bf16[2,128,256]{2,1,0:T(8,128)(2,1)S(1)}, u32[]{:S(2)}, u32[]{:S(2)}) %collective-permute-start.5) | collective-permute-done | bytes 131104 | tf_op jit(solution)/shard_map/ppermute | solution.py:15
  79.7 2.8 fusion.33
  82.6 18.9 %all-gather.10.cloned.1.call-done = bf16[1,128,4096]{2,1,0:T(8,128)(2,1)} async-done(((bf16[1,128,256]{2,1,0:T(8,128)(2,1)}), bf16[1,128,4096]{2,1,0:T(8,128)(2,1)}) %all-gather.10.cloned.1.call-update) | async-done | bytes 1048592 | tf_op jit(solution)/shard_map/all_gather | solution.py:30
  101.5 1.5 fusion.3
  103.5 42.5 %all-gather.12.cloned.1.call-done = bf16[1,128,4096]{2,1,0:T(8,128)(2,1)} async-done(((bf16[1,128,256]{2,1,0:T(8,128)(2,1)}), bf16[1,128,4096]{2,1,0:T(8,128)(2,1)}) %all-gather.12.cloned.1.call-update) | async-done | bytes 1048592 | tf_op jit(solution)/shard_map/all_gather | solution.py:30
  146.0 1.6 fusion.6
  148.2 1.9 convolution_convert_fusion.2
  150.1 18.8 %all_gather.21 = bf16[128,1024]{0,1:T(8,128)(2,1)S(1)} all-gather(bf16[128,64]{0,1:T(8,128)(2,1)S(1)} %convolution_convert_fusion.2), channel_id=1, replica_groups=mesh['section'=32,'tensor'=16] {'tensor'}, dimensions={1}, use_global_device_ids=true | all-gather | bytes 278528 | tf_op jit(solution)/shard_map/all_gather | solution.py:40
  171.0 1.5 fusion.104
  172.4 1.7 fusion.42
  177.9 2.0 convolution_convert_fusion.3
  179.9 18.4 %all_gather.19 = bf16[128,1024]{0,1:T(8,128)(2,1)} all-gather(bf16[128,64]{0,1:T(8,128)(2,1)S(1)} %convolution_convert_fusion.3), channel_id=1, replica_groups=mesh['section'=32,'tensor'=16] {'tensor'}, dimensions={1}, use_global_device_ids=true | all-gather | bytes 278528 | tf_op jit(solution)/shard_map/all_gather | solution.py:40
  198.8 1.6 fusion.99
  200.3 1.6 fusion.26
  203.1 3.1 convolution_convert_fusion
  206.4 2.2 fusion.13
  208.6 8.2 %all-gather.8.cloned.1.call-done = bf16[128,4096]{0,1:T(8,128)(2,1)} async-done(((bf16[128,256]{0,1:T(8,128)(2,1)}), bf16[128,4096]{0,1:T(8,128)(2,1)}) %all-gather.8.cloned.1.call-update) | async-done | bytes 1048592 | tf_op jit(solution)/shard_map/all_gather | solution.py:113
  218.2 3.0 fusion.2
  221.3 138.6 %all-reduce.3.cloned.1.call-done = (bf16[128,4096]{1,0:T(8,128)(2,1)}, bf16[128,4096]{1,0:T(8,128)(2,1)}) async-done(((bf16[128,4096]{1,0:T(8,128)(2,1)}, bf16[128,4096]{1,0:T(8,128)(2,1)}), (bf16[128,4096]{1,0:T(8,128)(2,1)}, bf16[128,4096]{1,0:T(8,128)(2,1)})) %all-reduce.3.cloned.1.call-update) | async-done | bytes 2097168 | tf_op jit(solution)/shard_map/psum | solution.py:25
  359.9 1.7 fusion.9
  361.8 7.9 %collective-permute-start.6 = (bf16[128,256]{1,0:T(8,128)(2,1)S(1)}, bf16[128,256]{1,0:T(8,128)(2,1)S(1)}, u32[]{:S(2)}, u32[]{:S(2)}) collective-permute-start(bf16[128,256]{1,0:T(8,128)(2,1)S(1)} %fusion.54), channel_id=1, source_target_pairs={{16,0},{32,16},{48,32},{64,48},{80,64},{96,80},{112,96},{128,112},... | collective-permute-start | bytes 196616 | tf_op jit(solution)/shard_map/ppermute | solution.py:21
  370.6 1.9 collective-permute-start
  372.5 6.7 %collective-permute-done = bf16[128,256]{1,0:T(8,128)(2,1)S(1)} collective-permute-done((bf16[128,256]{1,0:T(8,128)(2,1)S(1)}, bf16[128,256]{1,0:T(8,128)(2,1)S(1)}, u32[]{:S(2)}, u32[]{:S(2)}) %collective-permute-start) | collective-permute-done | bytes 65568 | tf_op jit(solution)/shard_map/ppermute | solution.py:21
  (65 shorter events, 17.2 us)
Async XLA Ops:
  7.2 161.7 %copy-start = (bf16[1,4096,256]{2,1,0:T(8,128)(2,1)S(1)}, bf16[1,4096,256]{2,1,0:T(8,128)(2,1)}, u32[]{:S(2)}) copy-start(bf16[1,4096,256]{2,1,0:T(8,128)(2,1)} %param.13) | copy-start | bytes 6291460
  7.2 72.5 %all-gather.14.cloned.1.call-start = ((), (), s32[]{:S(2)}) async-start(), calls=%async_computation.3 | async-start | bytes 1114112 | tf_op jit(solution)/shard_map/all_gather | solution.py:93
  7.9 93.6 %all-gather.10.cloned.1.call-start = ((), (), s32[]{:S(2)}) async-start(), calls=%async_computation.1 | async-start | bytes 1114112 | tf_op jit(solution)/shard_map/all_gather | solution.py:30
  8.7 137.3 %all-gather.12.cloned.1.call-start = ((), (), s32[]{:S(2)}) async-start(), calls=%async_computation.2 | async-start | bytes 1114112 | tf_op jit(solution)/shard_map/all_gather | solution.py:30
  11.1 8.0 %collective-permute-start.1 = (bf16[2,128,256]{2,1,0:T(8,128)(2,1)S(1)}, bf16[2,128,256]{2,1,0:T(8,128)(2,1)S(1)}, u32[]{:S(2)}, u32[]{:S(2)}) collective-permute-start(bf16[2,128,256]{2,1,0:T(8,128)(2,1)S(1)} %pad_maximum_fusion), channel_id=1, source_target_pairs={{0,16},{16,0},{32,48},{48,32},{64,80},{80,64},{96,112},{112,96},{1... | collective-permute-start | bytes 393224 | tf_op jit(solution)/shard_map/ppermute | solution.py:15
  19.1 6.8 %collective-permute-start.2 = (bf16[2,128,256]{2,1,0:T(8,128)(2,1)S(1)}, bf16[2,128,256]{2,1,0:T(8,128)(2,1)S(1)}, u32[]{:S(2)}, u32[]{:S(2)}) collective-permute-start(bf16[2,128,256]{2,1,0:T(8,128)(2,1)S(1)} %collective-permute-done.1), channel_id=1, source_target_pairs={{0,32},{16,48},{32,0},{48,16},{64,96},{80,112},{96,64},{112,80},{1... | collective-permute-start | bytes 393224 | tf_op jit(solution)/shard_map/ppermute | solution.py:15
  25.8 8.4 %collective-permute-start.3 = (bf16[2,128,256]{2,1,0:T(8,128)(2,1)S(1)}, bf16[2,128,256]{2,1,0:T(8,128)(2,1)S(1)}, u32[]{:S(2)}, u32[]{:S(2)}) collective-permute-start(bf16[2,128,256]{2,1,0:T(8,128)(2,1)S(1)} %collective-permute-done.2), channel_id=1, source_target_pairs={{0,64},{16,80},{32,96},{48,112},{64,0},{80,16},{96,32},{112,48},{1... | collective-permute-start | bytes 393224 | tf_op jit(solution)/shard_map/ppermute | solution.py:15
  34.2 15.7 %collective-permute-start.4 = (bf16[2,128,256]{2,1,0:T(8,128)(2,1)S(1)}, bf16[2,128,256]{2,1,0:T(8,128)(2,1)S(1)}, u32[]{:S(2)}, u32[]{:S(2)}) collective-permute-start(bf16[2,128,256]{2,1,0:T(8,128)(2,1)S(1)} %collective-permute-done.3), channel_id=1, source_target_pairs={{0,128},{16,144},{32,160},{48,176},{64,192},{80,208},{96,224},{112... | collective-permute-start | bytes 393224 | tf_op jit(solution)/shard_map/ppermute | solution.py:15
  49.9 28.3 %collective-permute-start.5 = (bf16[2,128,256]{2,1,0:T(8,128)(2,1)S(1)}, bf16[2,128,256]{2,1,0:T(8,128)(2,1)S(1)}, u32[]{:S(2)}, u32[]{:S(2)}) collective-permute-start(bf16[2,128,256]{2,1,0:T(8,128)(2,1)S(1)} %collective-permute-done.4), channel_id=1, source_target_pairs={{0,256},{16,272},{32,288},{48,304},{64,320},{80,336},{96,352},{112... | collective-permute-start | bytes 393224 | tf_op jit(solution)/shard_map/ppermute | solution.py:15
  78.2 0.6 copy-start.5
  79.6 137.2 %all-gather.8.cloned.1.call-start = ((), (), s32[]{:S(2)}) async-start(), calls=%async_computation | async-start | bytes 1114112 | tf_op jit(solution)/shard_map/all_gather | solution.py:113
  79.7 68.6 %copy-start.8 = (f32[1,4096]{1,0:T(1,128)S(1)}, f32[1,4096]{1,0:T(1,128)}, u32[]{:S(2)}) copy-start(f32[1,4096]{1,0:T(1,128)} %param.12) | copy-start | bytes 49156
  146.0 22.9 %copy-start.1 = (bf16[1,128,4096]{2,1,0:T(8,128)(2,1)S(1)}, bf16[1,128,4096]{2,1,0:T(8,128)(2,1)}, u32[]{:S(2)}) copy-start(bf16[1,128,4096]{2,1,0:T(8,128)(2,1)} %all-gather.12.cloned.1.call-done) | copy-start | bytes 3145732
  148.2 20.7 %copy-start.12 = (f32[128]{0:T(128)}, f32[128]{0:T(128)S(1)}, u32[]{:S(2)}) copy-start(f32[128]{0:T(128)S(1)} %get-tuple-element.10) | copy-start | bytes 1540
  177.8 182.1 %all-reduce.3.cloned.1.call-start = ((), (), s32[]{:S(2)}) async-start(), calls=%async_computation.4 | async-start | bytes 4194304 | tf_op jit(solution)/shard_map/psum | solution.py:25
  177.8 20.4 %copy-start.2 = (bf16[1,128,4096]{2,1,0:T(8,128)(2,1)S(1)}, bf16[1,128,4096]{2,1,0:T(8,128)(2,1)}, u32[]{:S(2)}) copy-start(bf16[1,128,4096]{2,1,0:T(8,128)(2,1)} %all-gather.10.cloned.1.call-done) | copy-start | bytes 3145732
  177.8 20.4 %copy-start.9 = (f32[1,4096]{1,0:T(1,128)S(1)}, f32[1,4096]{1,0:T(1,128)}, u32[]{:S(2)}) copy-start(f32[1,4096]{1,0:T(1,128)} %param.12) | copy-start | bytes 49156
  177.8 20.4 %copy-start.14 = (f32[128]{0:T(128)S(1)}, f32[128]{0:T(128)}, u32[]{:S(2)}) copy-start(f32[128]{0:T(128)} %add_rsqrt_fusion.1) | copy-start | bytes 1540
  216.7 1.5 copy-start.4
  218.2 141.6 %copy-start.10 = (f32[1,4096]{1,0:T(1,128)S(1)}, f32[1,4096]{1,0:T(1,128)}, u32[]{:S(2)}) copy-start(f32[1,4096]{1,0:T(1,128)} %param.12) | copy-start | bytes 49156
  359.9 1.8 copy-start.6
  359.9 1.8 copy-start.7
  359.9 1.8 copy-start.11
  359.9 1.8 copy-start.13
  359.9 9.8 %copy-start.3 = (bf16[1,128,256]{2,1,0:T(8,128)(2,1)S(1)}, bf16[1,128,256]{2,1,0:T(8,128)(2,1)}, u32[]{:S(2)}) copy-start(bf16[1,128,256]{2,1,0:T(8,128)(2,1)} %param.8) | copy-start | bytes 196612
  361.8 10.7 %collective-permute-start.6 = (bf16[128,256]{1,0:T(8,128)(2,1)S(1)}, bf16[128,256]{1,0:T(8,128)(2,1)S(1)}, u32[]{:S(2)}, u32[]{:S(2)}) collective-permute-start(bf16[128,256]{1,0:T(8,128)(2,1)S(1)} %fusion.54), channel_id=1, source_target_pairs={{16,0},{32,16},{48,32},{64,48},{80,64},{96,80},{112,96},{128,112},... | collective-permute-start | bytes 196616 | tf_op jit(solution)/shard_map/ppermute | solution.py:21
  370.6 8.6 %collective-permute-start = (bf16[128,256]{1,0:T(8,128)(2,1)S(1)}, bf16[128,256]{1,0:T(8,128)(2,1)S(1)}, u32[]{:S(2)}, u32[]{:S(2)}) collective-permute-start(bf16[128,256]{1,0:T(8,128)(2,1)S(1)} %fusion.55), channel_id=1, source_target_pairs={{496,0},{0,16},{16,32},{32,48},{48,64},{64,80},{80,96},{96,112},{1... | collective-permute-start | bytes 196616 | tf_op jit(solution)/shard_map/ppermute | solution.py:21
Sparse Core Ops, SparseCore 0:
  10.1 47.4 all-gather.13
  59.6 41.8 all-gather.9
  104.1 41.8 all-gather.11
  177.9 38.8 all-gather.7
  221.4 138.3 all-reduce.2
where the time goes:
time: 388 us; the launch traced here: 387 us
  waiting for transfers between devices  242 us (62%)
  starting transfers between devices  51.2 us (13%)
  blocking collectives  37.1 us (10%)
  matrix products  25.6 us (7%)
  between operations  14.8 us (4%)
  other arithmetic  11.6 us (3%)
  local copies, waits for them, and re-layouts  4.56 us (1%)
    psum x1, waiting for transfers between devices, combine_terms(): lax.psum(partial_value.astype(jnp.bfloat16), 'tensor').astype(jnp.float32)  139 us
    all_gather x2, waiting for transfers between devices, attend(): whole = lax.all_gather(layer_cols, 'tensor', axis=1, tiled=True)  61.3 us
    ppermute x5, starting transfers between devices, swapped(): lax.ppermute(shard, axis, [(i, i ^ 1 << bit) for i in range(lax.axis_size...  41.1 us
    all_gather x2, blocking collectives, attend(): keyvals = lax.all_gather(kv_part, 'tensor', axis=1, tiled=True)  37.1 us
    ppermute x5, waiting for transfers between devices, swapped(): lax.ppermute(shard, axis, [(i, i ^ 1 << bit) for i in range(lax.axis_size...  26 us
    ppermute x2, starting transfers between devices, from_behind(): return lax.ppermute(block, axis, route)  9.84 us
    all_gather x1, waiting for transfers between devices, body(): lax.all_gather(jnp.concatenate([dkey, dval], axis=1).astype(jnp.bfloat16)...  8.18 us
  transfers between devices with their start and end apart: 12, of which 10 were waited for; matrix products, arithmetic and copies ran while one was open for 5% of the time, Pallas kernels for 0%

commit v1 on v0

v1 whole, which is shorter than its diff:
```python
import jax
import jax.numpy as jnp
from jax import lax
from jax.sharding import Mesh, PartitionSpec as P

HEADS = 32
KV_HEADS = 4
HEAD_DIM = 128
EPS = 1e-05
SCALE = HEAD_DIM ** (-0.5)

SEC = ("z", "yh")
TEN = ("x", "yl", "c")
F32 = jnp.float32
BF16 = jnp.bfloat16


def shift(block, distance):
    return lax.ppermute(block, SEC, [(i, (i + distance) % 32) for i in range(32)])


def mirror(block):
    return lax.ppermute(block, SEC, [(i, 31 - i) for i in range(32)])


def swap(block, axis):
    return lax.ppermute(block, axis, [(0, 1), (1, 0)])


def gather(block):
    count, width = block.shape
    spread = jnp.broadcast_to(block, (16, count, width))
    got = lax.all_to_all(spread, TEN, 0, 0, tiled=True)
    return jnp.transpose(got, (1, 0, 2)).reshape(count, 16 * width)


def scatter_sum(term, core):
    count, width = term.shape
    blocks = jnp.transpose(term.astype(BF16).reshape(count, 8, 2, width // 16), (2, 1, 0, 3))
    even, odd = blocks[0], blocks[1]
    keep = jnp.where(core == 0, even, odd)
    away = jnp.where(core == 0, odd, even)
    pair = (keep.astype(F32) + swap(away, "c").astype(F32)).astype(BF16)
    got = lax.all_to_all(pair, ("x", "yl"), 0, 0, tiled=True)
    return got.astype(F32).sum(axis=0)


def head_rows(keyval_w):
    route = []
    for r in range(16):
        half, g = divmod(r // 2, 4)
        route.append((r, 4 * g + 2 * half + r % 2))
    first = lax.ppermute(keyval_w, TEN, route)
    other = swap(first, "yl")
    low = lax.axis_index("yl") == 0
    part = jnp.stack([jnp.where(low, first, other), jnp.where(low, other, first)])
    twin = swap(part, "c")
    even = lax.axis_index("c") == 0
    whole = jnp.stack([jnp.where(even, part, twin), jnp.where(even, twin, part)], axis=1)
    return whole.reshape(4 * keyval_w.shape[0], keyval_w.shape[1])


def project(x, gain, wq, wkv):
    wide = x.astype(F32)
    inv = lax.rsqrt(jnp.mean(wide * wide, axis=-1, keepdims=True) + EPS)
    normed = (wide * inv * gain).astype(BF16)
    q = jnp.dot(normed, wq, preferred_element_type=F32).astype(BF16)
    kv = lax.dot_general(
        normed, wkv, (((1,), (1,)), ((), ())), preferred_element_type=F32
    ).astype(BF16)
    count = x.shape[0]
    qh = q.reshape(count, -1, HEAD_DIM)
    k, v = kv[:, :HEAD_DIM], kv[:, HEAD_DIM:]
    scores = jnp.einsum("thd,sd->hts", qh, k, preferred_element_type=F32) * SCALE
    pos = jnp.arange(count, dtype=jnp.int32)
    scores = jnp.where((pos[:, None] >= pos[None, :])[None], scores, F32(-1e30))
    e = jnp.exp(scores - jnp.max(scores, axis=-1, keepdims=True))
    probs = e / jnp.sum(e, axis=-1, keepdims=True)
    return wide, inv, q, kv, probs


def body(section_input, section_grad, mirror_store, fetch_slot, norm_gain, w_query, w_keyval, w_output):
    x_cols, g_cols = section_input[0], section_grad[0]
    gain, wq, wo = norm_gain[0], w_query[0], w_output[0]
    count = x_cols.shape[0]
    core = lax.axis_index("c")

    fetched = mirror(mirror_store[0][fetch_slot[0]])
    wkv = head_rows(w_keyval[0])
    xg = gather(jnp.concatenate([x_cols, g_cols]))
    x_full, g_full = xg[:count], xg[count:]
    f_full = gather(fetched)
    evicted = mirror(x_cols)

    _, _, _, kv, probs = project(x_full, gain, wq, wkv)
    mixed = jnp.einsum(
        "hts,sd->thd", probs.astype(BF16), kv[:, HEAD_DIM:], preferred_element_type=F32
    ).astype(BF16)
    term = jnp.dot(mixed.reshape(count, -1), wo, preferred_element_type=F32)
    layer_out = (x_cols.astype(F32) + scatter_sum(term, core)).astype(BF16)
    forward_next = shift(layer_out, 1)

    wide, inv, q, kv, probs = project(f_full, gain, wq, wkv)
    qh = q.reshape(count, -1, HEAD_DIM)
    k, v = kv[:, :HEAD_DIM], kv[:, HEAD_DIM:]
    dmixed = lax.dot_general(
        g_full, wo, (((1,), (1,)), ((), ())), preferred_element_type=F32
    ).astype(BF16).reshape(count, -1, HEAD_DIM)
    dprob = jnp.einsum("thd,sd->hts", dmixed, v, preferred_element_type=F32)
    rowdot = jnp.sum(probs * dprob, axis=-1, keepdims=True)
    dscore = (probs * (dprob - rowdot)).astype(BF16)
    dq = (jnp.einsum("hts,sd->thd", dscore, k, preferred_element_type=F32) * SCALE).astype(BF16)
    dk = jnp.einsum("hts,thd->sd", dscore, qh, preferred_element_type=F32) * SCALE
    dv = jnp.einsum("hts,thd->sd", probs.astype(BF16), dmixed, preferred_element_type=F32)
    dkv = jnp.concatenate([dk, dv], axis=1).astype(BF16)
    dterm = lax.dot_general(
        dq.reshape(count, -1), wq, (((1,), (1,)), ((), ())), preferred_element_type=F32
    )
    dterm = gain * (dterm + jnp.dot(dkv, wkv, preferred_element_type=F32))
    stat = jnp.mean(wide * dterm, axis=-1, keepdims=True)
    dterm = inv * dterm - wide * (inv**3 * stat)
    dx = (g_cols.astype(F32) + scatter_sum(dterm, core)).astype(BF16)
    grad_prev = shift(dx, -1)
    return forward_next[None], grad_prev[None], evicted[None]


def solution(mesh):
    fine = Mesh(mesh.devices.reshape(16, 2, 4, 2, 2), SEC + TEN)
    cols = P(SEC, None, TEN)
    return jax.shard_map(
        body,
        mesh=fine,
        in_specs=(
            cols,
            cols,
            P(SEC, None, None, TEN),
            P(SEC),
            P(SEC, None),
            cols,
            P(SEC, TEN, None),
            P(SEC, TEN, None),
        ),
        out_specs=(cols, cols, cols),
        check_vma=False,
    )
```

time: 388 us -> 163 us (0.42)
  the two profiles are of different devices: /device:TPU:1 before, /device:TPU:120 now
where the time goes in v1:
time: 163 us; the launch traced here: 161 us
  starting transfers between devices  61.7 us (38%)
  waiting for transfers between devices  43 us (26%)
  local copies, waits for them, and re-layouts  25.3 us (16%)
  other arithmetic  19.4 us (12%)
  matrix products  9.75 us (6%)
  between operations  1.99 us (1%)
    ppermute x2, starting transfers between devices, mirror(): return lax.ppermute(block, SEC, [(i, 31 - i) for i in range(32)])  22.6 us
    all_to_all x2, waiting for transfers between devices, gather(): got = lax.all_to_all(spread, TEN, 0, 0, tiled=True)  14.5 us
    all_to_all x2, starting transfers between devices, gather(): got = lax.all_to_all(spread, TEN, 0, 0, tiled=True)  12.4 us
    ppermute x4, starting transfers between devices, swap(): return lax.ppermute(block, axis, [(0, 1), (1, 0)])  8.19 us
    unnamed x50, local copies, waits for them, and re-layouts  8.07 us
    all_to_all x2, starting transfers between devices, scatter_sum(): got = lax.all_to_all(pair, ('x', 'yl'), 0, 0, tiled=True)  8.04 us
    ppermute x2, waiting for transfers between devices, shift(): lax.ppermute(block, SEC, [(i, (i + distance) % 32) for i in range(32)])  7.83 us
    ppermute x2, starting transfers between devices, shift(): lax.ppermute(block, SEC, [(i, (i + distance) % 32) for i in range(32)])  7.79 us
  transfers between devices with their start and end apart: 13, of which 7 were waited for; matrix products, arithmetic and copies ran while one was open for 21% of the time, Pallas kernels for 0%

profile of v1, /device:TPU:120, one launch (start us, length us, event | category | flops | bytes accessed | tf_op | source)
XLA Modules:
  0.0 161.2 jit_solution(15772747952281017537)
XLA Ops:
  2.3 12.0 %collective-permute-start.5 = (bf16[128,256]{1,0:T(8,128)(2,1)S(1)}, bf16[128,256]{1,0:T(8,128)(2,1)S(1)}, u32[]{:S(2)}, u32[]{:S(2)}) collective-permute-start(bf16[128,256]{1,0:T(8,128)(2,1)S(1)} %dynamic-slice_bitcast_fusion), channel_id=1, source_target_pairs={{0,496},{16,480},{32,464},{48,448},{64,432},{80,416},{96,400},{112... | collective-permute-start | bytes 196616 | tf_op jit(solution)/shard_map/ppermute | solution.py:23
  14.4 2.7 %collective-permute-start = (bf16[64,4096]{1,0:T(8,128)(2,1)}, bf16[64,4096]{1,0:T(8,128)(2,1)}, u32[]{:S(2)}, u32[]{:S(2)}) collective-permute-start(bf16[64,4096]{1,0:T(8,128)(2,1)} %bitcast.197), channel_id=1, source_target_pairs={{0,0},{1,1},{2,4},{3,5},{4,8},{5,9},{6,12},{7,13},{8,2},{9,3},{10,... | collective-permute-start | bytes 1572872 | tf_op jit(solution)/shard_map/ppermute | solution.py:53
  18.6 7.7 %all-to-all-start.2 = ((bf16[16,128,256]{2,1,0:T(8,128)(2,1)}), bf16[16,128,256]{2,1,0:T(8,128)(2,1)S(1)}, u32[]{:S(2)}, u32[]{:S(2)}) async-start(bf16[16,128,256]{2,1,0:T(8,128)(2,1)} %broadcast_in_dim.51), calls=%async_computation.2 | async-start | bytes 2097152 | tf_op jit(solution)/shard_map/all_to_all | solution.py:33
  26.3 7.6 %collective-permute-done = bf16[64,4096]{1,0:T(8,128)(2,1)} collective-permute-done((bf16[64,4096]{1,0:T(8,128)(2,1)}, bf16[64,4096]{1,0:T(8,128)(2,1)}, u32[]{:S(2)}, u32[]{:S(2)}) %collective-permute-start) | collective-permute-done | bytes 524320 | tf_op jit(solution)/shard_map/ppermute | solution.py:53
  33.9 1.9 %collective-permute-start.1 = (bf16[64,4096]{1,0:T(8,128)(2,1)}, bf16[64,4096]{1,0:T(8,128)(2,1)}, u32[]{:S(2)}, u32[]{:S(2)}) collective-permute-start(bf16[64,4096]{1,0:T(8,128)(2,1)} %collective-permute-done), channel_id=1, source_target_pairs={{0,2},{2,0},{1,3},{3,1},{4,6},{6,4},{5,7},{7,5},{8,10},{10,8},{9,1... | collective-permute-start | bytes 1572872 | tf_op jit(solution)/shard_map/ppermute | solution.py:27
  37.8 5.1 %all-to-all-done.2 = bf16[16,128,256]{2,1,0:T(8,128)(2,1)S(1)} async-done(((bf16[16,128,256]{2,1,0:T(8,128)(2,1)}), bf16[16,128,256]{2,1,0:T(8,128)(2,1)S(1)}, u32[]{:S(2)}, u32[]{:S(2)}) %all-to-all-start.2) | async-done | bytes 1048608 | tf_op jit(solution)/shard_map/all_to_all | solution.py:33
  43.0 1.7 %broadcast_in_dim.47 = bf16[16,256,256]{1,2,0:T(8,128)(2,1)} broadcast(bf16[256,256]{0,1:T(8,128)(2,1)S(1)} %copy.50), dimensions={1,2} | broadcast | bytes 2228224 | tf_op jit(solution)/shard_map/broadcast_in_dim | solution.py:32
  44.6 4.7 %all-to-all-start = ((bf16[16,256,256]{1,2,0:T(8,128)(2,1)}), bf16[16,256,256]{1,2,0:T(8,128)(2,1)}, u32[]{:S(2)}, u32[]{:S(2)}) async-start(bf16[16,256,256]{1,2,0:T(8,128)(2,1)} %broadcast_in_dim.47), calls=%async_computation | async-start | bytes 4194304 | tf_op jit(solution)/shard_map/all_to_all | solution.py:33
  49.3 5.5 %collective-permute-done.1 = bf16[64,4096]{1,0:T(8,128)(2,1)} collective-permute-done((bf16[64,4096]{1,0:T(8,128)(2,1)}, bf16[64,4096]{1,0:T(8,128)(2,1)}, u32[]{:S(2)}, u32[]{:S(2)}) %collective-permute-start.1) | collective-permute-done | bytes 524320 | tf_op jit(solution)/shard_map/ppermute | solution.py:27
  57.4 2.0 %collective-permute-start.2 = (bf16[2,64,4096]{2,1,0:T(8,128)(2,1)}, bf16[2,64,4096]{2,1,0:T(8,128)(2,1)}, u32[]{:S(2)}, u32[]{:S(2)}) collective-permute-start(bf16[2,64,4096]{2,1,0:T(8,128)(2,1)} %pad_maximum_fusion.1), channel_id=1, source_target_pairs={{0,1},{1,0},{2,3},{3,2},{4,5},{5,4},{6,7},{7,6},{8,9},{9,8},{10,11... | collective-permute-start | bytes 3145736 | tf_op jit(solution)/shard_map/ppermute | solution.py:27
  59.4 1.6 %copy.56 = bf16[16,128,256]{1,2,0:T(8,128)(2,1)S(1)} copy(bf16[16,128,256]{2,1,0:T(8,128)(2,1)} %copy-done.12) | data formatting | bytes 2097152 | tf_op jit(solution)/shard_map/all_to_all | solution.py:33
  61.0 1.6 convert_element_type.135
  65.6 3.0 %copy.75 = f32[128,4096]{1,0:T(8,128)} copy(f32[128,4096]{0,1:T(8,128)} %bitcast.181) | data formatting | bytes 4194304 | tf_op jit(solution)/shard_map/convert_element_type | solution.py:64
  68.5 9.4 %all-to-all-done = bf16[16,256,256]{1,2,0:T(8,128)(2,1)} async-done(((bf16[16,256,256]{1,2,0:T(8,128)(2,1)}), bf16[16,256,256]{1,2,0:T(8,128)(2,1)}, u32[]{:S(2)}, u32[]{:S(2)}) %all-to-all-start) | async-done | bytes 2097184 | tf_op jit(solution)/shard_map/all_to_all | solution.py:33
  80.8 1.8 %fusion.3 = f32[128]{0:T(128)S(1)} fusion(bf16[256,16,256]{0,2,1:T(8,128)(2,1)} %bitcast.2), kind=kLoop, calls=%fused_computation.7 | loop fusion | flops 1572736 | bytes 1049088 | tf_op jit(solution)/shard_map/reduce_sum | solution.py:65
  82.6 1.7 %fusion.5 = bf16[128,16,256]{0,2,1:T(8,128)(2,1)S(1)} fusion(f32[16,256]{1,0:T(8,128)S(1)} %mul.126, f32[128]{0:T(128)S(1)} %add_rsqrt_fusion.1, bf16[256,16,256]{0,2,1:T(8,128)(2,1)} %bitcast.2), kind=kLoop, calls=%fused_computation.9 | loop fusion | flops 2097152 | bytes 2114048 | tf_op jit(solution)/shard_map/convert_element_type | solution.py:66
  92.4 2.1 %convolution_convert_fusion = bf16[128,4096]{1,0:T(8,128)(2,1)S(1)} fusion(bf16[128,256]{0,1:T(8,128)(2,1)S(1)} %bitcast.191, bf16[1,256,4096]{2,1,0:T(8,128)(2,1)} %param.15), kind=kOutput, calls=%fused_computation.4 | convolution fusion | flops 268959744 | bytes 3211264 | tf_op jit(solution)/shard_map/dot_general | solution.py:99
  94.5 1.6 reshape.143
  96.1 1.6 copy.90
  98.5 2.2 %collective-permute-start.3 = (bf16[8,128,256]{2,1,0:T(8,128)(2,1)}, bf16[8,128,256]{2,1,0:T(8,128)(2,1)}, u32[]{:S(2)}, u32[]{:S(2)}) collective-permute-start(bf16[8,128,256]{2,1,0:T(8,128)(2,1)} %select_bitcast_fusion.3), channel_id=1, source_target_pairs={{0,1},{1,0},{2,3},{3,2},{4,5},{5,4},{6,7},{7,6},{8,9},{9,8},{10,11... | collective-permute-start | bytes 1572872 | tf_op jit(solution)/shard_map/ppermute | solution.py:27
  105.3 2.6 %reshape.147 = bf16[128,8,2,256]{3,2,1,0:T(2,128)(2,1)} reshape(bf16[128,4096]{1,0:T(8,128)(2,1)} %subtract_convert_fusion) | data formatting | bytes 2097152 | tf_op jit(solution)/shard_map/reshape | solution.py:39
  107.9 1.6 copy.89
  111.3 2.1 %collective-permute-start.6 = (bf16[8,128,256]{2,1,0:T(8,128)(2,1)}, bf16[8,128,256]{2,1,0:T(8,128)(2,1)}, u32[]{:S(2)}, u32[]{:S(2)}) collective-permute-start(bf16[8,128,256]{2,1,0:T(8,128)(2,1)} %select_bitcast_fusion.2), channel_id=1, source_target_pairs={{0,1},{1,0},{2,3},{3,2},{4,5},{5,4},{6,7},{7,6},{8,9},{9,8},{10,11... | collective-permute-start | bytes 1572872 | tf_op jit(solution)/shard_map/ppermute | solution.py:27
  113.4 2.0 %fusion.40 = bf16[8,128,256]{2,1,0:T(8,128)(2,1)} fusion(bf16[8,128,256]{2,1,0:T(8,128)(2,1)} %collective-permute-done.3, pred[]{:T(512)S(6)} %eq.4, bf16[2,8,128,256]{3,2,1,0:T(8,128)(2,1)S(1)} %bitcast.178), kind=kLoop, calls=%fused_computation.53 | loop fusion | flops 1310720 | bytes 2097153 | tf_op jit(solution)/shard_map/convert_element_type | solution.py:43
  115.4 4.1 %all-to-all-start.1 = ((bf16[8,128,256]{2,1,0:T(8,128)(2,1)}), bf16[8,128,256]{2,1,0:T(8,128)(2,1)S(1)}, u32[]{:S(2)}, u32[]{:S(2)}) async-start(bf16[8,128,256]{2,1,0:T(8,128)(2,1)} %fusion.40), calls=%async_computation.1 | async-start | bytes 1048576 | tf_op jit(solution)/shard_map/all_to_all | solution.py:44
  119.5 2.4 %fusion.39 = bf16[8,128,256]{2,1,0:T(8,128)(2,1)} fusion(bf16[8,128,256]{2,1,0:T(8,128)(2,1)} %collective-permute-done.6, pred[]{:T(512)S(6)} %eq.4, bf16[2,8,128,256]{3,2,1,0:T(8,128)(2,1)} %bitcast.180), kind=kLoop, calls=%fused_computation.51 | loop fusion | flops 1310720 | bytes 2097153 | tf_op jit(solution)/shard_map/convert_element_type | solution.py:43
  121.9 7.0 %all-to-all-done.1 = bf16[8,128,256]{2,1,0:T(8,128)(2,1)S(1)} async-done(((bf16[8,128,256]{2,1,0:T(8,128)(2,1)}), bf16[8,128,256]{2,1,0:T(8,128)(2,1)S(1)}, u32[]{:S(2)}, u32[]{:S(2)}) %all-to-all-start.1) | async-done | bytes 524320 | tf_op jit(solution)/shard_map/all_to_all | solution.py:44
  128.9 4.0 %all-to-all-start.3 = ((bf16[8,128,256]{2,1,0:T(8,128)(2,1)}), bf16[8,128,256]{2,1,0:T(8,128)(2,1)S(1)}, u32[]{:S(2)}, u32[]{:S(2)}) async-start(bf16[8,128,256]{2,1,0:T(8,128)(2,1)} %fusion.39), calls=%async_computation.3 | async-start | bytes 1048576 | tf_op jit(solution)/shard_map/all_to_all | solution.py:44
  132.9 10.6 %collective-permute-start.8 = (bf16[128,256]{1,0:T(8,128)(2,1)S(1)}, bf16[128,256]{1,0:T(8,128)(2,1)S(1)}, u32[]{:S(2)}, u32[]{:S(2)}) collective-permute-start(bf16[128,256]{1,0:T(8,128)(2,1)S(1)} %bitcast.189), channel_id=1, source_target_pairs={{0,496},{16,480},{32,464},{48,448},{64,432},{80,416},{96,400},{112... | collective-permute-start | bytes 196616 | tf_op jit(solution)/shard_map/ppermute | solution.py:23
  143.5 5.9 %collective-permute-start.4 = (bf16[128,256]{1,0:T(8,128)(2,1)S(1)}, bf16[128,256]{1,0:T(8,128)(2,1)S(1)}, u32[]{:S(2)}, u32[]{:S(2)}) collective-permute-start(bf16[128,256]{1,0:T(8,128)(2,1)S(1)} %add_convert_fusion.1), channel_id=1, source_target_pairs={{0,16},{16,32},{32,48},{48,64},{64,80},{80,96},{96,112},{112,128},... | collective-permute-start | bytes 196616 | tf_op jit(solution)/shard_map/ppermute | solution.py:19
  149.5 1.9 %collective-permute-start.7 = (bf16[128,256]{1,0:T(8,128)(2,1)S(1)}, bf16[128,256]{1,0:T(8,128)(2,1)S(1)}, u32[]{:S(2)}, u32[]{:S(2)}) collective-permute-start(bf16[128,256]{1,0:T(8,128)(2,1)S(1)} %add_convert_fusion), channel_id=1, source_target_pairs={{0,496},{16,0},{32,16},{48,32},{64,48},{80,64},{96,80},{112,96},{1... | collective-permute-start | bytes 196616 | tf_op jit(solution)/shard_map/ppermute | solution.py:19
  151.5 7.8 %collective-permute-done.7 = bf16[128,256]{1,0:T(8,128)(2,1)S(1)} collective-permute-done((bf16[128,256]{1,0:T(8,128)(2,1)S(1)}, bf16[128,256]{1,0:T(8,128)(2,1)S(1)}, u32[]{:S(2)}, u32[]{:S(2)}) %collective-permute-start.7) | collective-permute-done | bytes 65568 | tf_op jit(solution)/shard_map/ppermute | solution.py:19
  (99 shorter events, 29.9 us)
Async XLA Ops:
  0.6 64.2 %copy-start = (bf16[1,4096,256]{2,1,0:T(8,128)(2,1)S(1)}, bf16[1,4096,256]{2,1,0:T(8,128)(2,1)}, u32[]{:S(2)}) copy-start(bf16[1,4096,256]{2,1,0:T(8,128)(2,1)} %param.13) | copy-start | bytes 6291460
  0.6 35.7 %copy-start.15 = (f32[1,4096]{1,0:T(1,128)S(1)}, f32[1,4096]{1,0:T(1,128)}, u32[]{:S(2)}) copy-start(f32[1,4096]{1,0:T(1,128)} %param.12) | copy-start | bytes 49156
  0.7 36.4 %copy-start.14 = (bf16[1,128,256]{2,1,0:T(8,128)(2,1)S(1)}, bf16[1,128,256]{2,1,0:T(8,128)(2,1)}, u32[]{:S(2)}) copy-start(bf16[1,128,256]{2,1,0:T(8,128)(2,1)} %param.8) | copy-start | bytes 196612
  0.7 36.4 %copy-start.13 = (bf16[1,128,256]{2,1,0:T(8,128)(2,1)S(1)}, bf16[1,128,256]{2,1,0:T(8,128)(2,1)}, u32[]{:S(2)}) copy-start(bf16[1,128,256]{2,1,0:T(8,128)(2,1)} %param.9) | copy-start | bytes 196612
  2.3 15.2 %collective-permute-start.5 = (bf16[128,256]{1,0:T(8,128)(2,1)S(1)}, bf16[128,256]{1,0:T(8,128)(2,1)S(1)}, u32[]{:S(2)}, u32[]{:S(2)}) collective-permute-start(bf16[128,256]{1,0:T(8,128)(2,1)S(1)} %dynamic-slice_bitcast_fusion), channel_id=1, source_target_pairs={{0,496},{16,480},{32,464},{48,448},{64,432},{80,416},{96,400},{112... | collective-permute-start | bytes 196616 | tf_op jit(solution)/shard_map/ppermute | solution.py:23
  14.4 19.5 %collective-permute-start = (bf16[64,4096]{1,0:T(8,128)(2,1)}, bf16[64,4096]{1,0:T(8,128)(2,1)}, u32[]{:S(2)}, u32[]{:S(2)}) collective-permute-start(bf16[64,4096]{1,0:T(8,128)(2,1)} %bitcast.197), channel_id=1, source_target_pairs={{0,0},{1,1},{2,4},{3,5},{4,8},{5,9},{6,12},{7,13},{8,2},{9,3},{10,... | collective-permute-start | bytes 1572872 | tf_op jit(solution)/shard_map/ppermute | solution.py:53
  18.6 24.3 %all-to-all-start.2 = ((bf16[16,128,256]{2,1,0:T(8,128)(2,1)}), bf16[16,128,256]{2,1,0:T(8,128)(2,1)S(1)}, u32[]{:S(2)}, u32[]{:S(2)}) async-start(bf16[16,128,256]{2,1,0:T(8,128)(2,1)} %broadcast_in_dim.51), calls=%async_computation.2 | async-start | bytes 2097152 | tf_op jit(solution)/shard_map/all_to_all | solution.py:33
  33.9 21.0 %collective-permute-start.1 = (bf16[64,4096]{1,0:T(8,128)(2,1)}, bf16[64,4096]{1,0:T(8,128)(2,1)}, u32[]{:S(2)}, u32[]{:S(2)}) collective-permute-start(bf16[64,4096]{1,0:T(8,128)(2,1)} %collective-permute-done), channel_id=1, source_target_pairs={{0,2},{2,0},{1,3},{3,1},{4,6},{6,4},{5,7},{7,5},{8,10},{10,8},{9,1... | collective-permute-start | bytes 1572872 | tf_op jit(solution)/shard_map/ppermute | solution.py:27
  43.0 1.7 %copy-start.12 = (bf16[16,128,256]{2,1,0:T(8,128)(2,1)}, bf16[16,128,256]{2,1,0:T(8,128)(2,1)S(1)}, u32[]{:S(2)}) copy-start(bf16[16,128,256]{2,1,0:T(8,128)(2,1)S(1)} %all-to-all-done.2) | copy-start | bytes 3145732
  44.6 33.3 %all-to-all-start = ((bf16[16,256,256]{1,2,0:T(8,128)(2,1)}), bf16[16,256,256]{1,2,0:T(8,128)(2,1)}, u32[]{:S(2)}, u32[]{:S(2)}) async-start(bf16[16,256,256]{1,2,0:T(8,128)(2,1)} %broadcast_in_dim.47), calls=%async_computation | async-start | bytes 4194304 | tf_op jit(solution)/shard_map/all_to_all | solution.py:33
  56.1 1.2 copy-start.8
  56.1 1.3 copy-start.10
  57.4 27.6 %collective-permute-start.2 = (bf16[2,64,4096]{2,1,0:T(8,128)(2,1)}, bf16[2,64,4096]{2,1,0:T(8,128)(2,1)}, u32[]{:S(2)}, u32[]{:S(2)}) collective-permute-start(bf16[2,64,4096]{2,1,0:T(8,128)(2,1)} %pad_maximum_fusion.1), channel_id=1, source_target_pairs={{0,1},{1,0},{2,3},{3,2},{4,5},{5,4},{6,7},{7,6},{8,9},{9,8},{10,11... | collective-permute-start | bytes 3145736 | tf_op jit(solution)/shard_map/ppermute | solution.py:27
  63.2 2.3 %copy-start.21 = (f32[128]{0:T(128)}, f32[128]{0:T(128)S(1)}, u32[]{:S(2)}) copy-start(f32[128]{0:T(128)S(1)} %multiply_reduce_fusion.1) | copy-start | bytes 1540
  63.2 2.3 %copy-start.19 = (f32[128]{0:T(128)}, f32[128]{0:T(128)S(1)}, u32[]{:S(2)}) copy-start(f32[128]{0:T(128)S(1)} %add_rsqrt_fusion) | copy-start | bytes 1540
  77.9 1.9 %copy-start.7 = (bf16[1,256,4096]{2,1,0:T(8,128)(2,1)S(1)}, bf16[1,256,4096]{2,1,0:T(8,128)(2,1)}, u32[]{:S(2)}) copy-start(bf16[1,256,4096]{2,1,0:T(8,128)(2,1)} %param.15) | copy-start | bytes 6291460
  84.3 1.0 copy-start.9
  84.3 1.2 copy-start.11
  86.9 1.4 copy-start.5
  87.1 2.1 %copy-start.1 = (bf16[2,2,64,4096]{3,2,1,0:T(8,128)(2,1)}, bf16[2,2,64,4096]{3,2,1,0:T(8,128)(2,1)S(1)}, u32[]{:S(2)}) copy-start(bf16[2,2,64,4096]{3,2,1,0:T(8,128)(2,1)S(1)} %pad_maximum_fusion) | copy-start | bytes 6291460
  98.5 14.9 %collective-permute-start.3 = (bf16[8,128,256]{2,1,0:T(8,128)(2,1)}, bf16[8,128,256]{2,1,0:T(8,128)(2,1)}, u32[]{:S(2)}, u32[]{:S(2)}) collective-permute-start(bf16[8,128,256]{2,1,0:T(8,128)(2,1)} %select_bitcast_fusion.3), channel_id=1, source_target_pairs={{0,1},{1,0},{2,3},{3,2},{4,5},{5,4},{6,7},{7,6},{8,9},{9,8},{10,11... | collective-permute-start | bytes 1572872 | tf_op jit(solution)/shard_map/ppermute | solution.py:27
  100.7 1.6 copy-start.2
  100.7 2.2 %copy-start.3 = (f32[128,4096]{1,0:T(8,128)S(1)}, f32[128,4096]{1,0:T(8,128)}, u32[]{:S(2)}) copy-start(f32[128,4096]{1,0:T(8,128)} %copy.75) | copy-start | bytes 6291460
  100.7 2.2 %copy-start.16 = (f32[1,4096]{1,0:T(1,128)S(1)}, f32[1,4096]{1,0:T(1,128)}, u32[]{:S(2)}) copy-start(f32[1,4096]{1,0:T(1,128)} %param.12) | copy-start | bytes 49156
  100.8 2.2 %copy-start.18 = (bf16[128,128]{0,1:T(8,128)(2,1)S(1)}, bf16[128,128]{0,1:T(8,128)(2,1)}, u32[]{:S(2)}) copy-start(bf16[128,128]{0,1:T(8,128)(2,1)} %fusion.38) | copy-start | bytes 98308
  109.4 1.0 copy-start.6
  111.3 8.3 %collective-permute-start.6 = (bf16[8,128,256]{2,1,0:T(8,128)(2,1)}, bf16[8,128,256]{2,1,0:T(8,128)(2,1)}, u32[]{:S(2)}, u32[]{:S(2)}) collective-permute-start(bf16[8,128,256]{2,1,0:T(8,128)(2,1)} %select_bitcast_fusion.2), channel_id=1, source_target_pairs={{0,1},{1,0},{2,3},{3,2},{4,5},{5,4},{6,7},{7,6},{8,9},{9,8},{10,11... | collective-permute-start | bytes 1572872 | tf_op jit(solution)/shard_map/ppermute | solution.py:27
  115.4 13.5 %all-to-all-start.1 = ((bf16[8,128,256]{2,1,0:T(8,128)(2,1)}), bf16[8,128,256]{2,1,0:T(8,128)(2,1)S(1)}, u32[]{:S(2)}, u32[]{:S(2)}) async-start(bf16[8,128,256]{2,1,0:T(8,128)(2,1)} %fusion.40), calls=%async_computation.1 | async-start | bytes 1048576 | tf_op jit(solution)/shard_map/all_to_all | solution.py:44
  128.9 20.5 %all-to-all-start.3 = ((bf16[8,128,256]{2,1,0:T(8,128)(2,1)}), bf16[8,128,256]{2,1,0:T(8,128)(2,1)S(1)}, u32[]{:S(2)}, u32[]{:S(2)}) async-start(bf16[8,128,256]{2,1,0:T(8,128)(2,1)} %fusion.39), calls=%async_computation.3 | async-start | bytes 1048576 | tf_op jit(solution)/shard_map/all_to_all | solution.py:44
  132.9 18.6 %collective-permute-start.8 = (bf16[128,256]{1,0:T(8,128)(2,1)S(1)}, bf16[128,256]{1,0:T(8,128)(2,1)S(1)}, u32[]{:S(2)}, u32[]{:S(2)}) collective-permute-start(bf16[128,256]{1,0:T(8,128)(2,1)S(1)} %bitcast.189), channel_id=1, source_target_pairs={{0,496},{16,480},{32,464},{48,448},{64,432},{80,416},{96,400},{112... | collective-permute-start | bytes 196616 | tf_op jit(solution)/shard_map/ppermute | solution.py:23
  143.5 7.9 %collective-permute-start.4 = (bf16[128,256]{1,0:T(8,128)(2,1)S(1)}, bf16[128,256]{1,0:T(8,128)(2,1)S(1)}, u32[]{:S(2)}, u32[]{:S(2)}) collective-permute-start(bf16[128,256]{1,0:T(8,128)(2,1)S(1)} %add_convert_fusion.1), channel_id=1, source_target_pairs={{0,16},{16,32},{32,48},{48,64},{64,80},{80,96},{96,112},{112,128},... | collective-permute-start | bytes 196616 | tf_op jit(solution)/shard_map/ppermute | solution.py:19
  149.5 9.8 %collective-permute-start.7 = (bf16[128,256]{1,0:T(8,128)(2,1)S(1)}, bf16[128,256]{1,0:T(8,128)(2,1)S(1)}, u32[]{:S(2)}, u32[]{:S(2)}) collective-permute-start(bf16[128,256]{1,0:T(8,128)(2,1)S(1)} %add_convert_fusion), channel_id=1, source_target_pairs={{0,496},{16,0},{32,16},{48,32},{64,48},{80,64},{96,80},{112,96},{1... | collective-permute-start | bytes 196616 | tf_op jit(solution)/shard_map/ppermute | solution.py:19
  (4 other events, 3.5 us)

commit v2 on v1

v2 whole, which is shorter than its diff:
```python
import jax
import jax.numpy as jnp
from jax import lax
from jax.experimental import pallas as pl
from jax.experimental.pallas import tpu as pltpu
from jax.sharding import Mesh, PartitionSpec as P

HEAD_DIM = 128
EPS = 1e-05
SCALE = HEAD_DIM ** (-0.5)
D = 4096
T = 128
W = 256
N = D // W

SEC = ("z", "yh")
TEN = ("x", "yl", "c")
F32 = jnp.float32
BF16 = jnp.bfloat16
NT = (((1,), (1,)), ((), ()))
TN = (((0,), (0,)), ((), ()))


def dot(a, b, dims=(((1,), (0,)), ((), ()))):
    return lax.dot_general(a, b, dims, preferred_element_type=F32)


def call(kernel, outs, core, *args, scratch=(), flops=0):
    nbytes = sum(a.size * a.dtype.itemsize for a in args)
    return pl.pallas_call(
        kernel,
        out_shape=tuple(pltpu.VMEM(s, d) for s, d in outs),
        in_specs=[pl.BlockSpec(memory_space=pltpu.SMEM)]
        + [pl.BlockSpec(memory_space=pltpu.VMEM)] * len(args),
        out_specs=tuple(pl.BlockSpec(memory_space=pltpu.VMEM) for _ in outs),
        scratch_shapes=list(scratch),
        compiler_params=pltpu.CompilerParams(vmem_limit_bytes=24 * 2**20),
        cost_estimate=pl.CostEstimate(flops=flops, bytes_accessed=nbytes, transcendentals=0),
    )(core, *(pltpu.with_memory_space_constraint(a, pltpu.VMEM) for a in args))


def blocks(core, own, other):
    for ref, side in ((own, core), (other, 1 - core)):
        for j in range(8):
            yield ref.at[j], pl.multiple_of((2 * j + side) * W, W)


def recompute(core, xa, xb, gain, wq, wkv, xg):
    squares = jnp.zeros((T, W), F32)
    for x, at in blocks(core, xa, xb):
        wide = x[...].astype(F32)
        squares += wide * wide
        xg[:, pl.ds(at, W)] = (wide * gain[:, pl.ds(at, W)]).astype(BF16)
    inv = lax.rsqrt(jnp.sum(squares, axis=-1, keepdims=True) * (1.0 / D) + EPS)
    q = dot(xg[...], wq[...]) * inv
    kv = dot(xg[...], wkv[...], NT) * inv
    qb, kvb = q.astype(BF16), kv.astype(BF16)
    k, v = kvb[:, :HEAD_DIM], kvb[:, HEAD_DIM:]
    row = lax.broadcasted_iota(jnp.int32, (T, T), 0)
    col = lax.broadcasted_iota(jnp.int32, (T, T), 1)
    probs = []
    for h in range(2):
        s = dot(qb[:, h * HEAD_DIM : (h + 1) * HEAD_DIM], k, NT) * SCALE
        s = jnp.where(row >= col, s, F32(-1e30))
        e = jnp.exp(s - jnp.max(s, axis=-1, keepdims=True))
        probs.append(e / jnp.sum(e, axis=-1, keepdims=True))
    return inv, q, kv, qb, k, v, probs


def forward_kernel(core_ref, xa, xb, gain, wq, wkv, wo, keep, send, xg):
    core = core_ref[0]
    _, _, _, _, _, v, probs = recompute(core, xa, xb, gain, wq, wkv, xg)
    mixed = jnp.concatenate([dot(p.astype(BF16), v).astype(BF16) for p in probs], axis=1)
    for out, at in blocks(core, keep, send):
        out[...] = dot(mixed, wo[:, pl.ds(at, W)]).astype(BF16)


def dmixed_kernel(core_ref, ga, gb, wo, dmixed, g):
    for block, at in blocks(core_ref[0], ga, gb):
        g[:, pl.ds(at, W)] = block[...]
    dmixed[...] = dot(g[...], wo[...], NT).astype(BF16)


def backward_kernel(core_ref, xa, xb, gain, wq, wkv, dmixed, keep, send, xg):
    core = core_ref[0]
    inv, q, kv, qb, k, v, probs = recompute(core, xa, xb, gain, wq, wkv, xg)
    dq, dk, dv = [], 0.0, 0.0
    for h, p in enumerate(probs):
        lanes = slice(h * HEAD_DIM, (h + 1) * HEAD_DIM)
        dm = dmixed[:, lanes]
        dprob = dot(dm, v, NT)
        rowdot = jnp.sum(p * dprob, axis=-1, keepdims=True)
        dscore = (p * (dprob - rowdot)).astype(BF16)
        dq.append(dot(dscore, k) * SCALE)
        dk += dot(dscore, qb[:, lanes], TN)
        dv += dot(p.astype(BF16), dm, TN)
    dq = jnp.concatenate(dq, axis=1)
    dkv = jnp.concatenate([dk * SCALE, dv], axis=1)
    share = jnp.sum(dq * q + dkv * kv, axis=-1, keepdims=True)
    coef = inv * inv * share * (1.0 / D)
    dqs, dkvs = (dq * inv).astype(BF16), (dkv * inv).astype(BF16)
    for (out, at), (x, _) in zip(blocks(core, keep, send), blocks(core, xa, xb)):
        term = dot(dqs, wq[pl.ds(at, W), :], NT) + dot(dkvs, wkv[:, pl.ds(at, W)])
        term = term * gain[:, pl.ds(at, W)] - coef * x[...].astype(F32)
        out[...] = term.astype(BF16)


def pair_kernel(_, keep, got, out):
    out[...] = (keep[...].astype(F32) + got[...].astype(F32)).astype(BF16)


def finish_kernel(_, base, got, out):
    total = base[...].astype(F32)
    for j in range(8):
        total += got[j].astype(F32)
    out[...] = total.astype(BF16)


def shift(block, distance):
    return lax.ppermute(block, SEC, [(i, (i + distance) % 32) for i in range(32)])


def mirror(block):
    return lax.ppermute(block, SEC, [(i, 31 - i) for i in range(32)])


def swap(block, axis):
    return lax.ppermute(block, axis, [(0, 1), (1, 0)])


def exchange(parts):
    return lax.all_to_all(parts, ("x", "yl"), 0, 0, tiled=True)


def head_rows(keyval_w):
    route = []
    for r in range(16):
        half, g = divmod(r // 2, 4)
        route.append((r, 4 * g + 2 * half + r % 2))
    first = lax.ppermute(keyval_w, TEN, route)
    other = swap(first, "yl")
    low = lax.axis_index("yl") == 0
    part = jnp.stack([jnp.where(low, first, other), jnp.where(low, other, first)])
    twin = swap(part, "c")
    even = lax.axis_index("c") == 0
    whole = jnp.stack([jnp.where(even, part, twin), jnp.where(even, twin, part)], axis=1)
    return whole.reshape(4 * keyval_w.shape[0], keyval_w.shape[1])


def body(section_input, section_grad, mirror_store, fetch_slot, norm_gain, w_query, w_keyval, w_output):
    x_cols, g_cols = section_input[0], section_grad[0]
    gain, wq, wo = norm_gain, w_query[0], w_output[0]
    core = lax.axis_index("c").astype(jnp.int32).reshape(1)
    half = ((8, T, W), BF16)
    xg = pltpu.VMEM((T, D), BF16)

    def gather(*blocks):
        spread = jnp.broadcast_to(jnp.stack(blocks), (8, len(blocks), T, W))
        own = exchange(spread)
        other = swap(own, "c")
        return [(own[:, i], other[:, i]) for i in range(len(blocks))]

    def total(base, keep, send):
        (pair,) = call(pair_kernel, [half], core, keep, swap(send, "c"))
        (out,) = call(finish_kernel, [((T, W), BF16)], core, base, exchange(pair))
        return out

    fetched = mirror(mirror_store[0][fetch_slot[0]])
    wkv = head_rows(w_keyval[0])
    ((xa, xb),) = gather(x_cols)
    ((ga, gb),) = gather(g_cols)
    ((fa, fb),) = gather(fetched)
    x_late, fa = lax.optimization_barrier((x_cols, fa))
    evicted = mirror(x_late)

    keep, send = call(
        forward_kernel, [half, half], core, xa, xb, gain, wq, wkv, wo, scratch=[xg], flops=10**9
    )
    forward_next = shift(total(x_cols, keep, send), 1)

    (dmixed,) = call(
        dmixed_kernel, [((T, W), BF16)], core, ga, gb, wo, scratch=[xg], flops=5 * 10**8
    )
    keep, send = call(
        backward_kernel, [half, half], core, fa, fb, gain, wq, wkv, dmixed, scratch=[xg], flops=10**9
    )
    grad_prev = shift(total(g_cols, keep, send), -1)
    return forward_next[None], grad_prev[None], evicted[None]


def solution(mesh):
    fine = Mesh(mesh.devices.reshape(16, 2, 4, 2, 2), SEC + TEN)
    cols = P(SEC, None, TEN)
    return jax.shard_map(
        body,
        mesh=fine,
        in_specs=(
            cols,
            cols,
            P(SEC, None, None, TEN),
            P(SEC),
            P(SEC, None),
            cols,
            P(SEC, TEN, None),
            P(SEC, TEN, None),
        ),
        out_specs=(cols, cols, cols),
        check_vma=False,
    )
```

time: 163 us -> 147 us (0.902)
  the two profiles are of different devices: /device:TPU:120 before, /device:TPU:130 now
where the time goes in v2:
time: 147 us; the launch traced here: 146 us
  starting transfers between devices  79.3 us (54%)
  waiting for transfers between devices  41.6 us (28%)
  Pallas kernels  13.2 us (9%)
  local copies, waits for them, and re-layouts  7.63 us (5%)
  other arithmetic  2.69 us (2%)
  between operations  1.6 us (1%)
    all_to_all x5, starting transfers between devices, exchange(): return lax.all_to_all(parts, ('x', 'yl'), 0, 0, tiled=True)  28.2 us
    ppermute x2, starting transfers between devices, mirror(): return lax.ppermute(block, SEC, [(i, 31 - i) for i in range(32)])  25.5 us
    ppermute x7, starting transfers between devices, swap(): return lax.ppermute(block, axis, [(0, 1), (1, 0)])  14.8 us
    all_to_all x5, waiting for transfers between devices, exchange(): return lax.all_to_all(parts, ('x', 'yl'), 0, 0, tiled=True)  14.1 us
    ppermute x1, waiting for transfers between devices, head_rows(): first = lax.ppermute(keyval_w, TEN, route)  13.3 us
    pallas_call x7, Pallas kernels, call(): pl.pallas_call(kernel, out_shape=tuple((pltpu.VMEM(s, d) for s, d in outs...  13.2 us
    ppermute x7, waiting for transfers between devices, swap(): return lax.ppermute(block, axis, [(0, 1), (1, 0)])  8.5 us
    ppermute x2, starting transfers between devices, shift(): lax.ppermute(block, SEC, [(i, (i + distance) % 32) for i in range(32)])  7.35 us
  transfers between devices with their start and end apart: 17, of which 7 were waited for; matrix products, arithmetic and copies ran while one was open for 4% of the time, Pallas kernels for 9%

profile of v2, /device:TPU:130, one launch (start us, length us, event | category | flops | bytes accessed | tf_op | source)
XLA Modules:
  0.0 146.0 jit_solution(9357212470376528694)
XLA Ops:
  0.6 3.5 %collective-permute-start.1 = (bf16[64,4096]{1,0:T(8,128)(2,1)}, bf16[64,4096]{1,0:T(8,128)(2,1)S(1)}, u32[]{:S(2)}, u32[]{:S(2)}) collective-permute-start(bf16[64,4096]{1,0:T(8,128)(2,1)} %bitcast.52), channel_id=1, source_target_pairs={{0,0},{1,1},{2,4},{3,5},{4,8},{5,9},{6,12},{7,13},{8,2},{9,3},{10,... | collective-permute-start | bytes 1572872 | tf_op jit(solution)/shard_map/ppermute | solution.py:140
  4.2 13.3 %collective-permute-done.1 = bf16[64,4096]{1,0:T(8,128)(2,1)S(1)} collective-permute-done((bf16[64,4096]{1,0:T(8,128)(2,1)}, bf16[64,4096]{1,0:T(8,128)(2,1)S(1)}, u32[]{:S(2)}, u32[]{:S(2)}) %collective-permute-start.1) | collective-permute-done | bytes 524320 | tf_op jit(solution)/shard_map/ppermute | solution.py:140
  17.4 2.6 %collective-permute-start.2 = (bf16[64,4096]{1,0:T(8,128)(2,1)S(1)}, bf16[64,4096]{1,0:T(8,128)(2,1)S(1)}, u32[]{:S(2)}, u32[]{:S(2)}) collective-permute-start(bf16[64,4096]{1,0:T(8,128)(2,1)S(1)} %collective-permute-done.1), channel_id=1, source_target_pairs={{0,2},{2,0},{1,3},{3,1},{4,6},{6,4},{5,7},{7,5},{8,10},{10,8},{9,1... | collective-permute-start | bytes 1572872 | tf_op jit(solution)/shard_map/ppermute | solution.py:128
  20.0 1.7 %broadcast_in_dim.21 = bf16[8,1,128,256]{3,2,1,0:T(8,128)(2,1)} broadcast(bf16[128,256]{1,0:T(8,128)(2,1)} %bitcast.44), dimensions={2,3} | broadcast | bytes 589824 | tf_op jit(solution)/shard_map/broadcast_in_dim | solution.py:158
  21.7 6.9 %all-to-all-start.3 = ((bf16[8,1,128,256]{3,2,1,0:T(8,128)(2,1)}), bf16[8,1,128,256]{3,2,1,0:T(8,128)(2,1)S(1)}, u32[]{:S(2)}, u32[]{:S(2)}) async-start(bf16[8,1,128,256]{3,2,1,0:T(8,128)(2,1)} %broadcast_in_dim.21), calls=%async_computation.3 | async-start | bytes 1048576 | tf_op jit(solution)/shard_map/all_to_all | solution.py:132
  28.5 8.5 %collective-permute-done.2 = bf16[64,4096]{1,0:T(8,128)(2,1)S(1)} collective-permute-done((bf16[64,4096]{1,0:T(8,128)(2,1)S(1)}, bf16[64,4096]{1,0:T(8,128)(2,1)S(1)}, u32[]{:S(2)}, u32[]{:S(2)}) %collective-permute-start.2) | collective-permute-done | bytes 524320 | tf_op jit(solution)/shard_map/ppermute | solution.py:128
  37.9 1.1 pad_maximum_fusion.1
  39.0 2.0 %collective-permute-start.3 = (bf16[2,64,4096]{2,1,0:T(8,128)(2,1)}, bf16[2,64,4096]{2,1,0:T(8,128)(2,1)}, u32[]{:S(2)}, u32[]{:S(2)}) collective-permute-start(bf16[2,64,4096]{2,1,0:T(8,128)(2,1)} %pad_maximum_fusion.1), channel_id=1, source_target_pairs={{0,1},{1,0},{2,3},{3,2},{4,5},{5,4},{6,7},{7,6},{8,9},{9,8},{10,11... | collective-permute-start | bytes 3145736 | tf_op jit(solution)/shard_map/ppermute | solution.py:128
  41.9 6.1 %all-to-all-start = ((bf16[8,1,128,256]{3,2,1,0:T(8,128)(2,1)}), bf16[8,1,128,256]{3,2,1,0:T(8,128)(2,1)S(1)}, u32[]{:S(2)}, u32[]{:S(2)}) async-start(bf16[8,1,128,256]{3,2,1,0:T(8,128)(2,1)} %broadcast_in_dim.18), calls=%async_computation | async-start | bytes 1048576 | tf_op jit(solution)/shard_map/all_to_all | solution.py:132
  48.6 13.1 %collective-permute-start.6 = (bf16[128,256]{1,0:T(8,128)(2,1)S(1)}, bf16[128,256]{1,0:T(8,128)(2,1)S(1)}, u32[]{:S(2)}, u32[]{:S(2)}) collective-permute-start(bf16[128,256]{1,0:T(8,128)(2,1)S(1)} %dynamic-slice_bitcast_fusion), channel_id=1, source_target_pairs={{0,496},{16,480},{32,464},{48,448},{64,432},{80,416},{96,400},{112... | collective-permute-start | bytes 196616 | tf_op jit(solution)/shard_map/ppermute | solution.py:124
  61.7 1.9 %collective-permute-start.8 = (bf16[8,1,128,256]{3,2,0,1:T(8,128)(2,1)S(1)}, bf16[8,1,128,256]{3,2,0,1:T(8,128)(2,1)}, u32[]{:S(2)}, u32[]{:S(2)}) collective-permute-start(bf16[8,1,128,256]{3,2,0,1:T(8,128)(2,1)S(1)} %bitcast.39), channel_id=1, source_target_pairs={{0,1},{1,0},{2,3},{3,2},{4,5},{5,4},{6,7},{7,6},{8,9},{9,8},{10,11... | collective-permute-start | bytes 1572872 | tf_op jit(solution)/shard_map/ppermute | solution.py:128
  64.3 0.9 broadcast_in_dim.20
  65.1 5.5 %all-to-all-start.2 = ((bf16[8,1,128,256]{3,2,1,0:T(8,128)(2,1)}), bf16[8,1,128,256]{3,2,1,0:T(8,128)(2,1)}, u32[]{:S(2)}, u32[]{:S(2)}) async-start(bf16[8,1,128,256]{3,2,1,0:T(8,128)(2,1)} %broadcast_in_dim.20), calls=%async_computation.2 | async-start | bytes 1048576 | tf_op jit(solution)/shard_map/all_to_all | solution.py:132
  70.6 1.9 %collective-permute-start = (bf16[8,1,128,256]{3,2,0,1:T(8,128)(2,1)S(1)}, bf16[8,1,128,256]{3,2,0,1:T(8,128)(2,1)}, u32[]{:S(2)}, u32[]{:S(2)}) collective-permute-start(bf16[8,1,128,256]{3,2,0,1:T(8,128)(2,1)S(1)} %bitcast.41), channel_id=1, source_target_pairs={{0,1},{1,0},{2,3},{3,2},{4,5},{5,4},{6,7},{7,6},{8,9},{9,8},{10,11... | collective-permute-start | bytes 1572872 | tf_op jit(solution)/shard_map/ppermute | solution.py:128
  72.5 6.0 %all-to-all-done.2 = bf16[8,1,128,256]{3,2,1,0:T(8,128)(2,1)} async-done(((bf16[8,1,128,256]{3,2,1,0:T(8,128)(2,1)}), bf16[8,1,128,256]{3,2,1,0:T(8,128)(2,1)}, u32[]{:S(2)}, u32[]{:S(2)}) %all-to-all-start.2) | async-done | bytes 524320 | tf_op jit(solution)/shard_map/all_to_all | solution.py:132
  78.5 2.0 %collective-permute-start.7 = (bf16[8,1,128,256]{3,2,0,1:T(8,128)(2,1)}, bf16[8,1,128,256]{3,2,0,1:T(8,128)(2,1)S(1)}, u32[]{:S(2)}, u32[]{:S(2)}) collective-permute-start(bf16[8,1,128,256]{3,2,0,1:T(8,128)(2,1)} %bitcast.18), channel_id=1, source_target_pairs={{0,1},{1,0},{2,3},{3,2},{4,5},{5,4},{6,7},{7,6},{8,9},{9,8},{10,11... | collective-permute-start | bytes 1572872 | tf_op jit(solution)/shard_map/ppermute | solution.py:128
  80.6 1.9 %shard_map.106.dmixed = bf16[128,256]{1,0:T(8,128)(2,1)S(1)} custom-call(s32[1]{0:T(128)} %bitcast.core_ref._, bf16[8,128,256]{2,1,0:T(8,128)(2,1)S(1)} %bitcast.40, bf16[8,128,256]{2,1,0:T(8,128)(2,1)} %bitcast.22.gb, bf16[256,4096]{1,0:T(8,128)(2,1)S(1)} %bitcast.37), custom_call_target="tpu_custom_call" | custom-call | flops 500000000 | bytes 3145728 | tf_op jit(solution)/shard_map/pallas_call | solution.py:30
  82.5 1.4 select_bitcast_fusion.1
  84.3 1.4 copy-done.1
  85.7 4.9 %shard_map.107 = (bf16[8,128,256]{2,1,0:T(8,128)(2,1)S(1)}, bf16[8,128,256]{2,1,0:T(8,128)(2,1)S(1)}) custom-call(s32[1]{0:T(128)} %bitcast.core_ref._, bf16[8,128,256]{2,1,0:T(8,128)(2,1)} %bitcast.17.xa, bf16[8,128,256]{2,1,0:T(8,128)(2,1)S(1)} %bitcast.43, f32[1,4096]{1,0:T(1,128)S(1)} %copy-done.5, bf16[4096,256]{1,0:T(8,128)(2,1)S(1)} %bitcast.35, ...), custom_call_target="tpu_custom_call" | custom-call | flops 1000000000 | bytes 5324800 | tf_op jit(solution)/shard_map/pallas_call | solution.py:30
  90.6 2.4 %collective-permute-start.9 = (bf16[8,128,256]{2,1,0:T(8,128)(2,1)S(1)}, bf16[8,128,256]{2,1,0:T(8,128)(2,1)S(1)}, u32[]{:S(2)}, u32[]{:S(2)}) collective-permute-start(bf16[8,128,256]{2,1,0:T(8,128)(2,1)S(1)} %get-tuple-element.13), channel_id=1, source_target_pairs={{0,1},{1,0},{2,3},{3,2},{4,5},{5,4},{6,7},{7,6},{8,9},{9,8},{10,11... | collective-permute-start | bytes 1572872 | tf_op jit(solution)/shard_map/ppermute | solution.py:128
  93.0 4.4 %shard_map.103 = (bf16[8,128,256]{2,1,0:T(8,128)(2,1)S(1)}, bf16[8,128,256]{2,1,0:T(8,128)(2,1)}) custom-call(s32[1]{0:T(128)} %bitcast.core_ref._, bf16[8,128,256]{2,1,0:T(8,128)(2,1)S(1)} %bitcast.42, bf16[8,128,256]{2,1,0:T(8,128)(2,1)} %bitcast.4.xb, f32[1,4096]{1,0:T(1,128)S(1)} %copy-done.5, bf16[4096,256]{1,0:T(8,128)(2,1)S(1)} %bitcast.36, ...), custom_call_target="tpu_custom_call" | custom-call | flops 1000000000 | bytes 7356416 | tf_op jit(solution)/shard_map/pallas_call | solution.py:30
  97.4 1.9 %collective-permute-start.4 = (bf16[8,128,256]{2,1,0:T(8,128)(2,1)}, bf16[8,128,256]{2,1,0:T(8,128)(2,1)S(1)}, u32[]{:S(2)}, u32[]{:S(2)}) collective-permute-start(bf16[8,128,256]{2,1,0:T(8,128)(2,1)} %get-tuple-element.10), channel_id=1, source_target_pairs={{0,1},{1,0},{2,3},{3,2},{4,5},{5,4},{6,7},{7,6},{8,9},{9,8},{10,11... | collective-permute-start | bytes 1572872 | tf_op jit(solution)/shard_map/ppermute | solution.py:128
  99.4 0.9 shard_map.108
  100.3 4.9 %all-to-all-start.4 = ((bf16[8,128,256]{2,1,0:T(8,128)(2,1)}), bf16[8,128,256]{2,1,0:T(8,128)(2,1)S(1)}, u32[]{:S(2)}, u32[]{:S(2)}) async-start(bf16[8,128,256]{2,1,0:T(8,128)(2,1)} %shard_map.108), calls=%async_computation.4 | async-start | bytes 1048576 | tf_op jit(solution)/shard_map/all_to_all | solution.py:132
  105.2 0.9 shard_map.104
  106.1 8.1 %all-to-all-done.4.got = bf16[8,128,256]{2,1,0:T(8,128)(2,1)S(1)} async-done(((bf16[8,128,256]{2,1,0:T(8,128)(2,1)}), bf16[8,128,256]{2,1,0:T(8,128)(2,1)S(1)}, u32[]{:S(2)}, u32[]{:S(2)}) %all-to-all-start.4) | async-done | bytes 524320 | tf_op jit(solution)/shard_map/all_to_all | solution.py:132
  114.2 4.8 %all-to-all-start.1 = ((bf16[8,128,256]{2,1,0:T(8,128)(2,1)}), bf16[8,128,256]{2,1,0:T(8,128)(2,1)S(1)}, u32[]{:S(2)}, u32[]{:S(2)}) async-start(bf16[8,128,256]{2,1,0:T(8,128)(2,1)} %shard_map.104), calls=%async_computation.1 | async-start | bytes 1048576 | tf_op jit(solution)/shard_map/all_to_all | solution.py:132
  119.1 12.4 %collective-permute-start.11 = (bf16[128,256]{1,0:T(8,128)(2,1)S(1)}, bf16[128,256]{1,0:T(8,128)(2,1)S(1)}, u32[]{:S(2)}, u32[]{:S(2)}) collective-permute-start(bf16[128,256]{1,0:T(8,128)(2,1)S(1)} %bitcast.47), channel_id=1, source_target_pairs={{0,496},{16,480},{32,464},{48,448},{64,432},{80,416},{96,400},{112... | collective-permute-start | bytes 196616 | tf_op jit(solution)/shard_map/ppermute | solution.py:124
  131.6 2.7 %collective-permute-start.10 = (bf16[128,256]{1,0:T(8,128)(2,1)S(1)}, bf16[128,256]{1,0:T(8,128)(2,1)S(1)}, u32[]{:S(2)}, u32[]{:S(2)}) collective-permute-start(bf16[128,256]{1,0:T(8,128)(2,1)S(1)} %shard_map.109), channel_id=1, source_target_pairs={{0,496},{16,0},{32,16},{48,32},{64,48},{80,64},{96,80},{112,96},{1... | collective-permute-start | bytes 196616 | tf_op jit(solution)/shard_map/ppermute | solution.py:120
  134.4 4.7 %collective-permute-start.5 = (bf16[128,256]{1,0:T(8,128)(2,1)S(1)}, bf16[128,256]{1,0:T(8,128)(2,1)S(1)}, u32[]{:S(2)}, u32[]{:S(2)}) collective-permute-start(bf16[128,256]{1,0:T(8,128)(2,1)S(1)} %shard_map.105), channel_id=1, source_target_pairs={{0,16},{16,32},{32,48},{48,64},{64,80},{80,96},{96,112},{112,128},... | collective-permute-start | bytes 196616 | tf_op jit(solution)/shard_map/ppermute | solution.py:120
  139.2 4.9 %collective-permute-done.5 = bf16[128,256]{1,0:T(8,128)(2,1)S(1)} collective-permute-done((bf16[128,256]{1,0:T(8,128)(2,1)S(1)}, bf16[128,256]{1,0:T(8,128)(2,1)S(1)}, u32[]{:S(2)}, u32[]{:S(2)}) %collective-permute-start.5) | collective-permute-done | bytes 65568 | tf_op jit(solution)/shard_map/ppermute | solution.py:120
  (41 shorter events, 4.9 us)
Async XLA Ops:
  0.6 48.0 %copy-start = (bf16[1,2,128,256]{3,2,1,0:T(8,128)(2,1)S(1)}, bf16[1,2,128,256]{3,2,1,0:T(8,128)(2,1)}, u32[]{:S(2)}) copy-start(bf16[1,2,128,256]{3,2,1,0:T(8,128)(2,1)} %param.10) | copy-start | bytes 393220
  0.6 16.8 %collective-permute-start.1 = (bf16[64,4096]{1,0:T(8,128)(2,1)}, bf16[64,4096]{1,0:T(8,128)(2,1)S(1)}, u32[]{:S(2)}, u32[]{:S(2)}) collective-permute-start(bf16[64,4096]{1,0:T(8,128)(2,1)} %bitcast.52), channel_id=1, source_target_pairs={{0,0},{1,1},{2,4},{3,5},{4,8},{5,9},{6,12},{7,13},{8,2},{9,3},{10,... | collective-permute-start | bytes 1572872 | tf_op jit(solution)/shard_map/ppermute | solution.py:140
  17.4 19.6 %collective-permute-start.2 = (bf16[64,4096]{1,0:T(8,128)(2,1)S(1)}, bf16[64,4096]{1,0:T(8,128)(2,1)S(1)}, u32[]{:S(2)}, u32[]{:S(2)}) collective-permute-start(bf16[64,4096]{1,0:T(8,128)(2,1)S(1)} %collective-permute-done.1), channel_id=1, source_target_pairs={{0,2},{2,0},{1,3},{3,1},{4,6},{6,4},{5,7},{7,5},{8,10},{10,8},{9,1... | collective-permute-start | bytes 1572872 | tf_op jit(solution)/shard_map/ppermute | solution.py:128
  21.7 19.3 %all-to-all-start.3 = ((bf16[8,1,128,256]{3,2,1,0:T(8,128)(2,1)}), bf16[8,1,128,256]{3,2,1,0:T(8,128)(2,1)S(1)}, u32[]{:S(2)}, u32[]{:S(2)}) async-start(bf16[8,1,128,256]{3,2,1,0:T(8,128)(2,1)} %broadcast_in_dim.21), calls=%async_computation.3 | async-start | bytes 1048576 | tf_op jit(solution)/shard_map/all_to_all | solution.py:132
  28.5 12.5 %copy-start.4 = (bf16[1,128,256]{2,1,0:T(8,128)(2,1)S(1)}, bf16[1,128,256]{2,1,0:T(8,128)(2,1)}, u32[]{:S(2)}) copy-start(bf16[1,128,256]{2,1,0:T(8,128)(2,1)} %param.8) | copy-start | bytes 196612
  37.1 0.8 copy-start.8
  37.1 4.8 %copy-start.6 = (bf16[1,64,4096]{2,1,0:T(8,128)(2,1)}, bf16[1,64,4096]{2,1,0:T(8,128)(2,1)S(1)}, u32[]{:S(2)}) copy-start(bf16[1,64,4096]{2,1,0:T(8,128)(2,1)S(1)} %get-tuple-element.17) | copy-start | bytes 1572868
  39.0 41.6 %copy-start.2 = (bf16[1,256,4096]{2,1,0:T(8,128)(2,1)S(1)}, bf16[1,256,4096]{2,1,0:T(8,128)(2,1)}, u32[]{:S(2)}) copy-start(bf16[1,256,4096]{2,1,0:T(8,128)(2,1)} %param.15) | copy-start | bytes 6291460
  39.0 43.5 %collective-permute-start.3 = (bf16[2,64,4096]{2,1,0:T(8,128)(2,1)}, bf16[2,64,4096]{2,1,0:T(8,128)(2,1)}, u32[]{:S(2)}, u32[]{:S(2)}) collective-permute-start(bf16[2,64,4096]{2,1,0:T(8,128)(2,1)} %pad_maximum_fusion.1), channel_id=1, source_target_pairs={{0,1},{1,0},{2,3},{3,2},{4,5},{5,4},{6,7},{7,6},{8,9},{9,8},{10,11... | collective-permute-start | bytes 3145736 | tf_op jit(solution)/shard_map/ppermute | solution.py:128
  41.9 22.4 %all-to-all-start = ((bf16[8,1,128,256]{3,2,1,0:T(8,128)(2,1)}), bf16[8,1,128,256]{3,2,1,0:T(8,128)(2,1)S(1)}, u32[]{:S(2)}, u32[]{:S(2)}) async-start(bf16[8,1,128,256]{3,2,1,0:T(8,128)(2,1)} %broadcast_in_dim.18), calls=%async_computation | async-start | bytes 1048576 | tf_op jit(solution)/shard_map/all_to_all | solution.py:132
  48.6 15.6 %collective-permute-start.6 = (bf16[128,256]{1,0:T(8,128)(2,1)S(1)}, bf16[128,256]{1,0:T(8,128)(2,1)S(1)}, u32[]{:S(2)}, u32[]{:S(2)}) collective-permute-start(bf16[128,256]{1,0:T(8,128)(2,1)S(1)} %dynamic-slice_bitcast_fusion), channel_id=1, source_target_pairs={{0,496},{16,480},{32,464},{48,448},{64,432},{80,416},{96,400},{112... | collective-permute-start | bytes 196616 | tf_op jit(solution)/shard_map/ppermute | solution.py:124
  61.7 18.8 %collective-permute-start.8 = (bf16[8,1,128,256]{3,2,0,1:T(8,128)(2,1)S(1)}, bf16[8,1,128,256]{3,2,0,1:T(8,128)(2,1)}, u32[]{:S(2)}, u32[]{:S(2)}) collective-permute-start(bf16[8,1,128,256]{3,2,0,1:T(8,128)(2,1)S(1)} %bitcast.39), channel_id=1, source_target_pairs={{0,1},{1,0},{2,3},{3,2},{4,5},{5,4},{6,7},{7,6},{8,9},{9,8},{10,11... | collective-permute-start | bytes 1572872 | tf_op jit(solution)/shard_map/ppermute | solution.py:128
  65.1 13.4 %all-to-all-start.2 = ((bf16[8,1,128,256]{3,2,1,0:T(8,128)(2,1)}), bf16[8,1,128,256]{3,2,1,0:T(8,128)(2,1)}, u32[]{:S(2)}, u32[]{:S(2)}) async-start(bf16[8,1,128,256]{3,2,1,0:T(8,128)(2,1)} %broadcast_in_dim.20), calls=%async_computation.2 | async-start | bytes 1048576 | tf_op jit(solution)/shard_map/all_to_all | solution.py:132
  70.6 22.4 %collective-permute-start = (bf16[8,1,128,256]{3,2,0,1:T(8,128)(2,1)S(1)}, bf16[8,1,128,256]{3,2,0,1:T(8,128)(2,1)}, u32[]{:S(2)}, u32[]{:S(2)}) collective-permute-start(bf16[8,1,128,256]{3,2,0,1:T(8,128)(2,1)S(1)} %bitcast.41), channel_id=1, source_target_pairs={{0,1},{1,0},{2,3},{3,2},{4,5},{5,4},{6,7},{7,6},{8,9},{9,8},{10,11... | collective-permute-start | bytes 1572872 | tf_op jit(solution)/shard_map/ppermute | solution.py:128
  78.5 4.0 %copy-start.7 = (bf16[1,64,4096]{2,1,0:T(8,128)(2,1)S(1)}, bf16[1,64,4096]{2,1,0:T(8,128)(2,1)}, u32[]{:S(2)}) copy-start(bf16[1,64,4096]{2,1,0:T(8,128)(2,1)} %copy-done.6) | copy-start | bytes 1572868
  78.5 4.0 %copy-start.9 = (bf16[1,64,4096]{2,1,0:T(8,128)(2,1)S(1)}, bf16[1,64,4096]{2,1,0:T(8,128)(2,1)}, u32[]{:S(2)}) copy-start(bf16[1,64,4096]{2,1,0:T(8,128)(2,1)} %copy-done.8) | copy-start | bytes 1572868
  78.5 5.8 %collective-permute-start.7 = (bf16[8,1,128,256]{3,2,0,1:T(8,128)(2,1)}, bf16[8,1,128,256]{3,2,0,1:T(8,128)(2,1)S(1)}, u32[]{:S(2)}, u32[]{:S(2)}) collective-permute-start(bf16[8,1,128,256]{3,2,0,1:T(8,128)(2,1)} %bitcast.18), channel_id=1, source_target_pairs={{0,1},{1,0},{2,3},{3,2},{4,5},{5,4},{6,7},{7,6},{8,9},{9,8},{10,11... | collective-permute-start | bytes 1572872 | tf_op jit(solution)/shard_map/ppermute | solution.py:128
  84.1 1.6 %copy-start.1 = (bf16[1,4096,256]{2,1,0:T(8,128)(2,1)S(1)}, bf16[1,4096,256]{2,1,0:T(8,128)(2,1)}, u32[]{:S(2)}) copy-start(bf16[1,4096,256]{2,1,0:T(8,128)(2,1)} %param.13) | copy-start | bytes 6291460
  84.1 1.6 %copy-start.5 = (f32[1,4096]{1,0:T(1,128)S(1)}, f32[1,4096]{1,0:T(1,128)}, u32[]{:S(2)}) copy-start(f32[1,4096]{1,0:T(1,128)} %gain.3) | copy-start | bytes 49156
  90.6 8.8 %collective-permute-start.9 = (bf16[8,128,256]{2,1,0:T(8,128)(2,1)S(1)}, bf16[8,128,256]{2,1,0:T(8,128)(2,1)S(1)}, u32[]{:S(2)}, u32[]{:S(2)}) collective-permute-start(bf16[8,128,256]{2,1,0:T(8,128)(2,1)S(1)} %get-tuple-element.13), channel_id=1, source_target_pairs={{0,1},{1,0},{2,3},{3,2},{4,5},{5,4},{6,7},{7,6},{8,9},{9,8},{10,11... | collective-permute-start | bytes 1572872 | tf_op jit(solution)/shard_map/ppermute | solution.py:128
  97.4 7.8 %collective-permute-start.4 = (bf16[8,128,256]{2,1,0:T(8,128)(2,1)}, bf16[8,128,256]{2,1,0:T(8,128)(2,1)S(1)}, u32[]{:S(2)}, u32[]{:S(2)}) collective-permute-start(bf16[8,128,256]{2,1,0:T(8,128)(2,1)} %get-tuple-element.10), channel_id=1, source_target_pairs={{0,1},{1,0},{2,3},{3,2},{4,5},{5,4},{6,7},{7,6},{8,9},{9,8},{10,11... | collective-permute-start | bytes 1572872 | tf_op jit(solution)/shard_map/ppermute | solution.py:128
  100.3 31.2 %copy-start.3 = (bf16[1,128,256]{2,1,0:T(8,128)(2,1)S(1)}, bf16[1,128,256]{2,1,0:T(8,128)(2,1)}, u32[]{:S(2)}) copy-start(bf16[1,128,256]{2,1,0:T(8,128)(2,1)} %param.9) | copy-start | bytes 196612
  100.3 13.9 %all-to-all-start.4 = ((bf16[8,128,256]{2,1,0:T(8,128)(2,1)}), bf16[8,128,256]{2,1,0:T(8,128)(2,1)S(1)}, u32[]{:S(2)}, u32[]{:S(2)}) async-start(bf16[8,128,256]{2,1,0:T(8,128)(2,1)} %shard_map.108), calls=%async_computation.4 | async-start | bytes 1048576 | tf_op jit(solution)/shard_map/all_to_all | solution.py:132
  114.2 20.0 %all-to-all-start.1 = ((bf16[8,128,256]{2,1,0:T(8,128)(2,1)}), bf16[8,128,256]{2,1,0:T(8,128)(2,1)S(1)}, u32[]{:S(2)}, u32[]{:S(2)}) async-start(bf16[8,128,256]{2,1,0:T(8,128)(2,1)} %shard_map.104), calls=%async_computation.1 | async-start | bytes 1048576 | tf_op jit(solution)/shard_map/all_to_all | solution.py:132
  119.1 19.9 %collective-permute-start.11 = (bf16[128,256]{1,0:T(8,128)(2,1)S(1)}, bf16[128,256]{1,0:T(8,128)(2,1)S(1)}, u32[]{:S(2)}, u32[]{:S(2)}) collective-permute-start(bf16[128,256]{1,0:T(8,128)(2,1)S(1)} %bitcast.47), channel_id=1, source_target_pairs={{0,496},{16,480},{32,464},{48,448},{64,432},{80,416},{96,400},{112... | collective-permute-start | bytes 196616 | tf_op jit(solution)/shard_map/ppermute | solution.py:124
  131.6 7.7 %collective-permute-start.10 = (bf16[128,256]{1,0:T(8,128)(2,1)S(1)}, bf16[128,256]{1,0:T(8,128)(2,1)S(1)}, u32[]{:S(2)}, u32[]{:S(2)}) collective-permute-start(bf16[128,256]{1,0:T(8,128)(2,1)S(1)} %shard_map.109), channel_id=1, source_target_pairs={{0,496},{16,0},{32,16},{48,32},{64,48},{80,64},{96,80},{112,96},{1... | collective-permute-start | bytes 196616 | tf_op jit(solution)/shard_map/ppermute | solution.py:120
  134.4 9.8 %collective-permute-start.5 = (bf16[128,256]{1,0:T(8,128)(2,1)S(1)}, bf16[128,256]{1,0:T(8,128)(2,1)S(1)}, u32[]{:S(2)}, u32[]{:S(2)}) collective-permute-start(bf16[128,256]{1,0:T(8,128)(2,1)S(1)} %shard_map.105), channel_id=1, source_target_pairs={{0,16},{16,32},{32,48},{48,64},{64,80},{80,96},{96,112},{112,128},... | collective-permute-start | bytes 196616 | tf_op jit(solution)/shard_map/ppermute | solution.py:120

commit v3 on v2

v3 whole, which is shorter than its diff:
```python
import jax
import jax.numpy as jnp
from jax import lax
from jax.experimental import pallas as pl
from jax.experimental.pallas import tpu as pltpu
from jax.sharding import Mesh, PartitionSpec as P

HEAD_DIM = 128
EPS = 1e-05
SCALE = HEAD_DIM ** (-0.5)
D = 4096
T = 128
W = 256
N = D // W

SEC = ("z", "yh")
TEN = ("x", "yl", "c")
F32 = jnp.float32
BF16 = jnp.bfloat16
NT = (((1,), (1,)), ((), ()))
TN = (((0,), (0,)), ((), ()))


def dot(a, b, dims=(((1,), (0,)), ((), ()))):
    return lax.dot_general(a, b, dims, preferred_element_type=F32)


def call(kernel, outs, core, *args, after=(), scratch=(), flops=0):
    nbytes = sum(a.size * a.dtype.itemsize for a in args)

    def ordered(core_ref, *refs):
        kernel(core_ref, *refs[: len(args)], *refs[len(args) + len(after) :])

    return pl.pallas_call(
        ordered,
        out_shape=tuple(pltpu.VMEM(s, d) for s, d in outs),
        in_specs=[pl.BlockSpec(memory_space=pltpu.SMEM)]
        + [pl.BlockSpec(memory_space=pltpu.VMEM)] * len(args)
        + [pl.BlockSpec(memory_space=pl.ANY)] * len(after),
        out_specs=tuple(pl.BlockSpec(memory_space=pltpu.VMEM) for _ in outs),
        scratch_shapes=list(scratch),
        compiler_params=pltpu.CompilerParams(vmem_limit_bytes=24 * 2**20),
        cost_estimate=pl.CostEstimate(flops=flops, bytes_accessed=nbytes, transcendentals=0),
    )(core, *(pltpu.with_memory_space_constraint(a, pltpu.VMEM) for a in args), *after)


def blocks(core, own, other, which=0):
    for ref, side in ((own, core), (other, 1 - core)):
        for j in range(8):
            yield ref.at[j, which], pl.multiple_of((2 * j + side) * W, W)


def recompute(core, xa, xb, which, gain, wq, wkv, xg):
    squares = jnp.zeros((T, W), F32)
    for x, at in blocks(core, xa, xb, which):
        wide = x[...].astype(F32)
        squares += wide * wide
        xg[:, pl.ds(at, W)] = (wide * gain[:, pl.ds(at, W)]).astype(BF16)
    inv = lax.rsqrt(jnp.sum(squares, axis=-1, keepdims=True) * (1.0 / D) + EPS)
    q = dot(xg[...], wq[...]) * inv
    kv = dot(xg[...], wkv[...], NT) * inv
    qb, kvb = q.astype(BF16), kv.astype(BF16)
    k, v = kvb[:, :HEAD_DIM], kvb[:, HEAD_DIM:]
    row = lax.broadcasted_iota(jnp.int32, (T, T), 0)
    col = lax.broadcasted_iota(jnp.int32, (T, T), 1)
    probs = []
    for h in range(2):
        s = dot(qb[:, h * HEAD_DIM : (h + 1) * HEAD_DIM], k, NT) * SCALE
        s = jnp.where(row >= col, s, F32(-1e30))
        e = jnp.exp(s - jnp.max(s, axis=-1, keepdims=True))
        probs.append(e / jnp.sum(e, axis=-1, keepdims=True))
    return inv, q, kv, qb, k, v, probs


def forward_kernel(core_ref, xa, xb, gain, wq, wkv, wo, keep, send, xg):
    core = core_ref[0]
    _, _, _, _, _, v, probs = recompute(core, xa, xb, 0, gain, wq, wkv, xg)
    mixed = jnp.concatenate([dot(p.astype(BF16), v).astype(BF16) for p in probs], axis=1)
    for out, at in blocks(core, keep, send):
        out[...] = dot(mixed, wo[:, pl.ds(at, W)]).astype(BF16)


def dmixed_kernel(core_ref, ga, gb, wo, dmixed, g):
    for block, at in blocks(core_ref[0], ga, gb):
        g[:, pl.ds(at, W)] = block[...]
    dmixed[...] = dot(g[...], wo[...], NT).astype(BF16)


def backward_kernel(core_ref, xa, xb, gain, wq, wkv, dmixed, keep, send, xg):
    core = core_ref[0]
    inv, q, kv, qb, k, v, probs = recompute(core, xa, xb, 1, gain, wq, wkv, xg)
    dq, dk, dv = [], 0.0, 0.0
    for h, p in enumerate(probs):
        lanes = slice(h * HEAD_DIM, (h + 1) * HEAD_DIM)
        dm = dmixed[:, lanes]
        dprob = dot(dm, v, NT)
        rowdot = jnp.sum(p * dprob, axis=-1, keepdims=True)
        dscore = (p * (dprob - rowdot)).astype(BF16)
        dq.append(dot(dscore, k) * SCALE)
        dk += dot(dscore, qb[:, lanes], TN)
        dv += dot(p.astype(BF16), dm, TN)
    dq = jnp.concatenate(dq, axis=1)
    dkv = jnp.concatenate([dk * SCALE, dv], axis=1)
    share = jnp.sum(dq * q + dkv * kv, axis=-1, keepdims=True)
    coef = inv * inv * share * (1.0 / D)
    dqs, dkvs = (dq * inv).astype(BF16), (dkv * inv).astype(BF16)
    for (out, at), (x, _) in zip(blocks(core, keep, send), blocks(core, xa, xb, 1)):
        term = dot(dqs, wq[pl.ds(at, W), :], NT) + dot(dkvs, wkv[:, pl.ds(at, W)])
        term = term * gain[:, pl.ds(at, W)] - coef * x[...].astype(F32)
        out[...] = term.astype(BF16)


def spread_kernel(_, *refs):
    *blocks_in, out = refs
    for i, block in enumerate(blocks_in):
        for j in range(8):
            out[j, i] = block[...]


def copy_kernel(_, block, out):
    out[...] = block[...]


def assemble_kernel(place, first, other, twin_first, twin_other, out):
    core, low = place[0], place[1]
    rows = first.shape[0]
    for ref, half, side in (
        (first, low, core),
        (other, 1 - low, core),
        (twin_first, low, 1 - core),
        (twin_other, 1 - low, 1 - core),
    ):
        out[pl.ds(pl.multiple_of((2 * half + side) * rows, rows), rows), :] = ref[...]


def pair_kernel(_, keep, got, out):
    out[...] = (keep[...].astype(F32) + got[...].astype(F32)).astype(BF16)


def finish_kernel(_, base, got, out):
    total = base[...].astype(F32)
    for j in range(8):
        total += got[j, 0].astype(F32)
    out[...] = total.astype(BF16)


def shift(block, distance):
    return lax.ppermute(block, SEC, [(i, (i + distance) % 32) for i in range(32)])


def mirror(block):
    return lax.ppermute(block, SEC, [(i, 31 - i) for i in range(32)])


def swap(block, axis):
    return lax.ppermute(block, axis, [(0, 1), (1, 0)])


def exchange(parts):
    return lax.all_to_all(parts, ("x", "yl"), 0, 0, tiled=True)


def body(section_input, section_grad, mirror_store, fetch_slot, norm_gain, w_query, w_keyval, w_output):
    x_cols, g_cols = section_input[0], section_grad[0]
    gain, wq, wo, keyval_w = norm_gain, w_query[0], w_output[0], w_keyval[0]
    core = lax.axis_index("c").astype(jnp.int32).reshape(1)
    place = jnp.stack([lax.axis_index("c"), lax.axis_index("yl")]).astype(jnp.int32)
    tile = ((T, W), BF16)
    half = ((8, 1, T, W), BF16)
    xg = pltpu.VMEM((T, D), BF16)

    def gather(*parts, after=()):
        n = len(parts)
        (spread,) = call(spread_kernel, [((8, n, T, W), BF16)], core, *parts, after=after)
        own = exchange(spread)
        return own, swap(own, "c")

    def total(base, keep, send, after=()):
        (pair,) = call(pair_kernel, [half], core, keep, swap(send, "c"), after=after)
        (out,) = call(finish_kernel, [tile], core, base, exchange(pair))
        return out

    fetched = mirror(mirror_store[0][fetch_slot[0]])

    route = []
    for r in range(16):
        part, g = divmod(r // 2, 4)
        route.append((r, 4 * g + 2 * part + r % 2))
    first = lax.ppermute(keyval_w, TEN, route)
    (first,) = call(copy_kernel, [(first.shape, BF16)], core, first, after=(fetched,))
    other = swap(first, "yl")
    (wkv,) = call(
        assemble_kernel, [((W, D), BF16)], place, first, other, swap(first, "c"), swap(other, "c")
    )

    ga, gb = gather(g_cols)
    xa, xb = gather(x_cols, fetched)
    (x_late,) = call(copy_kernel, [tile], core, x_cols, after=(fetched,))
    evicted = mirror(x_late)

    keep, send = call(
        forward_kernel, [half, half], core, xa, xb, gain, wq, wkv, wo, scratch=[xg], flops=10**9
    )
    forward_next = shift(total(x_cols, keep, send, after=(evicted,)), 1)

    (dmixed,) = call(dmixed_kernel, [tile], core, ga, gb, wo, scratch=[xg], flops=5 * 10**8)
    keep, send = call(
        backward_kernel, [half, half], core, xa, xb, gain, wq, wkv, dmixed, scratch=[xg], flops=10**9
    )
    grad_prev = shift(total(g_cols, keep, send), -1)
    return forward_next[None], grad_prev[None], evicted[None]


def solution(mesh):
    fine = Mesh(mesh.devices.reshape(16, 2, 4, 2, 2), SEC + TEN)
    cols = P(SEC, None, TEN)
    return jax.shard_map(
        body,
        mesh=fine,
        in_specs=(
            cols,
            cols,
            P(SEC, None, None, TEN),
            P(SEC),
            P(SEC, None),
            cols,
            P(SEC, TEN, None),
            P(SEC, TEN, None),
        ),
        out_specs=(cols, cols, cols),
        check_vma=False,
    )
```

time: 147 us -> 147 us (level)
  the two profiles are of different devices: /device:TPU:130 before, /device:TPU:8 now
where the time goes in v3:
time: 147 us; the launch traced here: 146 us
  waiting for transfers between devices  53.4 us (36%)
  starting transfers between devices  53.2 us (36%)
  blocking collectives  16.5 us (11%)
  Pallas kernels  16.4 us (11%)
  local copies, waits for them, and re-layouts  5.14 us (3%)
  between operations  1.57 us (1%)
    ppermute x1, waiting for transfers between devices, body(): first = lax.ppermute(keyval_w, TEN, route)  22.7 us
    ppermute x2, waiting for transfers between devices, mirror(): return lax.ppermute(block, SEC, [(i, 31 - i) for i in range(32)])  17.3 us
    all_to_all x1, blocking collectives, exchange(): return lax.all_to_all(parts, ('x', 'yl'), 0, 0, tiled=True)  16.5 us
    pallas_call x12, Pallas kernels, call(): pl.pallas_call(ordered, out_shape=tuple((pltpu.VMEM(s, d) for s, d in out...  16.4 us
    ppermute x2, starting transfers between devices, mirror(): return lax.ppermute(block, SEC, [(i, 31 - i) for i in range(32)])  16 us
    all_to_all x3, starting transfers between devices, exchange(): return lax.all_to_all(parts, ('x', 'yl'), 0, 0, tiled=True)  15.5 us
    ppermute x7, starting transfers between devices, swap(): return lax.ppermute(block, axis, [(0, 1), (1, 0)])  14.5 us
    ppermute x2, waiting for transfers between devices, shift(): lax.ppermute(block, SEC, [(i, (i + distance) % 32) for i in range(32)])  7.84 us
  transfers between devices with their start and end apart: 15, of which 5 were waited for; matrix products, arithmetic and copies ran while one was open for 0% of the time, Pallas kernels for 8%

profile of v3, /device:TPU:8, one launch (start us, length us, event | category | flops | bytes accessed | tf_op | source)
XLA Modules:
  0.0 146.3 jit_solution(66798420151835851)
XLA Ops:
  1.6 13.1 %collective-permute-start = (bf16[128,256]{1,0:T(8,128)(2,1)S(1)}, bf16[128,256]{1,0:T(8,128)(2,1)S(1)}, u32[]{:S(2)}, u32[]{:S(2)}) collective-permute-start(bf16[128,256]{1,0:T(8,128)(2,1)S(1)} %dynamic-slice_bitcast_fusion), channel_id=1, source_target_pairs={{0,496},{16,480},{32,464},{48,448},{64,432},{80,416},{96,400},{112... | collective-permute-start | bytes 196616 | tf_op jit(solution)/shard_map/ppermute | solution.py:152
  14.7 6.3 %collective-permute-done.refs_1_ = bf16[128,256]{1,0:T(8,128)(2,1)S(1)} collective-permute-done((bf16[128,256]{1,0:T(8,128)(2,1)S(1)}, bf16[128,256]{1,0:T(8,128)(2,1)S(1)}, u32[]{:S(2)}, u32[]{:S(2)}) %collective-permute-start) | collective-permute-done | bytes 65568 | tf_op jit(solution)/shard_map/ppermute | solution.py:152
  21.0 0.8 copy-done.4
  21.9 1.0 copy-done.3
  22.9 5.9 %all-to-all-start = ((bf16[8,2,128,256]{3,2,1,0:T(8,128)(2,1)}), bf16[8,2,128,256]{3,2,1,0:T(8,128)(2,1)S(1)}, u32[]{:S(2)}, u32[]{:S(2)}) async-start(bf16[8,2,128,256]{3,2,1,0:T(8,128)(2,1)} %copy-done.3), calls=%async_computation | async-start | bytes 2097152 | tf_op jit(solution)/shard_map/all_to_all | solution.py:160
  28.8 3.4 %collective-permute-start.2 = (bf16[64,4096]{1,0:T(8,128)(2,1)}, bf16[64,4096]{1,0:T(8,128)(2,1)S(1)}, u32[]{:S(2)}, u32[]{:S(2)}) collective-permute-start(bf16[64,4096]{1,0:T(8,128)(2,1)} %bitcast.28), channel_id=1, source_target_pairs={{0,0},{1,1},{2,4},{3,5},{4,8},{5,9},{6,12},{7,13},{8,2},{9,3},{10,... | collective-permute-start | bytes 1572872 | tf_op jit(solution)/shard_map/ppermute | solution.py:189
  32.1 22.7 %collective-permute-done.2.refs_0_ = bf16[64,4096]{1,0:T(8,128)(2,1)S(1)} collective-permute-done((bf16[64,4096]{1,0:T(8,128)(2,1)}, bf16[64,4096]{1,0:T(8,128)(2,1)S(1)}, u32[]{:S(2)}, u32[]{:S(2)}) %collective-permute-start.2) | collective-permute-done | bytes 524320 | tf_op jit(solution)/shard_map/ppermute | solution.py:189
  54.9 0.8 shard_map.104.refs_0_
  55.7 1.9 %collective-permute-start.3 = (bf16[64,4096]{1,0:T(8,128)(2,1)}, bf16[64,4096]{1,0:T(8,128)(2,1)}, u32[]{:S(2)}, u32[]{:S(2)}) collective-permute-start(bf16[64,4096]{1,0:T(8,128)(2,1)} %shard_map.104.refs_0_), channel_id=1, source_target_pairs={{0,2},{2,0},{1,3},{3,1},{4,6},{6,4},{5,7},{7,5},{8,10},{10,8},{9,1... | collective-permute-start | bytes 1572872 | tf_op jit(solution)/shard_map/ppermute | solution.py:156
  57.6 1.9 %collective-permute-start.1 = (bf16[8,2,128,256]{3,2,1,0:T(8,128)(2,1)S(1)}, bf16[8,2,128,256]{3,2,1,0:T(8,128)(2,1)}, u32[]{:S(2)}, u32[]{:S(2)}) collective-permute-start(bf16[8,2,128,256]{3,2,1,0:T(8,128)(2,1)S(1)} %all-to-all-done.refs_0_), channel_id=1, source_target_pairs={{0,1},{1,0},{2,3},{3,2},{4,5},{5,4},{6,7},{7,6},{8,9},{9,8},{10,11... | collective-permute-start | bytes 3145736 | tf_op jit(solution)/shard_map/ppermute | solution.py:156
  59.6 16.5 %all_to_all.20.refs_0_ = bf16[8,1,128,256]{3,2,1,0:T(8,128)(2,1)} all-to-all(bf16[8,1,128,256]{3,2,1,0:T(8,128)(2,1)S(1)} %shard_map.110), channel_id=1, replica_groups=mesh['z'=16,'yh'=2,'x'=4,'yl'=2,'c'=2] {'x','yl'}, dimensions={0} | all-to-all | bytes 1048576 | tf_op jit(solution)/shard_map/all_to_all | solution.py:160
  76.1 1.9 %collective-permute-start.9 = (bf16[8,1,128,256]{3,2,1,0:T(8,128)(2,1)}, bf16[8,1,128,256]{3,2,1,0:T(8,128)(2,1)}, u32[]{:S(2)}, u32[]{:S(2)}) collective-permute-start(bf16[8,1,128,256]{3,2,1,0:T(8,128)(2,1)} %all_to_all.20.refs_0_), channel_id=1, source_target_pairs={{0,1},{1,0},{2,3},{3,2},{4,5},{5,4},{6,7},{7,6},{8,9},{9,8},{10,11... | collective-permute-start | bytes 1572872 | tf_op jit(solution)/shard_map/ppermute | solution.py:156
  78.0 2.4 %collective-permute-start.4 = (bf16[64,4096]{1,0:T(8,128)(2,1)}, bf16[64,4096]{1,0:T(8,128)(2,1)}, u32[]{:S(2)}, u32[]{:S(2)}) collective-permute-start(bf16[64,4096]{1,0:T(8,128)(2,1)} %shard_map.104.refs_0_), channel_id=1, source_target_pairs={{0,1},{1,0},{2,3},{3,2},{4,5},{5,4},{6,7},{7,6},{8,9},{9,8},{10,11... | collective-permute-start | bytes 1572872 | tf_op jit(solution)/shard_map/ppermute | solution.py:156
  80.5 1.9 %collective-permute-start.5 = (bf16[64,4096]{1,0:T(8,128)(2,1)}, bf16[64,4096]{1,0:T(8,128)(2,1)}, u32[]{:S(2)}, u32[]{:S(2)}) collective-permute-start(bf16[64,4096]{1,0:T(8,128)(2,1)} %collective-permute-done.3.refs_1_), channel_id=1, source_target_pairs={{0,1},{1,0},{2,3},{3,2},{4,5},{5,4},{6,7},{7,6},{8,9},{9,8},{10,11... | collective-permute-start | bytes 1572872 | tf_op jit(solution)/shard_map/ppermute | solution.py:156
  82.5 2.1 %shard_map.111.refs_5_ = bf16[128,256]{1,0:T(8,128)(2,1)S(1)} custom-call(s32[1]{0:T(128)} %bitcast.core_ref, bf16[8,1,128,256]{3,2,1,0:T(8,128)(2,1)} %all_to_all.20.refs_0_, bf16[8,1,128,256]{3,2,1,0:T(8,128)(2,1)} %collective-permute-done.9.refs_1_, bf16[256,4096]{1,0:T(8,128)(2,1)S(1)} %bitcast.18), custom_call_target="tpu_custom_call" | custom-call | flops 500000000 | bytes 3145728 | tf_op jit(solution)/shard_map/pallas_call | solution.py:34
  84.6 1.8 %shard_map.105.refs_4_ = bf16[256,4096]{1,0:T(8,128)(2,1)S(1)} custom-call(s32[2]{0:T(128)S(1)} %pad_add_fusion.core_ref, bf16[64,4096]{1,0:T(8,128)(2,1)} %shard_map.104.refs_0_, bf16[64,4096]{1,0:T(8,128)(2,1)} %collective-permute-done.3.refs_1_, bf16[64,4096]{1,0:T(8,128)(2,1)} %collective-permute-done.4.refs_2_, ...), custom_call_target="tpu_custom_call" | custom-call | bytes 2097152 | tf_op jit(solution)/shard_map/pallas_call | solution.py:34
  86.8 5.0 %shard_map.112 = (bf16[8,1,128,256]{3,2,1,0:T(8,128)(2,1)S(1)}, bf16[8,1,128,256]{3,2,1,0:T(8,128)(2,1)S(1)}) custom-call(s32[1]{0:T(128)} %bitcast.core_ref, bf16[8,2,128,256]{3,2,1,0:T(8,128)(2,1)S(1)} %all-to-all-done.refs_0_, bf16[8,2,128,256]{3,2,1,0:T(8,128)(2,1)} %collective-permute-done.1.refs_1_, f32[1,4096]{1,0:T(1,128)S(1)} %copy-done.9, ...), custom_call_target="tpu_custom_call" | custom-call | flops 1000000000 | bytes 6373376 | tf_op jit(solution)/shard_map/pallas_call | solution.py:34
  91.8 2.4 %collective-permute-start.10 = (bf16[8,1,128,256]{3,2,1,0:T(8,128)(2,1)S(1)}, bf16[8,1,128,256]{3,2,1,0:T(8,128)(2,1)S(1)}, u32[]{:S(2)}, u32[]{:S(2)}) collective-permute-start(bf16[8,1,128,256]{3,2,1,0:T(8,128)(2,1)S(1)} %get-tuple-element.10), channel_id=1, source_target_pairs={{0,1},{1,0},{2,3},{3,2},{4,5},{5,4},{6,7},{7,6},{8,9},{9,8},{10,11... | collective-permute-start | bytes 1572872 | tf_op jit(solution)/shard_map/ppermute | solution.py:156
  94.2 4.6 %shard_map.106 = (bf16[8,1,128,256]{3,2,1,0:T(8,128)(2,1)S(1)}, bf16[8,1,128,256]{3,2,1,0:T(8,128)(2,1)}) custom-call(s32[1]{0:T(128)} %bitcast.core_ref, bf16[8,2,128,256]{3,2,1,0:T(8,128)(2,1)S(1)} %all-to-all-done.refs_0_, bf16[8,2,128,256]{3,2,1,0:T(8,128)(2,1)} %collective-permute-done.1.refs_1_, f32[1,4096]{1,0:T(1,128)S(1)} %copy-done.9, ...), custom_call_target="tpu_custom_call" | custom-call | flops 1000000000 | bytes 8404992 | tf_op jit(solution)/shard_map/pallas_call | solution.py:34
  98.8 0.8 copy-done.6
  99.6 2.0 %collective-permute-start.6 = (bf16[8,1,128,256]{3,2,1,0:T(8,128)(2,1)}, bf16[8,1,128,256]{3,2,1,0:T(8,128)(2,1)S(1)}, u32[]{:S(2)}, u32[]{:S(2)}) collective-permute-start(bf16[8,1,128,256]{3,2,1,0:T(8,128)(2,1)} %get-tuple-element.8), channel_id=1, source_target_pairs={{0,1},{1,0},{2,3},{3,2},{4,5},{5,4},{6,7},{7,6},{8,9},{9,8},{10,11... | collective-permute-start | bytes 1572872 | tf_op jit(solution)/shard_map/ppermute | solution.py:156
  101.7 0.9 shard_map.113
  102.6 3.9 %all-to-all-start.3 = ((bf16[8,1,128,256]{3,2,1,0:T(8,128)(2,1)}), bf16[8,1,128,256]{3,2,1,0:T(8,128)(2,1)S(1)}, u32[]{:S(2)}, u32[]{:S(2)}) async-start(bf16[8,1,128,256]{3,2,1,0:T(8,128)(2,1)} %shard_map.113), calls=%async_computation.3 | async-start | bytes 1048576 | tf_op jit(solution)/shard_map/all_to_all | solution.py:160
  106.5 2.8 %collective-permute-start.7 = (bf16[128,256]{1,0:T(8,128)(2,1)S(1)}, bf16[128,256]{1,0:T(8,128)(2,1)S(1)}, u32[]{:S(2)}, u32[]{:S(2)}) collective-permute-start(bf16[128,256]{1,0:T(8,128)(2,1)S(1)} %shard_map.107), channel_id=1, source_target_pairs={{0,496},{16,480},{32,464},{48,448},{64,432},{80,416},{96,400},{112... | collective-permute-start | bytes 196616 | tf_op jit(solution)/shard_map/ppermute | solution.py:152
  109.3 11.0 %collective-permute-done.7.refs_2_ = bf16[128,256]{1,0:T(8,128)(2,1)S(1)} collective-permute-done((bf16[128,256]{1,0:T(8,128)(2,1)S(1)}, bf16[128,256]{1,0:T(8,128)(2,1)S(1)}, u32[]{:S(2)}, u32[]{:S(2)}) %collective-permute-start.7) | collective-permute-done | bytes 65568 | tf_op jit(solution)/shard_map/ppermute | solution.py:152
  120.4 0.9 shard_map.108
  121.3 5.7 %all-to-all-start.1 = ((bf16[8,1,128,256]{3,2,1,0:T(8,128)(2,1)}), bf16[8,1,128,256]{3,2,1,0:T(8,128)(2,1)S(1)}, u32[]{:S(2)}, u32[]{:S(2)}) async-start(bf16[8,1,128,256]{3,2,1,0:T(8,128)(2,1)} %shard_map.108), calls=%async_computation.1 | async-start | bytes 1048576 | tf_op jit(solution)/shard_map/all_to_all | solution.py:160
  127.1 1.9 %collective-permute-start.11 = (bf16[128,256]{1,0:T(8,128)(2,1)S(1)}, bf16[128,256]{1,0:T(8,128)(2,1)S(1)}, u32[]{:S(2)}, u32[]{:S(2)}) collective-permute-start(bf16[128,256]{1,0:T(8,128)(2,1)S(1)} %shard_map.114), channel_id=1, source_target_pairs={{0,496},{16,0},{32,16},{48,32},{64,48},{80,64},{96,80},{112,96},{1... | collective-permute-start | bytes 196616 | tf_op jit(solution)/shard_map/ppermute | solution.py:148
  129.0 5.5 %all-to-all-done.1.refs_1_ = bf16[8,1,128,256]{3,2,1,0:T(8,128)(2,1)S(1)} async-done(((bf16[8,1,128,256]{3,2,1,0:T(8,128)(2,1)}), bf16[8,1,128,256]{3,2,1,0:T(8,128)(2,1)S(1)}, u32[]{:S(2)}, u32[]{:S(2)}) %all-to-all-start.1) | async-done | bytes 524320 | tf_op jit(solution)/shard_map/all_to_all | solution.py:160
  134.6 1.9 %collective-permute-start.8 = (bf16[128,256]{1,0:T(8,128)(2,1)S(1)}, bf16[128,256]{1,0:T(8,128)(2,1)S(1)}, u32[]{:S(2)}, u32[]{:S(2)}) collective-permute-start(bf16[128,256]{1,0:T(8,128)(2,1)S(1)} %shard_map.109), channel_id=1, source_target_pairs={{0,16},{16,32},{32,48},{48,64},{64,80},{80,96},{96,112},{112,128},... | collective-permute-start | bytes 196616 | tf_op jit(solution)/shard_map/ppermute | solution.py:148
  136.6 7.8 %collective-permute-done.8 = bf16[128,256]{1,0:T(8,128)(2,1)S(1)} collective-permute-done((bf16[128,256]{1,0:T(8,128)(2,1)S(1)}, bf16[128,256]{1,0:T(8,128)(2,1)S(1)}, u32[]{:S(2)}, u32[]{:S(2)}) %collective-permute-start.8) | collective-permute-done | bytes 65568 | tf_op jit(solution)/shard_map/ppermute | solution.py:148
  144.4 0.6 copy.15
  (36 shorter events, 2.3 us)
Async XLA Ops:
  0.6 0.9 copy-start
  1.6 19.4 %collective-permute-start = (bf16[128,256]{1,0:T(8,128)(2,1)S(1)}, bf16[128,256]{1,0:T(8,128)(2,1)S(1)}, u32[]{:S(2)}, u32[]{:S(2)}) collective-permute-start(bf16[128,256]{1,0:T(8,128)(2,1)S(1)} %dynamic-slice_bitcast_fusion), channel_id=1, source_target_pairs={{0,496},{16,480},{32,464},{48,448},{64,432},{80,416},{96,400},{112... | collective-permute-start | bytes 196616 | tf_op jit(solution)/shard_map/ppermute | solution.py:152
  21.0 0.8 copy-start.4
  21.8 37.7 %copy-start.8 = (bf16[1,128,256]{2,1,0:T(8,128)(2,1)S(1)}, bf16[1,128,256]{2,1,0:T(8,128)(2,1)}, u32[]{:S(2)}) copy-start(bf16[1,128,256]{2,1,0:T(8,128)(2,1)} %param.9) | copy-start | bytes 196612
  21.9 1.0 copy-start.3
  22.9 59.6 %copy-start.2 = (bf16[1,256,4096]{2,1,0:T(8,128)(2,1)S(1)}, bf16[1,256,4096]{2,1,0:T(8,128)(2,1)}, u32[]{:S(2)}) copy-start(bf16[1,256,4096]{2,1,0:T(8,128)(2,1)} %param.15) | copy-start | bytes 6291460
  22.9 34.7 %all-to-all-start = ((bf16[8,2,128,256]{3,2,1,0:T(8,128)(2,1)}), bf16[8,2,128,256]{3,2,1,0:T(8,128)(2,1)S(1)}, u32[]{:S(2)}, u32[]{:S(2)}) async-start(bf16[8,2,128,256]{3,2,1,0:T(8,128)(2,1)} %copy-done.3), calls=%async_computation | async-start | bytes 2097152 | tf_op jit(solution)/shard_map/all_to_all | solution.py:160
  28.8 26.1 %collective-permute-start.2 = (bf16[64,4096]{1,0:T(8,128)(2,1)}, bf16[64,4096]{1,0:T(8,128)(2,1)S(1)}, u32[]{:S(2)}, u32[]{:S(2)}) collective-permute-start(bf16[64,4096]{1,0:T(8,128)(2,1)} %bitcast.28), channel_id=1, source_target_pairs={{0,0},{1,1},{2,4},{3,5},{4,8},{5,9},{6,12},{7,13},{8,2},{9,3},{10,... | collective-permute-start | bytes 1572872 | tf_op jit(solution)/shard_map/ppermute | solution.py:189
  55.7 24.7 %collective-permute-start.3 = (bf16[64,4096]{1,0:T(8,128)(2,1)}, bf16[64,4096]{1,0:T(8,128)(2,1)}, u32[]{:S(2)}, u32[]{:S(2)}) collective-permute-start(bf16[64,4096]{1,0:T(8,128)(2,1)} %shard_map.104.refs_0_), channel_id=1, source_target_pairs={{0,2},{2,0},{1,3},{3,1},{4,6},{6,4},{5,7},{7,5},{8,10},{10,8},{9,1... | collective-permute-start | bytes 1572872 | tf_op jit(solution)/shard_map/ppermute | solution.py:156
  57.6 28.8 %collective-permute-start.1 = (bf16[8,2,128,256]{3,2,1,0:T(8,128)(2,1)S(1)}, bf16[8,2,128,256]{3,2,1,0:T(8,128)(2,1)}, u32[]{:S(2)}, u32[]{:S(2)}) collective-permute-start(bf16[8,2,128,256]{3,2,1,0:T(8,128)(2,1)S(1)} %all-to-all-done.refs_0_), channel_id=1, source_target_pairs={{0,1},{1,0},{2,3},{3,2},{4,5},{5,4},{6,7},{7,6},{8,9},{9,8},{10,11... | collective-permute-start | bytes 3145736 | tf_op jit(solution)/shard_map/ppermute | solution.py:156
  76.1 6.4 %collective-permute-start.9 = (bf16[8,1,128,256]{3,2,1,0:T(8,128)(2,1)}, bf16[8,1,128,256]{3,2,1,0:T(8,128)(2,1)}, u32[]{:S(2)}, u32[]{:S(2)}) collective-permute-start(bf16[8,1,128,256]{3,2,1,0:T(8,128)(2,1)} %all_to_all.20.refs_0_), channel_id=1, source_target_pairs={{0,1},{1,0},{2,3},{3,2},{4,5},{5,4},{6,7},{7,6},{8,9},{9,8},{10,11... | collective-permute-start | bytes 1572872 | tf_op jit(solution)/shard_map/ppermute | solution.py:156
  78.0 6.5 %collective-permute-start.4 = (bf16[64,4096]{1,0:T(8,128)(2,1)}, bf16[64,4096]{1,0:T(8,128)(2,1)}, u32[]{:S(2)}, u32[]{:S(2)}) collective-permute-start(bf16[64,4096]{1,0:T(8,128)(2,1)} %shard_map.104.refs_0_), channel_id=1, source_target_pairs={{0,1},{1,0},{2,3},{3,2},{4,5},{5,4},{6,7},{7,6},{8,9},{9,8},{10,11... | collective-permute-start | bytes 1572872 | tf_op jit(solution)/shard_map/ppermute | solution.py:156
  80.5 4.1 %collective-permute-start.5 = (bf16[64,4096]{1,0:T(8,128)(2,1)}, bf16[64,4096]{1,0:T(8,128)(2,1)}, u32[]{:S(2)}, u32[]{:S(2)}) collective-permute-start(bf16[64,4096]{1,0:T(8,128)(2,1)} %collective-permute-done.3.refs_1_), channel_id=1, source_target_pairs={{0,1},{1,0},{2,3},{3,2},{4,5},{5,4},{6,7},{7,6},{8,9},{9,8},{10,11... | collective-permute-start | bytes 1572872 | tf_op jit(solution)/shard_map/ppermute | solution.py:156
  84.5 2.2 %copy-start.1 = (bf16[1,4096,256]{2,1,0:T(8,128)(2,1)S(1)}, bf16[1,4096,256]{2,1,0:T(8,128)(2,1)}, u32[]{:S(2)}) copy-start(bf16[1,4096,256]{2,1,0:T(8,128)(2,1)} %param.13) | copy-start | bytes 6291460
  84.6 2.2 %copy-start.9 = (f32[1,4096]{1,0:T(1,128)S(1)}, f32[1,4096]{1,0:T(1,128)}, u32[]{:S(2)}) copy-start(f32[1,4096]{1,0:T(1,128)} %refs_2_.3) | copy-start | bytes 49156
  91.8 9.9 %collective-permute-start.10 = (bf16[8,1,128,256]{3,2,1,0:T(8,128)(2,1)S(1)}, bf16[8,1,128,256]{3,2,1,0:T(8,128)(2,1)S(1)}, u32[]{:S(2)}, u32[]{:S(2)}) collective-permute-start(bf16[8,1,128,256]{3,2,1,0:T(8,128)(2,1)S(1)} %get-tuple-element.10), channel_id=1, source_target_pairs={{0,1},{1,0},{2,3},{3,2},{4,5},{5,4},{6,7},{7,6},{8,9},{9,8},{10,11... | collective-permute-start | bytes 1572872 | tf_op jit(solution)/shard_map/ppermute | solution.py:156
  98.8 0.8 copy-start.6
  99.6 6.9 %copy-start.5 = (bf16[1,128,256]{2,1,0:T(8,128)(2,1)S(1)}, bf16[1,128,256]{2,1,0:T(8,128)(2,1)}, u32[]{:S(2)}) copy-start(bf16[1,128,256]{2,1,0:T(8,128)(2,1)} %param.8) | copy-start | bytes 196612
  99.6 20.8 %copy-start.7 = (bf16[8,1,128,256]{3,2,1,0:T(8,128)(2,1)S(1)}, bf16[8,1,128,256]{3,2,1,0:T(8,128)(2,1)}, u32[]{:S(2)}) copy-start(bf16[8,1,128,256]{3,2,1,0:T(8,128)(2,1)} %copy-done.6) | copy-start | bytes 1572868
  99.6 20.8 %collective-permute-start.6 = (bf16[8,1,128,256]{3,2,1,0:T(8,128)(2,1)}, bf16[8,1,128,256]{3,2,1,0:T(8,128)(2,1)S(1)}, u32[]{:S(2)}, u32[]{:S(2)}) collective-permute-start(bf16[8,1,128,256]{3,2,1,0:T(8,128)(2,1)} %get-tuple-element.8), channel_id=1, source_target_pairs={{0,1},{1,0},{2,3},{3,2},{4,5},{5,4},{6,7},{7,6},{8,9},{9,8},{10,11... | collective-permute-start | bytes 1572872 | tf_op jit(solution)/shard_map/ppermute | solution.py:156
  102.6 18.8 %all-to-all-start.3 = ((bf16[8,1,128,256]{3,2,1,0:T(8,128)(2,1)}), bf16[8,1,128,256]{3,2,1,0:T(8,128)(2,1)S(1)}, u32[]{:S(2)}, u32[]{:S(2)}) async-start(bf16[8,1,128,256]{3,2,1,0:T(8,128)(2,1)} %shard_map.113), calls=%async_computation.3 | async-start | bytes 1048576 | tf_op jit(solution)/shard_map/all_to_all | solution.py:160
  106.5 13.9 %collective-permute-start.7 = (bf16[128,256]{1,0:T(8,128)(2,1)S(1)}, bf16[128,256]{1,0:T(8,128)(2,1)S(1)}, u32[]{:S(2)}, u32[]{:S(2)}) collective-permute-start(bf16[128,256]{1,0:T(8,128)(2,1)S(1)} %shard_map.107), channel_id=1, source_target_pairs={{0,496},{16,480},{32,464},{48,448},{64,432},{80,416},{96,400},{112... | collective-permute-start | bytes 196616 | tf_op jit(solution)/shard_map/ppermute | solution.py:152
  121.3 13.2 %all-to-all-start.1 = ((bf16[8,1,128,256]{3,2,1,0:T(8,128)(2,1)}), bf16[8,1,128,256]{3,2,1,0:T(8,128)(2,1)S(1)}, u32[]{:S(2)}, u32[]{:S(2)}) async-start(bf16[8,1,128,256]{3,2,1,0:T(8,128)(2,1)} %shard_map.108), calls=%async_computation.1 | async-start | bytes 1048576 | tf_op jit(solution)/shard_map/all_to_all | solution.py:160
  127.1 9.5 %collective-permute-start.11 = (bf16[128,256]{1,0:T(8,128)(2,1)S(1)}, bf16[128,256]{1,0:T(8,128)(2,1)S(1)}, u32[]{:S(2)}, u32[]{:S(2)}) collective-permute-start(bf16[128,256]{1,0:T(8,128)(2,1)S(1)} %shard_map.114), channel_id=1, source_target_pairs={{0,496},{16,0},{32,16},{48,32},{64,48},{80,64},{96,80},{112,96},{1... | collective-permute-start | bytes 196616 | tf_op jit(solution)/shard_map/ppermute | solution.py:148
  134.6 9.8 %collective-permute-start.8 = (bf16[128,256]{1,0:T(8,128)(2,1)S(1)}, bf16[128,256]{1,0:T(8,128)(2,1)S(1)}, u32[]{:S(2)}, u32[]{:S(2)}) collective-permute-start(bf16[128,256]{1,0:T(8,128)(2,1)S(1)} %shard_map.109), channel_id=1, source_target_pairs={{0,16},{16,32},{32,48},{48,64},{64,80},{80,96},{96,112},{112,128},... | collective-permute-start | bytes 196616 | tf_op jit(solution)/shard_map/ppermute | solution.py:148

commit v4 on v3

v4 whole, which is shorter than its diff:
```python
import jax
import jax.numpy as jnp
from jax import lax
from jax.experimental import pallas as pl
from jax.experimental.pallas import tpu as pltpu
from jax.sharding import Mesh, PartitionSpec as P

HEAD_DIM = 128
EPS = 1e-05
SCALE = HEAD_DIM ** (-0.5)
D = 4096
T = 128
W = 256
N = D // W

SEC = ("z", "yh")
TEN = ("x", "yl", "c")
F32 = jnp.float32
BF16 = jnp.bfloat16
NT = (((1,), (1,)), ((), ()))
TN = (((0,), (0,)), ((), ()))


def dot(a, b, dims=(((1,), (0,)), ((), ()))):
    return lax.dot_general(a, b, dims, preferred_element_type=F32)


def call(kernel, outs, core, *args, after=(), scratch=(), flops=0):
    nbytes = sum(a.size * a.dtype.itemsize for a in args)

    def ordered(core_ref, *refs):
        kernel(core_ref, *refs[: len(args)], *refs[len(args) + len(after) :])

    return pl.pallas_call(
        ordered,
        out_shape=tuple(pltpu.VMEM(s, d) for s, d in outs),
        in_specs=[pl.BlockSpec(memory_space=pltpu.SMEM)]
        + [pl.BlockSpec(memory_space=pltpu.VMEM)] * len(args)
        + [pl.BlockSpec(memory_space=pl.ANY)] * len(after),
        out_specs=tuple(pl.BlockSpec(memory_space=pltpu.VMEM) for _ in outs),
        scratch_shapes=list(scratch),
        compiler_params=pltpu.CompilerParams(vmem_limit_bytes=24 * 2**20),
        cost_estimate=pl.CostEstimate(flops=flops, bytes_accessed=nbytes, transcendentals=0),
    )(core, *(pltpu.with_memory_space_constraint(a, pltpu.VMEM) for a in args), *after)


def in_hbm(a):
    return pltpu.with_memory_space_constraint(a, pltpu.HBM)


def blocks(core, own, other, which=0):
    for ref, side in ((own, core), (other, 1 - core)):
        for j in range(8):
            yield ref.at[j, which], pl.multiple_of((2 * j + side) * W, W)


def load_kernel(slot, store, x, g, held_out, x_out, g_out, sems):
    copies = [
        pltpu.make_async_copy(store.at[0, slot[0]], held_out, sems.at[0]),
        pltpu.make_async_copy(x.at[0], x_out, sems.at[1]),
        pltpu.make_async_copy(g.at[0], g_out, sems.at[2]),
    ]
    for copy in copies:
        copy.start()
    for copy in copies:
        copy.wait()


def spread_kernel(_, x, fetched, g, out):
    for j in range(8):
        out[j, 0] = x[...]
        out[j, 1] = fetched[...]
        out[j, 2] = g[...]


def assemble_kernel(core, first, twin, out):
    rows = first.shape[0]
    for ref, side in ((first, core[0]), (twin, 1 - core[0])):
        out[pl.ds(pl.multiple_of(side * rows, rows), rows), :] = ref[...]


def keyval_kernel(core_ref, own, other, gain, wkv, xg, inv_out, kv_out, kvb_out):
    for which in range(2):
        rows = slice(which * T, (which + 1) * T)
        squares = jnp.zeros((T, W), F32)
        for x, at in blocks(core_ref[0], own, other, which):
            wide = x[...].astype(F32)
            squares += wide * wide
            xg[rows, pl.ds(at, W)] = (wide * gain[:, pl.ds(at, W)]).astype(BF16)
        mean = jnp.sum(squares, axis=-1, keepdims=True) * (1.0 / D)
        inv_out[rows, :] = lax.rsqrt(mean + EPS)
    kv = dot(xg[...], wkv[...], NT) * inv_out[...]
    kv_out[...] = kv
    kvb_out[...] = kv.astype(BF16)


def queries_kernel(core_ref, own, other, xg, inv, wq, wo, q_out, dmixed, g):
    q_out[...] = dot(xg[...], wq[...]) * inv[...]
    for block, at in blocks(core_ref[0], own, other, 2):
        g[:, pl.ds(at, W)] = block[...]
    dmixed[...] = dot(g[...], wo[...], NT).astype(BF16)


def attend_kernel(low_ref, kvb, got, q, dmixed, mixed, dq_out, own_out, away_out):
    low = low_ref[0] == 0
    row = lax.broadcasted_iota(jnp.int32, (T, T), 0)
    col = lax.broadcasted_iota(jnp.int32, (T, T), 1)
    dk, dv = 0.0, 0.0
    for which in range(2):
        rows = slice(which * T, (which + 1) * T)
        k = jnp.where(low, kvb[rows, :], got[rows, :])
        v = jnp.where(low, got[rows, :], kvb[rows, :])
        for h in range(2):
            lanes = slice(h * HEAD_DIM, (h + 1) * HEAD_DIM)
            qb = q[rows, lanes].astype(BF16)
            s = dot(qb, k, NT) * SCALE
            s = jnp.where(row >= col, s, F32(-1e30))
            e = jnp.exp(s - jnp.max(s, axis=-1, keepdims=True))
            p = e / jnp.sum(e, axis=-1, keepdims=True)
            pb = p.astype(BF16)
            if which == 0:
                mixed[:, lanes] = dot(pb, v).astype(BF16)
                continue
            dm = dmixed[:, lanes]
            dprob = dot(dm, v, NT)
            dscore = (p * (dprob - jnp.sum(p * dprob, axis=-1, keepdims=True))).astype(BF16)
            dq_out[:, lanes] = dot(dscore, k) * SCALE
            dk += dot(dscore, qb, TN)
            dv += dot(pb, dm, TN)
    dk = dk * SCALE
    own_out[...] = jnp.where(low, dk, dv)
    away_out[...] = jnp.where(low, dv, dk).astype(BF16)


def output_kernel(core_ref, mixed, wo, keep, send):
    for out, at in blocks(core_ref[0], keep, send):
        out[...] = dot(mixed[...], wo[:, pl.ds(at, W)]).astype(BF16)


def input_kernel(core_ref, own, other, gain, wq, wkv, inv, q, kv, dq, mine, got, keep, send):
    core = core_ref[0]
    r = inv[T:, :]
    dkv = mine[...] + got[...].astype(F32)
    share = jnp.sum(dq[...] * q[T:, :], axis=-1, keepdims=True)
    share += jnp.sum(dkv * kv[T:, :], axis=-1, keepdims=True)
    coef = r * r * share * (1.0 / D)
    dqs, dkvs = (dq[...] * r).astype(BF16), (dkv * r).astype(BF16)
    for (out, at), (x, _) in zip(blocks(core, keep, send), blocks(core, own, other, 1)):
        term = dot(dqs, wq[pl.ds(at, W), :], NT) + dot(dkvs, wkv[:, pl.ds(at, W)])
        term = term * gain[:, pl.ds(at, W)] - coef * x[...].astype(F32)
        out[...] = term.astype(BF16)


def pair_kernel(_, keep_y, got_y, keep_dx, got_dx, x, out, x_out):
    for j in range(8):
        out[j, 0] = (keep_y[j, 0].astype(F32) + got_y[j, 0].astype(F32)).astype(BF16)
        out[j, 1] = (keep_dx[j, 0].astype(F32) + got_dx[j, 0].astype(F32)).astype(BF16)
    x_out[...] = x[...]


def finish_kernel(_, x, g, got, y_out, dx_out):
    for which, base, out in ((0, x, y_out), (1, g, dx_out)):
        total = base[...].astype(F32)
        for j in range(8):
            total += got[j, which].astype(F32)
        out[...] = total.astype(BF16)


def shift(block, distance):
    return lax.ppermute(block, SEC, [(i, (i + distance) % 32) for i in range(32)])


def mirror(block):
    return lax.ppermute(block, SEC, [(i, 31 - i) for i in range(32)])


def swap(block, axis):
    return lax.ppermute(block, axis, [(0, 1), (1, 0)])


def exchange(parts):
    return lax.all_to_all(parts, ("x", "yl"), 0, 0, tiled=True)


def body(section_input, section_grad, mirror_store, fetch_slot, norm_gain, w_query, w_keyval, w_output):
    gain, wq, wo, keyval_w = norm_gain, w_query[0], w_output[0], w_keyval[0]
    core = lax.axis_index("c").astype(jnp.int32).reshape(1)
    low = lax.axis_index("yl").astype(jnp.int32).reshape(1)
    tile = ((T, W), BF16)
    half = ((8, 1, T, W), BF16)

    held, x, g = pl.pallas_call(
        load_kernel,
        out_shape=tuple(pltpu.VMEM((T, W), BF16) for _ in range(3)),
        in_specs=[pl.BlockSpec(memory_space=pltpu.SMEM)]
        + [pl.BlockSpec(memory_space=pl.ANY)] * 3,
        out_specs=tuple(pl.BlockSpec(memory_space=pltpu.VMEM) for _ in range(3)),
        scratch_shapes=[pltpu.SemaphoreType.DMA((3,))],
    )(fetch_slot, *(in_hbm(a) for a in (mirror_store, section_input, section_grad)))
    fetched = mirror(held)

    route = []
    for r in range(16):
        part, group = divmod(r // 2, 4)
        route.append((r, 4 * group + 2 * part + r % 2))
    first = lax.ppermute(keyval_w, TEN, route)
    (wkv,) = call(assemble_kernel, [((HEAD_DIM, D), BF16)], core, first, swap(first, "c"))

    (spread,) = call(spread_kernel, [((8, 3, T, W), BF16)], core, x, fetched, g, after=(first,))
    own = exchange(spread)
    other = swap(own, "c")

    xg, inv, kv, kvb = call(
        keyval_kernel,
        [((2 * T, D), BF16), ((2 * T, 1), F32), ((2 * T, HEAD_DIM), F32), ((2 * T, HEAD_DIM), BF16)],
        core,
        own,
        other,
        gain,
        wkv,
    )
    q, dmixed = call(
        queries_kernel,
        [((2 * T, W), F32), tile],
        core,
        own,
        other,
        xg,
        inv,
        wq,
        wo,
        scratch=[pltpu.VMEM((T, D), BF16)],
        flops=10**9,
    )
    mixed, dq, mine, away = call(
        attend_kernel,
        [tile, ((T, W), F32), ((T, HEAD_DIM), F32), ((T, HEAD_DIM), BF16)],
        low,
        kvb,
        swap(kvb, "yl"),
        q,
        dmixed,
    )
    keep_y, send_y = call(output_kernel, [half, half], core, mixed, wo, flops=10**9)
    keep_dx, send_dx = call(
        input_kernel,
        [half, half],
        core,
        own,
        other,
        gain,
        wq,
        wkv,
        inv,
        q,
        kv,
        dq,
        mine,
        swap(away, "yl"),
    )
    pair, x_late = call(
        pair_kernel,
        [((8, 2, T, W), BF16), tile],
        core,
        keep_y,
        swap(send_y, "c"),
        keep_dx,
        swap(send_dx, "c"),
        x,
    )
    y, dx = call(finish_kernel, [tile, tile], core, x, g, exchange(pair))
    forward_next, grad_prev = shift(y, 1), shift(dx, -1)
    evicted = mirror(x_late)
    return forward_next[None], grad_prev[None], evicted[None]


def solution(mesh):
    fine = Mesh(mesh.devices.reshape(16, 2, 4, 2, 2), SEC + TEN)
    cols = P(SEC, None, TEN)
    return jax.shard_map(
        body,
        mesh=fine,
        in_specs=(
            cols,
            cols,
            P(SEC, None, None, TEN),
            P(SEC),
            P(SEC, None),
            cols,
            P(SEC, TEN, None),
            P(SEC, TEN, None),
        ),
        out_specs=(cols, cols, cols),
        check_vma=False,
    )
```

time: 147 us -> 117 us (0.80)
  the two profiles are of different devices: /device:TPU:8 before, /device:TPU:1 now
where the time goes in v4:
time: 117 us; the launch traced here: 116 us
  starting transfers between devices  55.1 us (47%)
  waiting for transfers between devices  24.2 us (21%)
  blocking collectives  23.2 us (20%)
  Pallas kernels  9.58 us (8%)
  local copies, waits for them, and re-layouts  1.91 us (2%)
  between operations  1.52 us (1%)
    all_to_all x1, blocking collectives, exchange(): return lax.all_to_all(parts, ('x', 'yl'), 0, 0, tiled=True)  23.2 us
    ppermute x2, starting transfers between devices, mirror(): return lax.ppermute(block, SEC, [(i, 31 - i) for i in range(32)])  19.6 us
    ppermute x6, starting transfers between devices, swap(): return lax.ppermute(block, axis, [(0, 1), (1, 0)])  17.7 us
    all_to_all x1, waiting for transfers between devices, exchange(): return lax.all_to_all(parts, ('x', 'yl'), 0, 0, tiled=True)  11.5 us
    ppermute x2, starting transfers between devices, shift(): lax.ppermute(block, SEC, [(i, (i + distance) % 32) for i in range(32)])  8.9 us
    pallas_call x9, Pallas kernels, call(): pl.pallas_call(ordered, out_shape=tuple((pltpu.VMEM(s, d) for s, d in out...  8.65 us
    ppermute x2, waiting for transfers between devices, mirror(): return lax.ppermute(block, SEC, [(i, 31 - i) for i in range(32)])  6.33 us
    ppermute x1, starting transfers between devices, body(): first = lax.ppermute(keyval_w, TEN, route)  5.36 us
  transfers between devices with their start and end apart: 12, of which 6 were waited for; matrix products, arithmetic and copies ran while one was open for 0% of the time, Pallas kernels for 5%

profile of v4, /device:TPU:1, one launch (start us, length us, event | category | flops | bytes accessed | tf_op | source)
XLA Modules:
  0.0 115.6 jit_solution(10586558627588897519)
XLA Ops:
  0.6 5.4 %collective-permute-start.1 = (bf16[64,4096]{1,0:T(8,128)(2,1)}, bf16[64,4096]{1,0:T(8,128)(2,1)}, u32[]{:S(2)}, u32[]{:S(2)}) collective-permute-start(bf16[64,4096]{1,0:T(8,128)(2,1)} %bitcast.15), channel_id=1, source_target_pairs={{0,0},{1,1},{2,4},{3,5},{4,8},{5,9},{6,12},{7,13},{8,2},{9,3},{10,... | collective-permute-start | bytes 1572872 | tf_op jit(solution)/shard_map/ppermute | solution.py:206
  6.6 0.9 shard_map.103
  7.6 14.6 %collective-permute-start = (bf16[128,256]{1,0:T(8,128)(2,1)S(1)}, bf16[128,256]{1,0:T(8,128)(2,1)S(1)}, u32[]{:S(2)}, u32[]{:S(2)}) collective-permute-start(bf16[128,256]{1,0:T(8,128)(2,1)S(1)} %get-tuple-element.26), channel_id=1, source_target_pairs={{0,496},{16,480},{32,464},{48,448},{64,432},{80,416},{96,400},{112... | collective-permute-start | bytes 196616 | tf_op jit(solution)/shard_map/ppermute | solution.py:174
  22.2 6.3 %collective-permute-done.refs_1_ = bf16[128,256]{1,0:T(8,128)(2,1)S(1)} collective-permute-done((bf16[128,256]{1,0:T(8,128)(2,1)S(1)}, bf16[128,256]{1,0:T(8,128)(2,1)S(1)}, u32[]{:S(2)}, u32[]{:S(2)}) %collective-permute-start) | collective-permute-done | bytes 65568 | tf_op jit(solution)/shard_map/ppermute | solution.py:174
  28.5 0.1 shard_map.104
  28.6 23.2 %all_to_all.10.refs_0_ = bf16[8,3,128,256]{3,2,1,0:T(8,128)(2,1)S(1)} all-to-all(bf16[8,3,128,256]{3,2,1,0:T(8,128)(2,1)S(1)} %shard_map.104), channel_id=1, replica_groups=mesh['z'=16,'yh'=2,'x'=4,'yl'=2,'c'=2] {'x','yl'}, dimensions={0} | all-to-all | bytes 3145728 | tf_op jit(solution)/shard_map/all_to_all | solution.py:182
  51.8 4.3 %collective-permute-start.2 = (bf16[8,3,128,256]{3,2,1,0:T(8,128)(2,1)S(1)}, bf16[8,3,128,256]{3,2,1,0:T(8,128)(2,1)S(1)}, u32[]{:S(2)}, u32[]{:S(2)}) collective-permute-start(bf16[8,3,128,256]{3,2,1,0:T(8,128)(2,1)S(1)} %all_to_all.10.refs_0_), channel_id=1, source_target_pairs={{0,1},{1,0},{2,3},{3,2},{4,5},{5,4},{6,7},{7,6},{8,9},{9,8},{10,11... | collective-permute-start | bytes 4718600 | tf_op jit(solution)/shard_map/ppermute | solution.py:178
  56.1 1.9 %collective-permute-start.3 = (bf16[64,4096]{1,0:T(8,128)(2,1)}, bf16[64,4096]{1,0:T(8,128)(2,1)}, u32[]{:S(2)}, u32[]{:S(2)}) collective-permute-start(bf16[64,4096]{1,0:T(8,128)(2,1)} %collective-permute-done.1.refs_3_.refs_0_), channel_id=1, source_target_pairs={{0,1},{1,0},{2,3},{3,2},{4,5},{5,4},{6,7},{7,6},{8,9},{9,8},{10,11... | collective-permute-start | bytes 1572872 | tf_op jit(solution)/shard_map/ppermute | solution.py:178
  58.0 2.2 %collective-permute-done.3.refs_1_ = bf16[64,4096]{1,0:T(8,128)(2,1)} collective-permute-done((bf16[64,4096]{1,0:T(8,128)(2,1)}, bf16[64,4096]{1,0:T(8,128)(2,1)}, u32[]{:S(2)}, u32[]{:S(2)}) %collective-permute-start.3) | collective-permute-done | bytes 524320 | tf_op jit(solution)/shard_map/ppermute | solution.py:178
  60.3 1.3 %shard_map.105.refs_3_.refs_4_ = bf16[128,4096]{1,0:T(8,128)(2,1)S(1)} custom-call(s32[1]{0:T(128)} %bitcast.core_ref, bf16[64,4096]{1,0:T(8,128)(2,1)} %collective-permute-done.1.refs_3_.refs_0_, bf16[64,4096]{1,0:T(8,128)(2,1)} %collective-permute-done.3.refs_1_), custom_call_target="tpu_custom_call" | custom-call | bytes 1048576 | tf_op jit(solution)/shard_map/pallas_call | solution.py:34
  61.6 1.4 %shard_map.106 = (bf16[256,4096]{1,0:T(8,128)(2,1)S(1)}, f32[256,1]{1,0:T(8,128)S(1)}, f32[256,128]{1,0:T(8,128)S(1)}, bf16[256,128]{1,0:T(8,128)(2,1)S(1)}) custom-call(s32[1]{0:T(128)} %bitcast.core_ref, bf16[8,3,128,256]{3,2,1,0:T(8,128)(2,1)S(1)} %all_to_all.10.refs_0_, bf16[8,3,128,256]{3,2,1,0:T(8,128)(2,1)S(1)} %collective-permute-done.2.refs_1_, ...), custom_call_target="tpu_custom_call" | custom-call | bytes 4210688 | tf_op jit(solution)/shard_map/pallas_call | solution.py:34
  62.9 2.8 %collective-permute-start.4 = (bf16[256,128]{1,0:T(8,128)(2,1)S(1)}, bf16[256,128]{1,0:T(8,128)(2,1)S(1)}, u32[]{:S(2)}, u32[]{:S(2)}) collective-permute-start(bf16[256,128]{1,0:T(8,128)(2,1)S(1)} %get-tuple-element.27.refs_0_), channel_id=1, source_target_pairs={{0,2},{2,0},{1,3},{3,1},{4,6},{6,4},{5,7},{7,5},{8,10},{10,8},{9,1... | collective-permute-start | bytes 196616 | tf_op jit(solution)/shard_map/ppermute | solution.py:178
  65.8 1.4 %shard_map.107 = (f32[256,256]{1,0:T(8,128)S(1)}, bf16[128,256]{1,0:T(8,128)(2,1)S(1)}) custom-call(s32[1]{0:T(128)} %bitcast.core_ref, bf16[8,3,128,256]{3,2,1,0:T(8,128)(2,1)S(1)} %all_to_all.10.refs_0_, bf16[8,3,128,256]{3,2,1,0:T(8,128)(2,1)S(1)} %collective-permute-done.2.refs_1_, bf16[256,4096]{1,0:T(8,128)(2,1)S(1)} %get-tuple-element.28.refs_2_, ...), custom_call_target="tpu_custom_call" | custom-call | flops 1000000000 | bytes 9438208 | tf_op jit(solution)/shard_map/pallas_call | solution.py:34
  67.2 0.8 collective-permute-done.4.refs_1_
  68.0 1.5 %shard_map.108 = (bf16[128,256]{1,0:T(8,128)(2,1)S(1)}, f32[128,256]{1,0:T(8,128)S(1)}, f32[128,128]{1,0:T(8,128)S(1)}, bf16[128,128]{1,0:T(8,128)(2,1)S(1)}) custom-call(s32[1]{0:T(128)} %bitcast.1.core_ref, bf16[256,128]{1,0:T(8,128)(2,1)S(1)} %get-tuple-element.27.refs_0_, bf16[256,128]{1,0:T(8,128)(2,1)S(1)} %collective-permute-done.4.refs_1_, ...), custom_call_target="tpu_custom_call" | custom-call | bytes 458752 | tf_op jit(solution)/shard_map/pallas_call | solution.py:34
  69.4 2.8 %collective-permute-start.6 = (bf16[128,128]{1,0:T(8,128)(2,1)S(1)}, bf16[128,128]{1,0:T(8,128)(2,1)S(1)}, u32[]{:S(2)}, u32[]{:S(2)}) collective-permute-start(bf16[128,128]{1,0:T(8,128)(2,1)S(1)} %get-tuple-element.38), channel_id=1, source_target_pairs={{0,2},{2,0},{1,3},{3,1},{4,6},{6,4},{5,7},{7,5},{8,10},{10,8},{9,1... | collective-permute-start | bytes 98312 | tf_op jit(solution)/shard_map/ppermute | solution.py:178
  72.3 0.5 shard_map.109
  72.8 3.7 %collective-permute-start.5 = (bf16[8,1,128,256]{3,2,1,0:T(8,128)(2,1)S(1)}, bf16[8,1,128,256]{3,2,1,0:T(8,128)(2,1)S(1)}, u32[]{:S(2)}, u32[]{:S(2)}) collective-permute-start(bf16[8,1,128,256]{3,2,1,0:T(8,128)(2,1)S(1)} %get-tuple-element.34), channel_id=1, source_target_pairs={{0,1},{1,0},{2,3},{3,2},{4,5},{5,4},{6,7},{7,6},{8,9},{9,8},{10,11... | collective-permute-start | bytes 1572872 | tf_op jit(solution)/shard_map/ppermute | solution.py:178
  76.4 1.2 %shard_map.110 = (bf16[8,1,128,256]{3,2,1,0:T(8,128)(2,1)S(1)}, bf16[8,1,128,256]{3,2,1,0:T(8,128)(2,1)S(1)}) custom-call(s32[1]{0:T(128)} %bitcast.core_ref, bf16[8,3,128,256]{3,2,1,0:T(8,128)(2,1)S(1)} %all_to_all.10.refs_0_, bf16[8,3,128,256]{3,2,1,0:T(8,128)(2,1)S(1)} %collective-permute-done.2.refs_1_, f32[1,4096]{1,0:T(1,128)S(1)} %copy-done.2, ...), custom_call_target="tpu_custom_call" | custom-call | bytes 6931456 | tf_op jit(solution)/shard_map/pallas_call | solution.py:34
  77.7 2.2 %collective-permute-start.7 = (bf16[8,1,128,256]{3,2,1,0:T(8,128)(2,1)S(1)}, bf16[8,1,128,256]{3,2,1,0:T(8,128)(2,1)S(1)}, u32[]{:S(2)}, u32[]{:S(2)}) collective-permute-start(bf16[8,1,128,256]{3,2,1,0:T(8,128)(2,1)S(1)} %get-tuple-element.40), channel_id=1, source_target_pairs={{0,1},{1,0},{2,3},{3,2},{4,5},{5,4},{6,7},{7,6},{8,9},{9,8},{10,11... | collective-permute-start | bytes 1572872 | tf_op jit(solution)/shard_map/ppermute | solution.py:178
  79.9 1.6 %collective-permute-done.7.refs_3_ = bf16[8,1,128,256]{3,2,1,0:T(8,128)(2,1)S(1)} collective-permute-done((bf16[8,1,128,256]{3,2,1,0:T(8,128)(2,1)S(1)}, bf16[8,1,128,256]{3,2,1,0:T(8,128)(2,1)S(1)}, u32[]{:S(2)}, u32[]{:S(2)}) %collective-permute-start.7) | collective-permute-done | bytes 524320 | tf_op jit(solution)/shard_map/ppermute | solution.py:178
  81.5 1.2 %shard_map.111 = (bf16[8,2,128,256]{3,2,1,0:T(8,128)(2,1)}, bf16[128,256]{1,0:T(8,128)(2,1)S(1)}) custom-call(s32[1]{0:T(128)} %bitcast.core_ref, bf16[8,1,128,256]{3,2,1,0:T(8,128)(2,1)S(1)} %get-tuple-element.33.refs_0_, bf16[8,1,128,256]{3,2,1,0:T(8,128)(2,1)S(1)} %collective-permute-done.5.refs_1_, ...), custom_call_target="tpu_custom_call" | custom-call | bytes 2162688 | tf_op jit(solution)/shard_map/pallas_call | solution.py:34
  82.7 3.6 %all-to-all-start.1 = ((bf16[8,2,128,256]{3,2,1,0:T(8,128)(2,1)}), bf16[8,2,128,256]{3,2,1,0:T(8,128)(2,1)S(1)}, u32[]{:S(2)}, u32[]{:S(2)}) async-start(bf16[8,2,128,256]{3,2,1,0:T(8,128)(2,1)} %get-tuple-element.41), calls=%async_computation.1 | async-start | bytes 2097152 | tf_op jit(solution)/shard_map/all_to_all | solution.py:182
  86.3 5.0 %collective-permute-start.10 = (bf16[128,256]{1,0:T(8,128)(2,1)S(1)}, bf16[128,256]{1,0:T(8,128)(2,1)S(1)}, u32[]{:S(2)}, u32[]{:S(2)}) collective-permute-start(bf16[128,256]{1,0:T(8,128)(2,1)S(1)} %get-tuple-element.44), channel_id=1, source_target_pairs={{0,496},{16,480},{32,464},{48,448},{64,432},{80,416},{96,400},{112... | collective-permute-start | bytes 196616 | tf_op jit(solution)/shard_map/ppermute | solution.py:174
  91.3 11.5 %all-to-all-done.1.refs_2_ = bf16[8,2,128,256]{3,2,1,0:T(8,128)(2,1)S(1)} async-done(((bf16[8,2,128,256]{3,2,1,0:T(8,128)(2,1)}), bf16[8,2,128,256]{3,2,1,0:T(8,128)(2,1)S(1)}, u32[]{:S(2)}, u32[]{:S(2)}) %all-to-all-start.1) | async-done | bytes 1048608 | tf_op jit(solution)/shard_map/all_to_all | solution.py:182
  102.8 0.2 shard_map.112
  103.0 3.5 %collective-permute-start.8 = (bf16[128,256]{1,0:T(8,128)(2,1)S(1)}, bf16[128,256]{1,0:T(8,128)(2,1)S(1)}, u32[]{:S(2)}, u32[]{:S(2)}) collective-permute-start(bf16[128,256]{1,0:T(8,128)(2,1)S(1)} %get-tuple-element.42), channel_id=1, source_target_pairs={{0,16},{16,32},{32,48},{48,64},{64,80},{80,96},{96,112},{112,128},... | collective-permute-start | bytes 196616 | tf_op jit(solution)/shard_map/ppermute | solution.py:170
  106.5 5.4 %collective-permute-start.9 = (bf16[128,256]{1,0:T(8,128)(2,1)S(1)}, bf16[128,256]{1,0:T(8,128)(2,1)S(1)}, u32[]{:S(2)}, u32[]{:S(2)}) collective-permute-start(bf16[128,256]{1,0:T(8,128)(2,1)S(1)} %get-tuple-element.43), channel_id=1, source_target_pairs={{0,496},{16,0},{32,16},{48,32},{64,48},{80,64},{96,80},{112,96},{1... | collective-permute-start | bytes 196616 | tf_op jit(solution)/shard_map/ppermute | solution.py:170
  111.9 1.8 %collective-permute-done.9 = bf16[128,256]{1,0:T(8,128)(2,1)S(1)} collective-permute-done((bf16[128,256]{1,0:T(8,128)(2,1)S(1)}, bf16[128,256]{1,0:T(8,128)(2,1)S(1)}, u32[]{:S(2)}, u32[]{:S(2)}) %collective-permute-start.9) | collective-permute-done | bytes 65568 | tf_op jit(solution)/shard_map/ppermute | solution.py:170
  113.7 0.6 copy.15
  114.3 0.6 copy.16
  115.0 0.6 copy.17
  (12 shorter events, 0.0 us)
Async XLA Ops:
  0.6 27.9 %collective-permute-start.1 = (bf16[64,4096]{1,0:T(8,128)(2,1)}, bf16[64,4096]{1,0:T(8,128)(2,1)}, u32[]{:S(2)}, u32[]{:S(2)}) collective-permute-start(bf16[64,4096]{1,0:T(8,128)(2,1)} %bitcast.15), channel_id=1, source_target_pairs={{0,0},{1,1},{2,4},{3,5},{4,8},{5,9},{6,12},{7,13},{8,2},{9,3},{10,... | collective-permute-start | bytes 1572872 | tf_op jit(solution)/shard_map/ppermute | solution.py:206
  7.6 20.9 %collective-permute-start = (bf16[128,256]{1,0:T(8,128)(2,1)S(1)}, bf16[128,256]{1,0:T(8,128)(2,1)S(1)}, u32[]{:S(2)}, u32[]{:S(2)}) collective-permute-start(bf16[128,256]{1,0:T(8,128)(2,1)S(1)} %get-tuple-element.26), channel_id=1, source_target_pairs={{0,496},{16,480},{32,464},{48,448},{64,432},{80,416},{96,400},{112... | collective-permute-start | bytes 196616 | tf_op jit(solution)/shard_map/ppermute | solution.py:174
  28.6 33.0 %copy-start.2 = (f32[1,4096]{1,0:T(1,128)S(1)}, f32[1,4096]{1,0:T(1,128)}, u32[]{:S(2)}) copy-start(f32[1,4096]{1,0:T(1,128)} %refs_2_.3) | copy-start | bytes 49156
  51.8 9.7 %collective-permute-start.2 = (bf16[8,3,128,256]{3,2,1,0:T(8,128)(2,1)S(1)}, bf16[8,3,128,256]{3,2,1,0:T(8,128)(2,1)S(1)}, u32[]{:S(2)}, u32[]{:S(2)}) collective-permute-start(bf16[8,3,128,256]{3,2,1,0:T(8,128)(2,1)S(1)} %all_to_all.10.refs_0_), channel_id=1, source_target_pairs={{0,1},{1,0},{2,3},{3,2},{4,5},{5,4},{6,7},{7,6},{8,9},{9,8},{10,11... | collective-permute-start | bytes 4718600 | tf_op jit(solution)/shard_map/ppermute | solution.py:178
  56.1 4.1 %collective-permute-start.3 = (bf16[64,4096]{1,0:T(8,128)(2,1)}, bf16[64,4096]{1,0:T(8,128)(2,1)}, u32[]{:S(2)}, u32[]{:S(2)}) collective-permute-start(bf16[64,4096]{1,0:T(8,128)(2,1)} %collective-permute-done.1.refs_3_.refs_0_), channel_id=1, source_target_pairs={{0,1},{1,0},{2,3},{3,2},{4,5},{5,4},{6,7},{7,6},{8,9},{9,8},{10,11... | collective-permute-start | bytes 1572872 | tf_op jit(solution)/shard_map/ppermute | solution.py:178
  61.5 4.2 %copy-start = (bf16[1,4096,256]{2,1,0:T(8,128)(2,1)S(1)}, bf16[1,4096,256]{2,1,0:T(8,128)(2,1)}, u32[]{:S(2)}) copy-start(bf16[1,4096,256]{2,1,0:T(8,128)(2,1)} %param.13) | copy-start | bytes 6291460
  61.5 4.2 %copy-start.1 = (bf16[1,256,4096]{2,1,0:T(8,128)(2,1)S(1)}, bf16[1,256,4096]{2,1,0:T(8,128)(2,1)}, u32[]{:S(2)}) copy-start(bf16[1,256,4096]{2,1,0:T(8,128)(2,1)} %param.15) | copy-start | bytes 6291460
  62.9 5.0 %collective-permute-start.4 = (bf16[256,128]{1,0:T(8,128)(2,1)S(1)}, bf16[256,128]{1,0:T(8,128)(2,1)S(1)}, u32[]{:S(2)}, u32[]{:S(2)}) collective-permute-start(bf16[256,128]{1,0:T(8,128)(2,1)S(1)} %get-tuple-element.27.refs_0_), channel_id=1, source_target_pairs={{0,2},{2,0},{1,3},{3,1},{4,6},{6,4},{5,7},{7,5},{8,10},{10,8},{9,1... | collective-permute-start | bytes 196616 | tf_op jit(solution)/shard_map/ppermute | solution.py:178
  69.4 7.0 %collective-permute-start.6 = (bf16[128,128]{1,0:T(8,128)(2,1)S(1)}, bf16[128,128]{1,0:T(8,128)(2,1)S(1)}, u32[]{:S(2)}, u32[]{:S(2)}) collective-permute-start(bf16[128,128]{1,0:T(8,128)(2,1)S(1)} %get-tuple-element.38), channel_id=1, source_target_pairs={{0,2},{2,0},{1,3},{3,1},{4,6},{6,4},{5,7},{7,5},{8,10},{10,8},{9,1... | collective-permute-start | bytes 98312 | tf_op jit(solution)/shard_map/ppermute | solution.py:178
  72.8 7.1 %collective-permute-start.5 = (bf16[8,1,128,256]{3,2,1,0:T(8,128)(2,1)S(1)}, bf16[8,1,128,256]{3,2,1,0:T(8,128)(2,1)S(1)}, u32[]{:S(2)}, u32[]{:S(2)}) collective-permute-start(bf16[8,1,128,256]{3,2,1,0:T(8,128)(2,1)S(1)} %get-tuple-element.34), channel_id=1, source_target_pairs={{0,1},{1,0},{2,3},{3,2},{4,5},{5,4},{6,7},{7,6},{8,9},{9,8},{10,11... | collective-permute-start | bytes 1572872 | tf_op jit(solution)/shard_map/ppermute | solution.py:178
  77.7 3.8 %collective-permute-start.7 = (bf16[8,1,128,256]{3,2,1,0:T(8,128)(2,1)S(1)}, bf16[8,1,128,256]{3,2,1,0:T(8,128)(2,1)S(1)}, u32[]{:S(2)}, u32[]{:S(2)}) collective-permute-start(bf16[8,1,128,256]{3,2,1,0:T(8,128)(2,1)S(1)} %get-tuple-element.40), channel_id=1, source_target_pairs={{0,1},{1,0},{2,3},{3,2},{4,5},{5,4},{6,7},{7,6},{8,9},{9,8},{10,11... | collective-permute-start | bytes 1572872 | tf_op jit(solution)/shard_map/ppermute | solution.py:178
  82.7 20.1 %all-to-all-start.1 = ((bf16[8,2,128,256]{3,2,1,0:T(8,128)(2,1)}), bf16[8,2,128,256]{3,2,1,0:T(8,128)(2,1)S(1)}, u32[]{:S(2)}, u32[]{:S(2)}) async-start(bf16[8,2,128,256]{3,2,1,0:T(8,128)(2,1)} %get-tuple-element.41), calls=%async_computation.1 | async-start | bytes 2097152 | tf_op jit(solution)/shard_map/all_to_all | solution.py:182
  86.3 25.6 %collective-permute-start.10 = (bf16[128,256]{1,0:T(8,128)(2,1)S(1)}, bf16[128,256]{1,0:T(8,128)(2,1)S(1)}, u32[]{:S(2)}, u32[]{:S(2)}) collective-permute-start(bf16[128,256]{1,0:T(8,128)(2,1)S(1)} %get-tuple-element.44), channel_id=1, source_target_pairs={{0,496},{16,480},{32,464},{48,448},{64,432},{80,416},{96,400},{112... | collective-permute-start | bytes 196616 | tf_op jit(solution)/shard_map/ppermute | solution.py:174
  103.0 8.9 %collective-permute-start.8 = (bf16[128,256]{1,0:T(8,128)(2,1)S(1)}, bf16[128,256]{1,0:T(8,128)(2,1)S(1)}, u32[]{:S(2)}, u32[]{:S(2)}) collective-permute-start(bf16[128,256]{1,0:T(8,128)(2,1)S(1)} %get-tuple-element.42), channel_id=1, source_target_pairs={{0,16},{16,32},{32,48},{48,64},{64,80},{80,96},{96,112},{112,128},... | collective-permute-start | bytes 196616 | tf_op jit(solution)/shard_map/ppermute | solution.py:170
  106.5 7.2 %collective-permute-start.9 = (bf16[128,256]{1,0:T(8,128)(2,1)S(1)}, bf16[128,256]{1,0:T(8,128)(2,1)S(1)}, u32[]{:S(2)}, u32[]{:S(2)}) collective-permute-start(bf16[128,256]{1,0:T(8,128)(2,1)S(1)} %get-tuple-element.43), channel_id=1, source_target_pairs={{0,496},{16,0},{32,16},{48,32},{64,48},{80,64},{96,80},{112,96},{1... | collective-permute-start | bytes 196616 | tf_op jit(solution)/shard_map/ppermute | solution.py:170

commit v5 on v4

v5 whole, which is shorter than its diff:
```python
import jax
import jax.numpy as jnp
from jax import lax
from jax.experimental import pallas as pl
from jax.experimental.pallas import tpu as pltpu
from jax.sharding import Mesh, PartitionSpec as P

HEAD_DIM = 128
EPS = 1e-05
SCALE = HEAD_DIM ** (-0.5)
D = 4096
T = 128
W = 256
N = D // W
PAD = 16

SEC = ("z", "yh")
TEN = ("x", "yl", "c")
F32 = jnp.float32
BF16 = jnp.bfloat16
NT = (((1,), (1,)), ((), ()))
TN = (((0,), (0,)), ((), ()))


def dot(a, b, dims=(((1,), (0,)), ((), ()))):
    return lax.dot_general(a, b, dims, preferred_element_type=F32)


def call(kernel, outs, place, *args, after=(), anywhere=(), scratch=(), flops=0):
    nbytes = sum(a.size * a.dtype.itemsize for a in args)
    n = len(args) + len(anywhere)

    def ordered(core, low, *refs):
        kernel(core, low, *refs[:n], *refs[n + len(after) :])

    return pl.pallas_call(
        ordered,
        out_shape=tuple(pltpu.VMEM(s, d) for s, d in outs),
        in_specs=[pl.BlockSpec(memory_space=pltpu.SMEM)] * 2
        + [pl.BlockSpec(memory_space=pltpu.VMEM)] * len(args)
        + [pl.BlockSpec(memory_space=pl.ANY)] * (len(anywhere) + len(after)),
        out_specs=tuple(pl.BlockSpec(memory_space=pltpu.VMEM) for _ in outs),
        scratch_shapes=list(scratch),
        compiler_params=pltpu.CompilerParams(vmem_limit_bytes=16 * 2**20),
        cost_estimate=pl.CostEstimate(flops=flops, bytes_accessed=nbytes, transcendentals=0),
    )(*place, *(pltpu.with_memory_space_constraint(a, pltpu.VMEM) for a in args), *anywhere, *after)


def in_hbm(a):
    return pltpu.with_memory_space_constraint(a, pltpu.HBM)


def at(index, size=W):
    return pl.ds(pl.multiple_of(index * size, size), size)


def load_kernel(slot, store, x, g, held, x_out, g_out, sems):
    copies = [
        pltpu.make_async_copy(store.at[0, slot[0]], held.at[:T, :], sems.at[0]),
        pltpu.make_async_copy(x.at[0], x_out, sems.at[1]),
        pltpu.make_async_copy(g.at[0], g_out, sems.at[2]),
    ]
    for copy in copies:
        copy.start()
    held[T:, :] = jnp.zeros((PAD, W), BF16)
    for copy in copies:
        copy.wait()


def trade_kernel(core, low, x, g, base, away):
    @pl.when(core[0] == 0)
    def _():
        base[...] = x[...]
        away[...] = g[...]

    @pl.when(core[0] == 1)
    def _():
        base[...] = g[...]
        away[...] = x[...]


def spread_kernel(core, low, base, twin, fetched, out):
    for j in range(8):
        out[j, core[0]] = base[...]
        out[j, 1 - core[0]] = twin[...]
        out[j, 2] = fetched[:T, :]


def pick_kernel(core, low, own, out):
    out[...] = own[:, 2]


def keyval_kernel(
    core, low, own, even, gain, first, twin, xg, inv_out, kv_out, kvb_out, wkv, squares, sems
):
    half = first.shape[0]
    copies = []
    for i, (ref, side) in enumerate(((first, core[0]), (twin, 1 - core[0]))):
        copies.append(pltpu.make_async_copy(ref, wkv.at[at(side, half), :], sems.at[i]))
        copies[i].start()

    def scaled(left, right):
        total = jnp.zeros((T, W), F32)
        for j in range(8):
            for side, block in enumerate((left(j), right(j))):
                here = slice((2 * j + side) * W, (2 * j + side + 1) * W)
                wide = block.astype(F32)
                total += wide * wide
                xg[:, here] = (wide * gain[:, here]).astype(BF16)
        squares[...] = total

    @pl.when(core[0] == 0)
    def _():
        scaled(lambda j: own[j, 0], lambda j: own[j, 1])

    @pl.when(core[0] == 1)
    def _():
        scaled(lambda j: even[j], lambda j: own[j, 2])

    inv = lax.rsqrt(jnp.sum(squares[...], axis=-1, keepdims=True) * (1.0 / D) + EPS)
    inv_out[...] = inv
    for copy in copies:
        copy.wait()
    kv = dot(xg[...], wkv[...], NT) * inv
    kv_out[...] = kv
    kvb_out[...] = kv.astype(BF16)


def loads(weights, refs, sems):
    copies = [pltpu.make_async_copy(w, refs.at[i], sems.at[i]) for i, w in enumerate(weights)]
    for copy in copies:
        copy.start()
    return copies


def queries_kernel(core, low, xg, inv, wq, wq2, q_out, rows, sems):
    for i, load in enumerate(loads((wq, wq2), rows, sems)):
        load.wait()
        q_out[:, i * W : (i + 1) * W] = dot(xg[...], rows[i]) * inv[...]


def dmixed_kernel(core, low, own, wo, wo2, dmixed, cols, g, sems):
    copies = loads((wo, wo2), cols, sems)

    @pl.when(core[0] == 1)
    def _():
        for r in range(N):
            g[:, r * W : (r + 1) * W] = own[r // 2, r % 2]

    for i, copy in enumerate(copies):
        copy.wait()

        @pl.when(core[0] == 1)
        def _(i=i):
            dmixed[:, i * W : (i + 1) * W] = dot(g[...], cols[i], NT).astype(BF16)


def softmax(qb, k):
    row = lax.broadcasted_iota(jnp.int32, (T, T), 0)
    col = lax.broadcasted_iota(jnp.int32, (T, T), 1)
    s = jnp.where(row >= col, dot(qb, k, NT) * SCALE, F32(-1e30))
    e = jnp.exp(s - jnp.max(s, axis=-1, keepdims=True))
    return e / jnp.sum(e, axis=-1, keepdims=True)


def attend_kernel(core, low, kvb, got, q, dmixed, mixed, dq_out, own_out, away_out):
    keys = low[0] == 0
    k = jnp.where(keys, kvb[...], got[...])
    v = jnp.where(keys, got[...], kvb[...])

    @pl.when(core[0] == 0)
    def _():
        for h in range(4):
            lanes = slice(h * HEAD_DIM, (h + 1) * HEAD_DIM)
            p = softmax(q[:, lanes].astype(BF16), k)
            mixed[:, lanes] = dot(p.astype(BF16), v).astype(BF16)
        away_out[...] = jnp.zeros((T, HEAD_DIM), BF16)

    @pl.when(core[0] == 1)
    def _():
        dk, dv = 0.0, 0.0
        for h in range(4):
            lanes = slice(h * HEAD_DIM, (h + 1) * HEAD_DIM)
            qb, dm = q[:, lanes].astype(BF16), dmixed[:, lanes]
            p = softmax(qb, k)
            dprob = dot(dm, v, NT)
            dscore = (p * (dprob - jnp.sum(p * dprob, axis=-1, keepdims=True))).astype(BF16)
            dq_out[:, lanes] = dot(dscore, k) * SCALE
            dk += dot(dscore, qb, TN)
            dv += dot(p.astype(BF16), dm, TN)
        dk = dk * SCALE
        own_out[...] = jnp.where(keys, dk, dv)
        away_out[...] = jnp.where(keys, dv, dk).astype(BF16)


def terms_kernel(
    core, low, own, even, gain, wkv, rows, cols, inv, q, kv, mixed, dq, mine, got, x, out, x_out
):
    x_out[...] = x[...]

    @pl.when(core[0] == 0)
    def _():
        for r in range(N):
            here = slice(r * W, (r + 1) * W)
            term = dot(mixed[:, :W], cols[0, :, here]) + dot(mixed[:, W:], cols[1, :, here])
            out[r // 2, r % 2] = term.astype(BF16)

    @pl.when(core[0] == 1)
    def _():
        r_norm = inv[...]
        dkv = mine[...] + got[...].astype(F32)
        share = jnp.sum(dq[...] * q[...], axis=-1, keepdims=True)
        share += jnp.sum(dkv * kv[...], axis=-1, keepdims=True)
        coef = r_norm * r_norm * share * (1.0 / D)
        dqs, dkvs = (dq[...] * r_norm).astype(BF16), (dkv * r_norm).astype(BF16)
        for r in range(N):
            here = slice(r * W, (r + 1) * W)
            f = own[r // 2, 2] if r % 2 else even[r // 2]
            term = dot(dqs[:, :W], rows[0, here, :], NT) + dot(dqs[:, W:], rows[1, here, :], NT)
            term += dot(dkvs, wkv[:, here])
            out[r // 2, r % 2] = (term * gain[:, here] - coef * f.astype(F32)).astype(BF16)


def finish_kernel(core, low, base, twin, got, same, cross):
    for start, side, out in ((base, core[0], same), (twin, 1 - core[0], cross)):
        total = start[...].astype(F32)
        for j in range(8):
            total += got[j, side].astype(F32)
        out[...] = total.astype(BF16)


def store_kernel(core, same, cross, evicted, y_out, dx_out, evicted_out, sems):
    last = pltpu.make_async_copy(evicted, evicted_out.at[0], sems.at[2])
    last.start()

    @pl.when(core[0] == 0)
    def _():
        pltpu.make_async_copy(same, y_out.at[0], sems.at[0]).start()
        pltpu.make_async_copy(cross, dx_out.at[0], sems.at[1]).start()

    @pl.when(core[0] == 1)
    def _():
        pltpu.make_async_copy(cross, y_out.at[0], sems.at[0]).start()
        pltpu.make_async_copy(same, dx_out.at[0], sems.at[1]).start()

    pltpu.make_async_copy(same, y_out.at[0], sems.at[0]).wait()
    pltpu.make_async_copy(cross, dx_out.at[0], sems.at[1]).wait()
    last.wait()


def deliver(block, cross):
    route = []
    for i in range(32):
        route.append((2 * i, 2 * ((i + 1) % 32) + cross))
        route.append((2 * i + 1, 2 * ((i - 1) % 32) + 1 - cross))
    return lax.ppermute(block, SEC + ("c",), route)


def mirror(block):
    return lax.ppermute(block, SEC, [(i, 31 - i) for i in range(32)])


def swap(block, axis):
    return lax.ppermute(block, axis, [(0, 1), (1, 0)])


def exchange(parts):
    return lax.all_to_all(parts, ("x", "yl"), 0, 0, tiled=True)


def body(section_input, section_grad, mirror_store, fetch_slot, norm_gain, w_query, w_keyval, w_output):
    gain, wq, wo, keyval_w = norm_gain, w_query[0], w_output[0], w_keyval[0]
    place = [lax.axis_index(a).astype(jnp.int32).reshape(1) for a in ("c", "yl")]
    tile = ((T, W), BF16)
    wide = ((T, 2 * W), F32)
    column = ((T, HEAD_DIM), F32)
    smem = pl.BlockSpec(memory_space=pltpu.SMEM)
    vmem = pl.BlockSpec(memory_space=pltpu.VMEM)
    small = pltpu.CompilerParams(vmem_limit_bytes=6 * 2**20)

    held, x, g = pl.pallas_call(
        load_kernel,
        out_shape=tuple(pltpu.VMEM((rows, W), BF16) for rows in (T + PAD, T, T)),
        in_specs=[smem] + [pl.BlockSpec(memory_space=pl.ANY)] * 3,
        out_specs=(vmem,) * 3,
        scratch_shapes=[pltpu.SemaphoreType.DMA((3,))],
        compiler_params=small,
    )(fetch_slot, *(in_hbm(a) for a in (mirror_store, section_input, section_grad)))
    fetched = mirror(held)
    base, away = call(trade_kernel, [tile, tile], place, x, g)
    base_twin = swap(away, "c")

    route = []
    for r in range(16):
        part, group = divmod(r // 2, 4)
        route.append((r, 4 * group + 2 * part + r % 2))
    first = lax.ppermute(keyval_w, TEN, route)
    twin = swap(first, "c")

    (spread,) = call(
        spread_kernel, [((8, 3, T, W), BF16)], place, base, base_twin, fetched, after=(first,)
    )
    own = exchange(spread)
    wq2, wo2 = swap(wq, "c"), swap(wo, "c")
    (picked,) = call(pick_kernel, [((8, T, W), BF16)], place, own, flops=6 * 10**9)
    even = swap(picked, "c")

    dmixed, cols = call(
        dmixed_kernel,
        [((T, 2 * W), BF16), ((2, W, D), BF16)],
        place,
        own,
        anywhere=(wo, wo2),
        scratch=[pltpu.VMEM((T, D), BF16), pltpu.SemaphoreType.DMA((2,))],
        flops=10**9,
    )
    xg, inv, kv, kvb, wkv = call(
        keyval_kernel,
        [((T, D), BF16), ((T, 1), F32), column, ((T, HEAD_DIM), BF16), ((HEAD_DIM, D), BF16)],
        place,
        own,
        even,
        gain,
        anywhere=(first, twin),
        after=(dmixed,),
        flops=10**9,
        scratch=[pltpu.VMEM((T, W), F32), pltpu.SemaphoreType.DMA((2,))],
    )
    q, rows = call(
        queries_kernel,
        [wide, ((2, D, W), BF16)],
        place,
        xg,
        inv,
        anywhere=(wq, wq2),
        scratch=[pltpu.SemaphoreType.DMA((2,))],
        flops=10**9,
    )
    mixed, dq, mine, away = call(
        attend_kernel,
        [((T, 2 * W), BF16), wide, column, ((T, HEAD_DIM), BF16)],
        place,
        kvb,
        swap(kvb, "yl"),
        q,
        dmixed,
    )
    terms, x_late = call(
        terms_kernel,
        [((8, 2, T, W), BF16), tile],
        place,
        own,
        even,
        gain,
        wkv,
        rows,
        cols,
        inv,
        q,
        kv,
        mixed,
        dq,
        mine,
        swap(away, "yl"),
        x,
        flops=10**9,
    )
    evicted = mirror(x_late)
    same, cross = call(finish_kernel, [tile, tile], place, base, base_twin, exchange(terms))
    last = (deliver(same, 0), deliver(cross, 1), evicted)
    return pl.pallas_call(
        store_kernel,
        out_shape=tuple(pltpu.HBM((1, T, W), BF16) for _ in range(3)),
        in_specs=[smem] + [vmem] * 3,
        out_specs=tuple(pl.BlockSpec(memory_space=pl.ANY) for _ in range(3)),
        scratch_shapes=[pltpu.SemaphoreType.DMA((3,))],
        compiler_params=small,
    )(place[0], *(pltpu.with_memory_space_constraint(a, pltpu.VMEM) for a in last))


def solution(mesh):
    fine = Mesh(mesh.devices.reshape(16, 2, 4, 2, 2), SEC + TEN)
    cols = P(SEC, None, TEN)
    return jax.shard_map(
        body,
        mesh=fine,
        in_specs=(
            cols,
            cols,
            P(SEC, None, None, TEN),
            P(SEC),
            P(SEC, None),
            cols,
            P(SEC, TEN, None),
            P(SEC, TEN, None),
        ),
        out_specs=(cols, cols, cols),
        check_vma=False,
    )
```

time: 117 us -> 112 us (0.957)
  blocking collectives: 23.2 us -> 0 us
  waiting for transfers between devices: 24.2 us -> 37 us
  Pallas kernels: 9.58 us -> 13.7 us
  starting transfers between devices: 55.1 us -> 58.7 us
  local copies, waits for them, and re-layouts: 1.91 us -> 0.02 us
    all_to_all x1 -> x0, blocking collectives: 23.2 us -> none  [exchange(): return lax.all_to_all(parts, ('x', 'yl'), 0, 0, tiled=True)]
    all_to_all x1 -> x2, waiting for transfers between devices: 11.5 us -> 26.4 us  [exchange(): return lax.all_to_all(parts, ('x', 'yl'), 0, 0, tiled=True)]
    all_to_all x1 -> x2, starting transfers between devices: 3.56 us -> 8.75 us  [exchange(): return lax.all_to_all(parts, ('x', 'yl'), 0, 0, tiled=True)]
    ppermute x1, starting transfers between devices: 5.36 us -> 1.7 us  [body(): first = lax.ppermute(keyval_w, TEN, route)]
    pallas_call x9, Pallas kernels: 8.65 us -> 12.1 us  [call(): pl.pallas_call(ordered, out_shape=tuple((pltpu.VMEM(s, d) for s, d in out...]
    ppermute x2, waiting for transfers between devices: 6.33 us -> 3.25 us  [mirror(): return lax.ppermute(block, SEC, [(i, 31 - i) for i in range(32)])]
    ppermute x2, waiting for transfers between devices: 1.76 us -> 4.57 us  [deliver(): return lax.ppermute(block, SEC + ('c',), route)]
    unnamed x9 -> x6, local copies, waits for them, and re-layouts: 1.91 us -> 0.02 us
  transfers between devices with their start and end apart: 12 -> 14, of which waited for: 6 -> 8; matrix products, arithmetic and copies ran while one was open for 0% -> 0% of each run, Pallas kernels for 5% -> 6%
where the time goes in v5:
time: 112 us; the launch traced here: 111 us
  starting transfers between devices  58.7 us (52%)
  waiting for transfers between devices  37 us (33%)
  Pallas kernels  13.7 us (12%)
  between operations  1.52 us (1%)
    all_to_all x2, waiting for transfers between devices, exchange(): return lax.all_to_all(parts, ('x', 'yl'), 0, 0, tiled=True)  26.4 us
    ppermute x2, starting transfers between devices, mirror(): return lax.ppermute(block, SEC, [(i, 31 - i) for i in range(32)])  20.5 us
    ppermute x7, starting transfers between devices, swap(): return lax.ppermute(block, axis, [(0, 1), (1, 0)])  19.1 us
    pallas_call x9, Pallas kernels, call(): pl.pallas_call(ordered, out_shape=tuple((pltpu.VMEM(s, d) for s, d in out...  12.1 us
    all_to_all x2, starting transfers between devices, exchange(): return lax.all_to_all(parts, ('x', 'yl'), 0, 0, tiled=True)  8.75 us
    ppermute x2, starting transfers between devices, deliver(): return lax.ppermute(block, SEC + ('c',), route)  8.58 us
    ppermute x2, waiting for transfers between devices, deliver(): return lax.ppermute(block, SEC + ('c',), route)  4.57 us
    ppermute x2, waiting for transfers between devices, mirror(): return lax.ppermute(block, SEC, [(i, 31 - i) for i in range(32)])  3.25 us
  transfers between devices with their start and end apart: 14, of which 8 were waited for; matrix products, arithmetic and copies ran while one was open for 0% of the time, Pallas kernels for 6%

profile of v5, /device:TPU:1, one launch (start us, length us, event | category | flops | bytes accessed | tf_op | source)
XLA Modules:
  0.0 110.9 jit_solution(11342635122873732810)
XLA Ops:
  0.6 1.7 %collective-permute-start.2 = (bf16[64,4096]{1,0:T(8,128)(2,1)}, bf16[64,4096]{1,0:T(8,128)(2,1)S(1)}, u32[]{:S(2)}, u32[]{:S(2)}) collective-permute-start(bf16[64,4096]{1,0:T(8,128)(2,1)} %bitcast.9), channel_id=1, source_target_pairs={{0,0},{1,1},{2,4},{3,5},{4,8},{5,9},{6,12},{7,13},{8,2},{9,3},{10,... | collective-permute-start | bytes 1572872 | tf_op jit(solution)/shard_map/ppermute | solution.py:297
  3.0 0.9 shard_map.103
  3.9 14.6 %collective-permute-start.1 = (bf16[144,256]{1,0:T(8,128)(2,1)S(1)}, bf16[144,256]{1,0:T(8,128)(2,1)S(1)}, u32[]{:S(2)}, u32[]{:S(2)}) collective-permute-start(bf16[144,256]{1,0:T(8,128)(2,1)S(1)} %get-tuple-element.29), channel_id=1, source_target_pairs={{0,496},{16,480},{32,464},{48,448},{64,432},{80,416},{96,400},{112... | collective-permute-start | bytes 221192 | tf_op jit(solution)/shard_map/ppermute | solution.py:260
  18.5 2.9 %collective-permute-start = (bf16[128,256]{1,0:T(8,128)(2,1)S(1)}, bf16[128,256]{1,0:T(8,128)(2,1)S(1)}, u32[]{:S(2)}, u32[]{:S(2)}) collective-permute-start(bf16[128,256]{1,0:T(8,128)(2,1)S(1)} %get-tuple-element.28), channel_id=1, source_target_pairs={{0,1},{1,0},{2,3},{3,2},{4,5},{5,4},{6,7},{7,6},{8,9},{9,8},{10,11... | collective-permute-start | bytes 196616 | tf_op jit(solution)/shard_map/ppermute | solution.py:264
  21.4 0.9 collective-permute-done.refs_1_
  22.3 3.2 %collective-permute-done.1.refs_2_ = bf16[144,256]{1,0:T(8,128)(2,1)S(1)} collective-permute-done((bf16[144,256]{1,0:T(8,128)(2,1)S(1)}, bf16[144,256]{1,0:T(8,128)(2,1)S(1)}, u32[]{:S(2)}, u32[]{:S(2)}) %collective-permute-start.1) | collective-permute-done | bytes 73760 | tf_op jit(solution)/shard_map/ppermute | solution.py:260
  25.5 1.3 %shard_map.105 = bf16[8,3,128,256]{3,2,1,0:T(8,128)(2,1)} custom-call(s32[1]{0:T(128)} %bitcast.core, s32[1]{0:T(128)} %bitcast.1.low, bf16[128,256]{1,0:T(8,128)(2,1)S(1)} %get-tuple-element.27.refs_0_, bf16[128,256]{1,0:T(8,128)(2,1)S(1)} %collective-permute-done.refs_1_, bf16[144,256]{1,0:T(8,128)(2,1)S(1)} %collective-permute-done.1.refs_2_, ...), custom_call_target="tpu_custom_call" | custom-call | bytes 204800 | tf_op jit(solution)/shard_map/pallas_call | solution.py:36
  26.8 5.2 %all-to-all-start = ((bf16[8,3,128,256]{3,2,1,0:T(8,128)(2,1)}), bf16[8,3,128,256]{3,2,1,0:T(8,128)(2,1)S(1)}, u32[]{:S(2)}, u32[]{:S(2)}) async-start(bf16[8,3,128,256]{3,2,1,0:T(8,128)(2,1)} %shard_map.105), calls=%async_computation | async-start | bytes 3145728 | tf_op jit(solution)/shard_map/all_to_all | solution.py:268
  32.0 3.1 %collective-permute-start.5 = (bf16[256,4096]{1,0:T(8,128)(2,1)}, bf16[256,4096]{1,0:T(8,128)(2,1)}, u32[]{:S(2)}, u32[]{:S(2)}) collective-permute-start(bf16[256,4096]{1,0:T(8,128)(2,1)} %bitcast.5), channel_id=1, source_target_pairs={{0,1},{1,0},{2,3},{3,2},{4,5},{5,4},{6,7},{7,6},{8,9},{9,8},{10,11... | collective-permute-start | bytes 6291464 | tf_op jit(solution)/shard_map/ppermute | solution.py:264
  35.2 1.9 %collective-permute-start.6 = (bf16[4096,256]{1,0:T(8,128)(2,1)}, bf16[4096,256]{1,0:T(8,128)(2,1)}, u32[]{:S(2)}, u32[]{:S(2)}) collective-permute-start(bf16[4096,256]{1,0:T(8,128)(2,1)} %bitcast.7), channel_id=1, source_target_pairs={{0,1},{1,0},{2,3},{3,2},{4,5},{5,4},{6,7},{7,6},{8,9},{9,8},{10,11... | collective-permute-start | bytes 6291464 | tf_op jit(solution)/shard_map/ppermute | solution.py:264
  37.1 2.4 %collective-permute-start.4 = (bf16[64,4096]{1,0:T(8,128)(2,1)S(1)}, bf16[64,4096]{1,0:T(8,128)(2,1)S(1)}, u32[]{:S(2)}, u32[]{:S(2)}) collective-permute-start(bf16[64,4096]{1,0:T(8,128)(2,1)S(1)} %collective-permute-done.2.refs_3_), channel_id=1, source_target_pairs={{0,1},{1,0},{2,3},{3,2},{4,5},{5,4},{6,7},{7,6},{8,9},{9,8},{10,11... | collective-permute-start | bytes 1572872 | tf_op jit(solution)/shard_map/ppermute | solution.py:264
  39.5 15.3 %all-to-all-done.refs_0_ = bf16[8,3,128,256]{3,2,1,0:T(8,128)(2,1)S(1)} async-done(((bf16[8,3,128,256]{3,2,1,0:T(8,128)(2,1)}), bf16[8,3,128,256]{3,2,1,0:T(8,128)(2,1)S(1)}, u32[]{:S(2)}, u32[]{:S(2)}) %all-to-all-start) | async-done | bytes 1572896 | tf_op jit(solution)/shard_map/all_to_all | solution.py:268
  54.8 0.0 copy-start.2
  54.8 3.8 %collective-permute-start.3 = (bf16[8,128,256]{2,1,0:T(8,128)(2,1)S(1)}, bf16[8,128,256]{2,1,0:T(8,128)(2,1)S(1)}, u32[]{:S(2)}, u32[]{:S(2)}) collective-permute-start(bf16[8,128,256]{2,1,0:T(8,128)(2,1)S(1)} %shard_map.106), channel_id=1, source_target_pairs={{0,1},{1,0},{2,3},{3,2},{4,5},{5,4},{6,7},{7,6},{8,9},{9,8},{10,11... | collective-permute-start | bytes 1572872 | tf_op jit(solution)/shard_map/ppermute | solution.py:264
  58.7 2.6 %shard_map.107 = (bf16[128,512]{1,0:T(8,128)(2,1)S(1)}, bf16[2,256,4096]{2,1,0:T(8,128)(2,1)S(1)}) custom-call(s32[1]{0:T(128)} %bitcast.core, s32[1]{0:T(128)} %bitcast.1.low, bf16[8,3,128,256]{3,2,1,0:T(8,128)(2,1)S(1)} %all-to-all-done.refs_0_, bf16[256,4096]{1,0:T(8,128)(2,1)S(1)} %bitcast.6, bf16[256,4096]{1,0:T(8,128)(2,1)} %collective-permute-done.5.refs_2_), custom_call_target="tpu_custom_call" | custom-call | flops 1000000000 | bytes 1572864 | tf_op jit(solution)/shard_map/pallas_call | solution.py:36
  61.3 1.0 shard_map.108
  62.3 1.9 %collective-permute-start.7 = (bf16[128,128]{1,0:T(8,128)(2,1)S(1)}, bf16[128,128]{1,0:T(8,128)(2,1)S(1)}, u32[]{:S(2)}, u32[]{:S(2)}) collective-permute-start(bf16[128,128]{1,0:T(8,128)(2,1)S(1)} %get-tuple-element.38.refs_0_), channel_id=1, source_target_pairs={{0,2},{2,0},{1,3},{3,1},{4,6},{6,4},{5,7},{7,5},{8,10},{10,8},{9,1... | collective-permute-start | bytes 98312 | tf_op jit(solution)/shard_map/ppermute | solution.py:264
  64.3 2.4 %shard_map.109 = (f32[128,512]{1,0:T(8,128)S(1)}, bf16[2,4096,256]{2,1,0:T(8,128)(2,1)S(1)}) custom-call(s32[1]{0:T(128)} %bitcast.core, s32[1]{0:T(128)} %bitcast.1.low, bf16[128,4096]{1,0:T(8,128)(2,1)S(1)} %get-tuple-element.32.refs_0_, f32[128,1]{1,0:T(8,128)S(1)} %get-tuple-element.33.refs_1_.refs_6_, bf16[4096,256]{1,0:T(8,128)(2,1)S(1)} %bitcast.8, ...), custom_call_target="tpu_custom_call" | custom-call | flops 1000000000 | bytes 1049088 | tf_op jit(solution)/shard_map/pallas_call | solution.py:36
  66.7 0.3 collective-permute-done.7.refs_1_
  67.0 1.7 %shard_map.110 = (bf16[128,512]{1,0:T(8,128)(2,1)S(1)}, f32[128,512]{1,0:T(8,128)S(1)}, f32[128,128]{1,0:T(8,128)S(1)}, bf16[128,128]{1,0:T(8,128)(2,1)S(1)}) custom-call(s32[1]{0:T(128)} %bitcast.core, s32[1]{0:T(128)} %bitcast.1.low, bf16[128,128]{1,0:T(8,128)(2,1)S(1)} %get-tuple-element.38.refs_0_, bf16[128,128]{1,0:T(8,128)(2,1)S(1)} %collective-permute-done.7.refs_1_, ...), custom_call_target="tpu_custom_call" | custom-call | bytes 458752 | tf_op jit(solution)/shard_map/pallas_call | solution.py:36
  68.7 3.1 %collective-permute-start.8 = (bf16[128,128]{1,0:T(8,128)(2,1)S(1)}, bf16[128,128]{1,0:T(8,128)(2,1)S(1)}, u32[]{:S(2)}, u32[]{:S(2)}) collective-permute-start(bf16[128,128]{1,0:T(8,128)(2,1)S(1)} %get-tuple-element.42), channel_id=1, source_target_pairs={{0,2},{2,0},{1,3},{3,1},{4,6},{6,4},{5,7},{7,5},{8,10},{10,8},{9,1... | collective-permute-start | bytes 98312 | tf_op jit(solution)/shard_map/ppermute | solution.py:264
  71.8 1.6 %collective-permute-done.8.refs_12_ = bf16[128,128]{1,0:T(8,128)(2,1)S(1)} collective-permute-done((bf16[128,128]{1,0:T(8,128)(2,1)S(1)}, bf16[128,128]{1,0:T(8,128)(2,1)S(1)}, u32[]{:S(2)}, u32[]{:S(2)}) %collective-permute-start.8) | collective-permute-done | bytes 32800 | tf_op jit(solution)/shard_map/ppermute | solution.py:264
  73.4 2.9 %shard_map.111 = (bf16[8,2,128,256]{3,2,1,0:T(8,128)(2,1)}, bf16[128,256]{1,0:T(8,128)(2,1)S(1)}) custom-call(s32[1]{0:T(128)} %bitcast.core, s32[1]{0:T(128)} %bitcast.1.low, bf16[8,3,128,256]{3,2,1,0:T(8,128)(2,1)S(1)} %all-to-all-done.refs_0_, bf16[8,128,256]{2,1,0:T(8,128)(2,1)S(1)} %collective-permute-done.3.refs_1_, f32[1,4096]{1,0:T(1,128)S(1)} %copy-done.2, ...), custom_call_target="tpu_custom_call" | custom-call | flops 1000000000 | bytes 12435968 | tf_op jit(solution)/shard_map/pallas_call | solution.py:36
  76.3 3.6 %all-to-all-start.1 = ((bf16[8,2,128,256]{3,2,1,0:T(8,128)(2,1)}), bf16[8,2,128,256]{3,2,1,0:T(8,128)(2,1)S(1)}, u32[]{:S(2)}, u32[]{:S(2)}) async-start(bf16[8,2,128,256]{3,2,1,0:T(8,128)(2,1)} %get-tuple-element.43), calls=%async_computation.1 | async-start | bytes 2097152 | tf_op jit(solution)/shard_map/all_to_all | solution.py:268
  79.8 5.9 %collective-permute-start.11 = (bf16[128,256]{1,0:T(8,128)(2,1)S(1)}, bf16[128,256]{1,0:T(8,128)(2,1)S(1)}, u32[]{:S(2)}, u32[]{:S(2)}) collective-permute-start(bf16[128,256]{1,0:T(8,128)(2,1)S(1)} %get-tuple-element.46), channel_id=1, source_target_pairs={{0,496},{16,480},{32,464},{48,448},{64,432},{80,416},{96,400},{112... | collective-permute-start | bytes 196616 | tf_op jit(solution)/shard_map/ppermute | solution.py:260
  85.8 11.1 %all-to-all-done.1.refs_2_ = bf16[8,2,128,256]{3,2,1,0:T(8,128)(2,1)S(1)} async-done(((bf16[8,2,128,256]{3,2,1,0:T(8,128)(2,1)}), bf16[8,2,128,256]{3,2,1,0:T(8,128)(2,1)S(1)}, u32[]{:S(2)}, u32[]{:S(2)}) %all-to-all-start.1) | async-done | bytes 1048608 | tf_op jit(solution)/shard_map/all_to_all | solution.py:268
  96.9 0.2 shard_map.112
  97.0 6.7 %collective-permute-start.10 = (bf16[128,256]{1,0:T(8,128)(2,1)S(1)}, bf16[128,256]{1,0:T(8,128)(2,1)S(1)}, u32[]{:S(2)}, u32[]{:S(2)}) collective-permute-start(bf16[128,256]{1,0:T(8,128)(2,1)S(1)} %get-tuple-element.45), channel_id=1, source_target_pairs={{0,17},{1,496},{16,33},{17,0},{32,49},{33,16},{48,65},{49,32},{64,... | collective-permute-start | bytes 196616 | tf_op jit(solution)/shard_map/ppermute | solution.py:256
  103.7 1.9 %collective-permute-start.9 = (bf16[128,256]{1,0:T(8,128)(2,1)S(1)}, bf16[128,256]{1,0:T(8,128)(2,1)S(1)}, u32[]{:S(2)}, u32[]{:S(2)}) collective-permute-start(bf16[128,256]{1,0:T(8,128)(2,1)S(1)} %get-tuple-element.44), channel_id=1, source_target_pairs={{0,16},{1,497},{16,32},{17,1},{32,48},{33,17},{48,64},{49,33},{64,... | collective-permute-start | bytes 196616 | tf_op jit(solution)/shard_map/ppermute | solution.py:256
  105.7 0.6 collective-permute-done.10.cross
  106.2 4.0 %collective-permute-done.9.same = bf16[128,256]{1,0:T(8,128)(2,1)S(1)} collective-permute-done((bf16[128,256]{1,0:T(8,128)(2,1)S(1)}, bf16[128,256]{1,0:T(8,128)(2,1)S(1)}, u32[]{:S(2)}, u32[]{:S(2)}) %collective-permute-start.9) | collective-permute-done | bytes 65568 | tf_op jit(solution)/shard_map/ppermute | solution.py:256
  110.2 0.7 shard_map.113
  (13 shorter events, 0.1 us)
Async XLA Ops:
  0.6 24.9 %collective-permute-start.2 = (bf16[64,4096]{1,0:T(8,128)(2,1)}, bf16[64,4096]{1,0:T(8,128)(2,1)S(1)}, u32[]{:S(2)}, u32[]{:S(2)}) collective-permute-start(bf16[64,4096]{1,0:T(8,128)(2,1)} %bitcast.9), channel_id=1, source_target_pairs={{0,0},{1,1},{2,4},{3,5},{4,8},{5,9},{6,12},{7,13},{8,2},{9,3},{10,... | collective-permute-start | bytes 1572872 | tf_op jit(solution)/shard_map/ppermute | solution.py:297
  3.9 21.6 %collective-permute-start.1 = (bf16[144,256]{1,0:T(8,128)(2,1)S(1)}, bf16[144,256]{1,0:T(8,128)(2,1)S(1)}, u32[]{:S(2)}, u32[]{:S(2)}) collective-permute-start(bf16[144,256]{1,0:T(8,128)(2,1)S(1)} %get-tuple-element.29), channel_id=1, source_target_pairs={{0,496},{16,480},{32,464},{48,448},{64,432},{80,416},{96,400},{112... | collective-permute-start | bytes 221192 | tf_op jit(solution)/shard_map/ppermute | solution.py:260
  18.5 3.8 %collective-permute-start = (bf16[128,256]{1,0:T(8,128)(2,1)S(1)}, bf16[128,256]{1,0:T(8,128)(2,1)S(1)}, u32[]{:S(2)}, u32[]{:S(2)}) collective-permute-start(bf16[128,256]{1,0:T(8,128)(2,1)S(1)} %get-tuple-element.28), channel_id=1, source_target_pairs={{0,1},{1,0},{2,3},{3,2},{4,5},{5,4},{6,7},{7,6},{8,9},{9,8},{10,11... | collective-permute-start | bytes 196616 | tf_op jit(solution)/shard_map/ppermute | solution.py:264
  26.8 27.9 %all-to-all-start = ((bf16[8,3,128,256]{3,2,1,0:T(8,128)(2,1)}), bf16[8,3,128,256]{3,2,1,0:T(8,128)(2,1)S(1)}, u32[]{:S(2)}, u32[]{:S(2)}) async-start(bf16[8,3,128,256]{3,2,1,0:T(8,128)(2,1)} %shard_map.105), calls=%async_computation | async-start | bytes 3145728 | tf_op jit(solution)/shard_map/all_to_all | solution.py:268
  32.0 26.6 %collective-permute-start.5 = (bf16[256,4096]{1,0:T(8,128)(2,1)}, bf16[256,4096]{1,0:T(8,128)(2,1)}, u32[]{:S(2)}, u32[]{:S(2)}) collective-permute-start(bf16[256,4096]{1,0:T(8,128)(2,1)} %bitcast.5), channel_id=1, source_target_pairs={{0,1},{1,0},{2,3},{3,2},{4,5},{5,4},{6,7},{7,6},{8,9},{9,8},{10,11... | collective-permute-start | bytes 6291464 | tf_op jit(solution)/shard_map/ppermute | solution.py:264
  35.2 29.1 %collective-permute-start.6 = (bf16[4096,256]{1,0:T(8,128)(2,1)}, bf16[4096,256]{1,0:T(8,128)(2,1)}, u32[]{:S(2)}, u32[]{:S(2)}) collective-permute-start(bf16[4096,256]{1,0:T(8,128)(2,1)} %bitcast.7), channel_id=1, source_target_pairs={{0,1},{1,0},{2,3},{3,2},{4,5},{5,4},{6,7},{7,6},{8,9},{9,8},{10,11... | collective-permute-start | bytes 6291464 | tf_op jit(solution)/shard_map/ppermute | solution.py:264
  37.1 24.2 %collective-permute-start.4 = (bf16[64,4096]{1,0:T(8,128)(2,1)S(1)}, bf16[64,4096]{1,0:T(8,128)(2,1)S(1)}, u32[]{:S(2)}, u32[]{:S(2)}) collective-permute-start(bf16[64,4096]{1,0:T(8,128)(2,1)S(1)} %collective-permute-done.2.refs_3_), channel_id=1, source_target_pairs={{0,1},{1,0},{2,3},{3,2},{4,5},{5,4},{6,7},{7,6},{8,9},{9,8},{10,11... | collective-permute-start | bytes 1572872 | tf_op jit(solution)/shard_map/ppermute | solution.py:264
  54.8 3.9 %copy-start = (bf16[1,256,4096]{2,1,0:T(8,128)(2,1)S(1)}, bf16[1,256,4096]{2,1,0:T(8,128)(2,1)}, u32[]{:S(2)}) copy-start(bf16[1,256,4096]{2,1,0:T(8,128)(2,1)} %param.15) | copy-start | bytes 6291460
  54.8 6.5 %copy-start.2 = (f32[1,4096]{1,0:T(1,128)S(1)}, f32[1,4096]{1,0:T(1,128)}, u32[]{:S(2)}) copy-start(f32[1,4096]{1,0:T(1,128)} %refs_2_.3) | copy-start | bytes 49156
  54.8 6.4 %collective-permute-start.3 = (bf16[8,128,256]{2,1,0:T(8,128)(2,1)S(1)}, bf16[8,128,256]{2,1,0:T(8,128)(2,1)S(1)}, u32[]{:S(2)}, u32[]{:S(2)}) collective-permute-start(bf16[8,128,256]{2,1,0:T(8,128)(2,1)S(1)} %shard_map.106), channel_id=1, source_target_pairs={{0,1},{1,0},{2,3},{3,2},{4,5},{5,4},{6,7},{7,6},{8,9},{9,8},{10,11... | collective-permute-start | bytes 1572872 | tf_op jit(solution)/shard_map/ppermute | solution.py:264
  61.3 3.0 %copy-start.1 = (bf16[1,4096,256]{2,1,0:T(8,128)(2,1)S(1)}, bf16[1,4096,256]{2,1,0:T(8,128)(2,1)}, u32[]{:S(2)}) copy-start(bf16[1,4096,256]{2,1,0:T(8,128)(2,1)} %param.13) | copy-start | bytes 6291460
  62.3 4.7 %collective-permute-start.7 = (bf16[128,128]{1,0:T(8,128)(2,1)S(1)}, bf16[128,128]{1,0:T(8,128)(2,1)S(1)}, u32[]{:S(2)}, u32[]{:S(2)}) collective-permute-start(bf16[128,128]{1,0:T(8,128)(2,1)S(1)} %get-tuple-element.38.refs_0_), channel_id=1, source_target_pairs={{0,2},{2,0},{1,3},{3,1},{4,6},{6,4},{5,7},{7,5},{8,10},{10,8},{9,1... | collective-permute-start | bytes 98312 | tf_op jit(solution)/shard_map/ppermute | solution.py:264
  68.7 4.7 %collective-permute-start.8 = (bf16[128,128]{1,0:T(8,128)(2,1)S(1)}, bf16[128,128]{1,0:T(8,128)(2,1)S(1)}, u32[]{:S(2)}, u32[]{:S(2)}) collective-permute-start(bf16[128,128]{1,0:T(8,128)(2,1)S(1)} %get-tuple-element.42), channel_id=1, source_target_pairs={{0,2},{2,0},{1,3},{3,1},{4,6},{6,4},{5,7},{7,5},{8,10},{10,8},{9,1... | collective-permute-start | bytes 98312 | tf_op jit(solution)/shard_map/ppermute | solution.py:264
  76.3 20.6 %all-to-all-start.1 = ((bf16[8,2,128,256]{3,2,1,0:T(8,128)(2,1)}), bf16[8,2,128,256]{3,2,1,0:T(8,128)(2,1)S(1)}, u32[]{:S(2)}, u32[]{:S(2)}) async-start(bf16[8,2,128,256]{3,2,1,0:T(8,128)(2,1)} %get-tuple-element.43), calls=%async_computation.1 | async-start | bytes 2097152 | tf_op jit(solution)/shard_map/all_to_all | solution.py:268
  79.8 25.8 %collective-permute-start.11 = (bf16[128,256]{1,0:T(8,128)(2,1)S(1)}, bf16[128,256]{1,0:T(8,128)(2,1)S(1)}, u32[]{:S(2)}, u32[]{:S(2)}) collective-permute-start(bf16[128,256]{1,0:T(8,128)(2,1)S(1)} %get-tuple-element.46), channel_id=1, source_target_pairs={{0,496},{16,480},{32,464},{48,448},{64,432},{80,416},{96,400},{112... | collective-permute-start | bytes 196616 | tf_op jit(solution)/shard_map/ppermute | solution.py:260
  97.0 9.2 %collective-permute-start.10 = (bf16[128,256]{1,0:T(8,128)(2,1)S(1)}, bf16[128,256]{1,0:T(8,128)(2,1)S(1)}, u32[]{:S(2)}, u32[]{:S(2)}) collective-permute-start(bf16[128,256]{1,0:T(8,128)(2,1)S(1)} %get-tuple-element.45), channel_id=1, source_target_pairs={{0,17},{1,496},{16,33},{17,0},{32,49},{33,16},{48,65},{49,32},{64,... | collective-permute-start | bytes 196616 | tf_op jit(solution)/shard_map/ppermute | solution.py:256
  103.7 6.5 %collective-permute-start.9 = (bf16[128,256]{1,0:T(8,128)(2,1)S(1)}, bf16[128,256]{1,0:T(8,128)(2,1)S(1)}, u32[]{:S(2)}, u32[]{:S(2)}) collective-permute-start(bf16[128,256]{1,0:T(8,128)(2,1)S(1)} %get-tuple-element.44), channel_id=1, source_target_pairs={{0,16},{1,497},{16,32},{17,1},{32,48},{33,17},{48,64},{49,33},{64,... | collective-permute-start | bytes 196616 | tf_op jit(solution)/shard_map/ppermute | solution.py:256

commit v6 on v5

--- a/solution.py
+++ b/solution.py
@@ -79,7 +79,8 @@
         away[...] = x[...]
 
 
-def spread_kernel(core, low, base, twin, fetched, out):
+def spread_kernel(core, low, base, twin, fetched, x, out, x_out):
+    x_out[...] = x[...]
     for j in range(8):
         out[j, core[0]] = base[...]
         out[j, 1 - core[0]] = twin[...]
@@ -193,17 +194,26 @@
         away_out[...] = jnp.where(keys, dv, dk).astype(BF16)
 
 
-def terms_kernel(
-    core, low, own, even, gain, wkv, rows, cols, inv, q, kv, mixed, dq, mine, got, x, out, x_out
-):
-    x_out[...] = x[...]
-
+def products_kernel(core, low, rows, cols, mixed, dq, inv, part):
     @pl.when(core[0] == 0)
     def _():
         for r in range(N):
             here = slice(r * W, (r + 1) * W)
-            term = dot(mixed[:, :W], cols[0, :, here]) + dot(mixed[:, W:], cols[1, :, here])
-            out[r // 2, r % 2] = term.astype(BF16)
+            part[r] = dot(mixed[:, :W], cols[0, :, here]) + dot(mixed[:, W:], cols[1, :, here])
+
+    @pl.when(core[0] == 1)
+    def _():
+        dqs = (dq[...] * inv[...]).astype(BF16)
+        for r in range(N):
+            here = slice(r * W, (r + 1) * W)
+            part[r] = dot(dqs[:, :W], rows[0, here, :], NT) + dot(dqs[:, W:], rows[1, here, :], NT)
+
+
+def terms_kernel(core, low, part, own, even, gain, wkv, inv, q, kv, dq, mine, got, out):
+    @pl.when(core[0] == 0)
+    def _():
+        for r in range(N):
+            out[r // 2, r % 2] = part[r].astype(BF16)
 
     @pl.when(core[0] == 1)
     def _():
@@ -212,12 +222,11 @@
         share = jnp.sum(dq[...] * q[...], axis=-1, keepdims=True)
         share += jnp.sum(dkv * kv[...], axis=-1, keepdims=True)
         coef = r_norm * r_norm * share * (1.0 / D)
-        dqs, dkvs = (dq[...] * r_norm).astype(BF16), (dkv * r_norm).astype(BF16)
+        dkvs = (dkv * r_norm).astype(BF16)
         for r in range(N):
             here = slice(r * W, (r + 1) * W)
             f = own[r // 2, 2] if r % 2 else even[r // 2]
-            term = dot(dqs[:, :W], rows[0, here, :], NT) + dot(dqs[:, W:], rows[1, here, :], NT)
-            term += dot(dkvs, wkv[:, here])
+            term = part[r] + dot(dkvs, wkv[:, here])
             out[r // 2, r % 2] = (term * gain[:, here] - coef * f.astype(F32)).astype(BF16)
 
 
@@ -297,12 +306,20 @@
     first = lax.ppermute(keyval_w, TEN, route)
     twin = swap(first, "c")
 
-    (spread,) = call(
-        spread_kernel, [((8, 3, T, W), BF16)], place, base, base_twin, fetched, after=(first,)
+    spread, x_late = call(
+        spread_kernel,
+        [((8, 3, T, W), BF16), tile],
+        place,
+        base,
+        base_twin,
+        fetched,
+        x,
+        after=(first,),
     )
     own = exchange(spread)
+    evicted = mirror(x_late)
     wq2, wo2 = swap(wq, "c"), swap(wo, "c")
-    (picked,) = call(pick_kernel, [((8, T, W), BF16)], place, own, flops=6 * 10**9)
+    (picked,) = call(pick_kernel, [((8, T, W), BF16)], place, own, flops=30 * 10**9, after=(evicted,))
     even = swap(picked, "c")
 
     dmixed, cols = call(
@@ -345,27 +362,25 @@
         q,
         dmixed,
     )
-    terms, x_late = call(
+    (part,) = call(
+        products_kernel, [((N, T, W), F32)], place, rows, cols, mixed, dq, inv, flops=10**9
+    )
+    (terms,) = call(
         terms_kernel,
-        [((8, 2, T, W), BF16), tile],
-        place,
+        [((8, 2, T, W), BF16)],
+        place,
+        part,
         own,
         even,
         gain,
         wkv,
-        rows,
-        cols,
         inv,
         q,
         kv,
-        mixed,
         dq,
         mine,
         swap(away, "yl"),
-        x,
-        flops=10**9,
-    )
-    evicted = mirror(x_late)
+    )
     same, cross = call(finish_kernel, [tile, tile], place, base, base_twin, exchange(terms))
     last = (deliver(same, 0), deliver(cross, 1), evicted)
     return pl.pallas_call(

time: 112 us -> 108 us (0.964)
  waiting for transfers between devices: 37 us -> 16.4 us
  blocking collectives: 0 us -> 16.7 us
    all_to_all x2 -> x1, waiting for transfers between devices: 26.4 us -> 7.93 us  [exchange(): return lax.all_to_all(parts, ('x', 'yl'), 0, 0, tiled=True)]
    all_to_all x0 -> x1, blocking collectives: none -> 16.7 us  [exchange(): return lax.all_to_all(parts, ('x', 'yl'), 0, 0, tiled=True)]
    all_to_all x2 -> x1, starting transfers between devices: 8.75 us -> 5.19 us  [exchange(): return lax.all_to_all(parts, ('x', 'yl'), 0, 0, tiled=True)]
    ppermute x2, starting transfers between devices: 8.58 us -> 11.1 us  [deliver(): return lax.ppermute(block, SEC + ('c',), route)]
    ppermute x7, waiting for transfers between devices: 2.77 us -> 1.26 us  [swap(): return lax.ppermute(block, axis, [(0, 1), (1, 0)])]
    ppermute x7, starting transfers between devices: 19.1 us -> 20.4 us  [swap(): return lax.ppermute(block, axis, [(0, 1), (1, 0)])]
    pallas_call x9 -> x10, Pallas kernels: 12.1 us -> 11.4 us  [call(): pl.pallas_call(ordered, out_shape=tuple((pltpu.VMEM(s, d) for s, d in out...]
  transfers between devices with their start and end apart: 14 -> 13, of which waited for: 8 -> 6; matrix products, arithmetic and copies ran while one was open for 0% -> 0% of each run, Pallas kernels for 6% -> 8%
where the time goes in v6:
time: 108 us; the launch traced here: 107 us
  starting transfers between devices  59.8 us (55%)
  blocking collectives  16.7 us (15%)
  waiting for transfers between devices  16.4 us (15%)
  Pallas kernels  13 us (12%)
  between operations  1.54 us (1%)
    ppermute x2, starting transfers between devices, mirror(): return lax.ppermute(block, SEC, [(i, 31 - i) for i in range(32)])  21.4 us
    ppermute x7, starting transfers between devices, swap(): return lax.ppermute(block, axis, [(0, 1), (1, 0)])  20.4 us
    all_to_all x1, blocking collectives, exchange(): return lax.all_to_all(parts, ('x', 'yl'), 0, 0, tiled=True)  16.7 us
    pallas_call x10, Pallas kernels, call(): pl.pallas_call(ordered, out_shape=tuple((pltpu.VMEM(s, d) for s, d in out...  11.4 us
    ppermute x2, starting transfers between devices, deliver(): return lax.ppermute(block, SEC + ('c',), route)  11.1 us
    all_to_all x1, waiting for transfers between devices, exchange(): return lax.all_to_all(parts, ('x', 'yl'), 0, 0, tiled=True)  7.93 us
    all_to_all x1, starting transfers between devices, exchange(): return lax.all_to_all(parts, ('x', 'yl'), 0, 0, tiled=True)  5.19 us
    ppermute x2, waiting for transfers between devices, deliver(): return lax.ppermute(block, SEC + ('c',), route)  4 us
  transfers between devices with their start and end apart: 13, of which 6 were waited for; matrix products, arithmetic and copies ran while one was open for 0% of the time, Pallas kernels for 8%

profile of v6, /device:TPU:1, one launch (start us, length us, event | category | flops | bytes accessed | tf_op | source)
XLA Modules:
  0.0 107.5 jit_solution(6266246955045934377)
XLA Ops:
  0.6 1.7 %collective-permute-start.2 = (bf16[64,4096]{1,0:T(8,128)(2,1)}, bf16[64,4096]{1,0:T(8,128)(2,1)S(1)}, u32[]{:S(2)}, u32[]{:S(2)}) collective-permute-start(bf16[64,4096]{1,0:T(8,128)(2,1)} %bitcast.9), channel_id=1, source_target_pairs={{0,0},{1,1},{2,4},{3,5},{4,8},{5,9},{6,12},{7,13},{8,2},{9,3},{10,... | collective-permute-start | bytes 1572872 | tf_op jit(solution)/shard_map/ppermute | solution.py:306
  3.0 0.9 shard_map.103
  3.9 14.6 %collective-permute-start.1 = (bf16[144,256]{1,0:T(8,128)(2,1)S(1)}, bf16[144,256]{1,0:T(8,128)(2,1)S(1)}, u32[]{:S(2)}, u32[]{:S(2)}) collective-permute-start(bf16[144,256]{1,0:T(8,128)(2,1)S(1)} %get-tuple-element.29), channel_id=1, source_target_pairs={{0,496},{16,480},{32,464},{48,448},{64,432},{80,416},{96,400},{112... | collective-permute-start | bytes 221192 | tf_op jit(solution)/shard_map/ppermute | solution.py:269
  18.5 2.9 %collective-permute-start = (bf16[128,256]{1,0:T(8,128)(2,1)S(1)}, bf16[128,256]{1,0:T(8,128)(2,1)S(1)}, u32[]{:S(2)}, u32[]{:S(2)}) collective-permute-start(bf16[128,256]{1,0:T(8,128)(2,1)S(1)} %get-tuple-element.28), channel_id=1, source_target_pairs={{0,1},{1,0},{2,3},{3,2},{4,5},{5,4},{6,7},{7,6},{8,9},{9,8},{10,11... | collective-permute-start | bytes 196616 | tf_op jit(solution)/shard_map/ppermute | solution.py:273
  21.4 0.9 collective-permute-done.refs_1_
  22.3 3.2 %collective-permute-done.1.refs_2_ = bf16[144,256]{1,0:T(8,128)(2,1)S(1)} collective-permute-done((bf16[144,256]{1,0:T(8,128)(2,1)S(1)}, bf16[144,256]{1,0:T(8,128)(2,1)S(1)}, u32[]{:S(2)}, u32[]{:S(2)}) %collective-permute-start.1) | collective-permute-done | bytes 73760 | tf_op jit(solution)/shard_map/ppermute | solution.py:269
  25.5 1.3 %shard_map.105 = (bf16[8,3,128,256]{3,2,1,0:T(8,128)(2,1)}, bf16[128,256]{1,0:T(8,128)(2,1)S(1)}) custom-call(s32[1]{0:T(128)} %bitcast.core, s32[1]{0:T(128)} %bitcast.1.low, bf16[128,256]{1,0:T(8,128)(2,1)S(1)} %get-tuple-element.27.refs_0_, bf16[128,256]{1,0:T(8,128)(2,1)S(1)} %collective-permute-done.refs_1_, ...), custom_call_target="tpu_custom_call" | custom-call | bytes 270336 | tf_op jit(solution)/shard_map/pallas_call | solution.py:36
  26.8 5.2 %all-to-all-start = ((bf16[8,3,128,256]{3,2,1,0:T(8,128)(2,1)}), bf16[8,3,128,256]{3,2,1,0:T(8,128)(2,1)S(1)}, u32[]{:S(2)}, u32[]{:S(2)}) async-start(bf16[8,3,128,256]{3,2,1,0:T(8,128)(2,1)} %get-tuple-element.30), calls=%async_computation | async-start | bytes 3145728 | tf_op jit(solution)/shard_map/all_to_all | solution.py:277
  32.0 6.8 %collective-permute-start.3 = (bf16[128,256]{1,0:T(8,128)(2,1)S(1)}, bf16[128,256]{1,0:T(8,128)(2,1)S(1)}, u32[]{:S(2)}, u32[]{:S(2)}) collective-permute-start(bf16[128,256]{1,0:T(8,128)(2,1)S(1)} %get-tuple-element.31), channel_id=1, source_target_pairs={{0,496},{16,480},{32,464},{48,448},{64,432},{80,416},{96,400},{112... | collective-permute-start | bytes 196616 | tf_op jit(solution)/shard_map/ppermute | solution.py:269
  38.8 4.3 %collective-permute-start.6 = (bf16[256,4096]{1,0:T(8,128)(2,1)}, bf16[256,4096]{1,0:T(8,128)(2,1)}, u32[]{:S(2)}, u32[]{:S(2)}) collective-permute-start(bf16[256,4096]{1,0:T(8,128)(2,1)} %bitcast.5), channel_id=1, source_target_pairs={{0,1},{1,0},{2,3},{3,2},{4,5},{5,4},{6,7},{7,6},{8,9},{9,8},{10,11... | collective-permute-start | bytes 6291464 | tf_op jit(solution)/shard_map/ppermute | solution.py:273
  43.2 1.9 %collective-permute-start.7 = (bf16[4096,256]{1,0:T(8,128)(2,1)}, bf16[4096,256]{1,0:T(8,128)(2,1)}, u32[]{:S(2)}, u32[]{:S(2)}) collective-permute-start(bf16[4096,256]{1,0:T(8,128)(2,1)} %bitcast.7), channel_id=1, source_target_pairs={{0,1},{1,0},{2,3},{3,2},{4,5},{5,4},{6,7},{7,6},{8,9},{9,8},{10,11... | collective-permute-start | bytes 6291464 | tf_op jit(solution)/shard_map/ppermute | solution.py:273
  45.1 2.4 %collective-permute-start.5 = (bf16[64,4096]{1,0:T(8,128)(2,1)S(1)}, bf16[64,4096]{1,0:T(8,128)(2,1)S(1)}, u32[]{:S(2)}, u32[]{:S(2)}) collective-permute-start(bf16[64,4096]{1,0:T(8,128)(2,1)S(1)} %collective-permute-done.2.refs_4_.refs_3_), channel_id=1, source_target_pairs={{0,1},{1,0},{2,3},{3,2},{4,5},{5,4},{6,7},{7,6},{8,9},{9,8},{10,11... | collective-permute-start | bytes 1572872 | tf_op jit(solution)/shard_map/ppermute | solution.py:273
  47.6 7.9 %all-to-all-done.refs_0_.refs_1_ = bf16[8,3,128,256]{3,2,1,0:T(8,128)(2,1)S(1)} async-done(((bf16[8,3,128,256]{3,2,1,0:T(8,128)(2,1)}), bf16[8,3,128,256]{3,2,1,0:T(8,128)(2,1)S(1)}, u32[]{:S(2)}, u32[]{:S(2)}) %all-to-all-start) | async-done | bytes 1572896 | tf_op jit(solution)/shard_map/all_to_all | solution.py:277
  55.5 0.0 copy-start.2
  55.5 3.8 %collective-permute-start.4 = (bf16[8,128,256]{2,1,0:T(8,128)(2,1)S(1)}, bf16[8,128,256]{2,1,0:T(8,128)(2,1)S(1)}, u32[]{:S(2)}, u32[]{:S(2)}) collective-permute-start(bf16[8,128,256]{2,1,0:T(8,128)(2,1)S(1)} %shard_map.106), channel_id=1, source_target_pairs={{0,1},{1,0},{2,3},{3,2},{4,5},{5,4},{6,7},{7,6},{8,9},{9,8},{10,11... | collective-permute-start | bytes 1572872 | tf_op jit(solution)/shard_map/ppermute | solution.py:273
  59.4 2.6 %shard_map.107 = (bf16[128,512]{1,0:T(8,128)(2,1)S(1)}, bf16[2,256,4096]{2,1,0:T(8,128)(2,1)S(1)}) custom-call(s32[1]{0:T(128)} %bitcast.core, s32[1]{0:T(128)} %bitcast.1.low, bf16[8,3,128,256]{3,2,1,0:T(8,128)(2,1)S(1)} %all-to-all-done.refs_0_.refs_1_, bf16[256,4096]{1,0:T(8,128)(2,1)S(1)} %bitcast.6, bf16[256,4096]{1,0:T(8,128)(2,1)} %collective-permute-done.6.refs_2_), custom_call_target="tpu_custom_call" | custom-call | flops 1000000000 | bytes 1572864 | tf_op jit(solution)/shard_map/pallas_call | solution.py:36
  62.0 0.0 copy-start.1
  62.0 1.0 shard_map.108
  63.0 1.9 %collective-permute-start.8 = (bf16[128,128]{1,0:T(8,128)(2,1)S(1)}, bf16[128,128]{1,0:T(8,128)(2,1)S(1)}, u32[]{:S(2)}, u32[]{:S(2)}) collective-permute-start(bf16[128,128]{1,0:T(8,128)(2,1)S(1)} %get-tuple-element.37.refs_0_), channel_id=1, source_target_pairs={{0,2},{2,0},{1,3},{3,1},{4,6},{6,4},{5,7},{7,5},{8,10},{10,8},{9,1... | collective-permute-start | bytes 98312 | tf_op jit(solution)/shard_map/ppermute | solution.py:273
  65.0 2.4 %shard_map.109 = (f32[128,512]{1,0:T(8,128)S(1)}, bf16[2,4096,256]{2,1,0:T(8,128)(2,1)S(1)}) custom-call(s32[1]{0:T(128)} %bitcast.core, s32[1]{0:T(128)} %bitcast.1.low, bf16[128,4096]{1,0:T(8,128)(2,1)S(1)} %get-tuple-element.33.refs_0_, f32[128,1]{1,0:T(8,128)S(1)} %get-tuple-element.34.refs_1_.refs_4_.refs_5_, bf16[4096,256]{1,0:T(8,128)(2,1)S(1)} %bitcast.8, ...), custom_call_target="tpu_custom_call" | custom-call | flops 1000000000 | bytes 1049088 | tf_op jit(solution)/shard_map/pallas_call | solution.py:36
  67.4 0.3 collective-permute-done.8.refs_1_
  67.7 1.7 %shard_map.110 = (bf16[128,512]{1,0:T(8,128)(2,1)S(1)}, f32[128,512]{1,0:T(8,128)S(1)}, f32[128,128]{1,0:T(8,128)S(1)}, bf16[128,128]{1,0:T(8,128)(2,1)S(1)}) custom-call(s32[1]{0:T(128)} %bitcast.core, s32[1]{0:T(128)} %bitcast.1.low, bf16[128,128]{1,0:T(8,128)(2,1)S(1)} %get-tuple-element.37.refs_0_, bf16[128,128]{1,0:T(8,128)(2,1)S(1)} %collective-permute-done.8.refs_1_, ...), custom_call_target="tpu_custom_call" | custom-call | bytes 458752 | tf_op jit(solution)/shard_map/pallas_call | solution.py:36
  69.4 3.1 %collective-permute-start.9 = (bf16[128,128]{1,0:T(8,128)(2,1)S(1)}, bf16[128,128]{1,0:T(8,128)(2,1)S(1)}, u32[]{:S(2)}, u32[]{:S(2)}) collective-permute-start(bf16[128,128]{1,0:T(8,128)(2,1)S(1)} %get-tuple-element.44), channel_id=1, source_target_pairs={{0,2},{2,0},{1,3},{3,1},{4,6},{6,4},{5,7},{7,5},{8,10},{10,8},{9,1... | collective-permute-start | bytes 98312 | tf_op jit(solution)/shard_map/ppermute | solution.py:273
  72.5 1.5 %shard_map.111.refs_0_ = f32[16,128,256]{2,1,0:T(8,128)S(1)} custom-call(s32[1]{0:T(128)} %bitcast.core, s32[1]{0:T(128)} %bitcast.1.low, bf16[2,4096,256]{2,1,0:T(8,128)(2,1)S(1)} %get-tuple-element.35.refs_0_, bf16[2,256,4096]{2,1,0:T(8,128)(2,1)S(1)} %get-tuple-element.36.refs_1_, bf16[128,512]{1,0:T(8,128)(2,1)S(1)} %get-tuple-element.39.refs_2_, ...), custom_call_target="tpu_custom_call" | custom-call | flops 1000000000 | bytes 8782336 | tf_op jit(solution)/shard_map/pallas_call | solution.py:36
  74.0 0.1 collective-permute-done.9.refs_10_
  74.1 0.7 shard_map.112
  74.8 16.7 %all_to_all.10.refs_2_ = bf16[8,2,128,256]{3,2,1,0:T(8,128)(2,1)S(1)} all-to-all(bf16[8,2,128,256]{3,2,1,0:T(8,128)(2,1)S(1)} %shard_map.112), channel_id=1, replica_groups=mesh['z'=16,'yh'=2,'x'=4,'yl'=2,'c'=2] {'x','yl'}, dimensions={0} | all-to-all | bytes 2097152 | tf_op jit(solution)/shard_map/all_to_all | solution.py:277
  91.4 0.2 shard_map.113
  91.6 6.0 %collective-permute-start.10 = (bf16[128,256]{1,0:T(8,128)(2,1)S(1)}, bf16[128,256]{1,0:T(8,128)(2,1)S(1)}, u32[]{:S(2)}, u32[]{:S(2)}) collective-permute-start(bf16[128,256]{1,0:T(8,128)(2,1)S(1)} %get-tuple-element.45), channel_id=1, source_target_pairs={{0,16},{1,497},{16,32},{17,1},{32,48},{33,17},{48,64},{49,33},{64,... | collective-permute-start | bytes 196616 | tf_op jit(solution)/shard_map/ppermute | solution.py:265
  97.6 5.2 %collective-permute-start.11 = (bf16[128,256]{1,0:T(8,128)(2,1)S(1)}, bf16[128,256]{1,0:T(8,128)(2,1)S(1)}, u32[]{:S(2)}, u32[]{:S(2)}) collective-permute-start(bf16[128,256]{1,0:T(8,128)(2,1)S(1)} %get-tuple-element.46), channel_id=1, source_target_pairs={{0,17},{1,496},{16,33},{17,0},{32,49},{33,16},{48,65},{49,32},{64,... | collective-permute-start | bytes 196616 | tf_op jit(solution)/shard_map/ppermute | solution.py:265
  102.8 4.0 %collective-permute-done.11.cross = bf16[128,256]{1,0:T(8,128)(2,1)S(1)} collective-permute-done((bf16[128,256]{1,0:T(8,128)(2,1)S(1)}, bf16[128,256]{1,0:T(8,128)(2,1)S(1)}, u32[]{:S(2)}, u32[]{:S(2)}) %collective-permute-start.11) | collective-permute-done | bytes 65568 | tf_op jit(solution)/shard_map/ppermute | solution.py:265
  106.8 0.7 shard_map.114
  (13 shorter events, 0.1 us)
Async XLA Ops:
  0.6 24.9 %collective-permute-start.2 = (bf16[64,4096]{1,0:T(8,128)(2,1)}, bf16[64,4096]{1,0:T(8,128)(2,1)S(1)}, u32[]{:S(2)}, u32[]{:S(2)}) collective-permute-start(bf16[64,4096]{1,0:T(8,128)(2,1)} %bitcast.9), channel_id=1, source_target_pairs={{0,0},{1,1},{2,4},{3,5},{4,8},{5,9},{6,12},{7,13},{8,2},{9,3},{10,... | collective-permute-start | bytes 1572872 | tf_op jit(solution)/shard_map/ppermute | solution.py:306
  3.9 21.6 %collective-permute-start.1 = (bf16[144,256]{1,0:T(8,128)(2,1)S(1)}, bf16[144,256]{1,0:T(8,128)(2,1)S(1)}, u32[]{:S(2)}, u32[]{:S(2)}) collective-permute-start(bf16[144,256]{1,0:T(8,128)(2,1)S(1)} %get-tuple-element.29), channel_id=1, source_target_pairs={{0,496},{16,480},{32,464},{48,448},{64,432},{80,416},{96,400},{112... | collective-permute-start | bytes 221192 | tf_op jit(solution)/shard_map/ppermute | solution.py:269
  18.5 3.8 %collective-permute-start = (bf16[128,256]{1,0:T(8,128)(2,1)S(1)}, bf16[128,256]{1,0:T(8,128)(2,1)S(1)}, u32[]{:S(2)}, u32[]{:S(2)}) collective-permute-start(bf16[128,256]{1,0:T(8,128)(2,1)S(1)} %get-tuple-element.28), channel_id=1, source_target_pairs={{0,1},{1,0},{2,3},{3,2},{4,5},{5,4},{6,7},{7,6},{8,9},{9,8},{10,11... | collective-permute-start | bytes 196616 | tf_op jit(solution)/shard_map/ppermute | solution.py:273
  26.8 28.6 %all-to-all-start = ((bf16[8,3,128,256]{3,2,1,0:T(8,128)(2,1)}), bf16[8,3,128,256]{3,2,1,0:T(8,128)(2,1)S(1)}, u32[]{:S(2)}, u32[]{:S(2)}) async-start(bf16[8,3,128,256]{3,2,1,0:T(8,128)(2,1)} %get-tuple-element.30), calls=%async_computation | async-start | bytes 3145728 | tf_op jit(solution)/shard_map/all_to_all | solution.py:277
  32.0 15.5 %collective-permute-start.3 = (bf16[128,256]{1,0:T(8,128)(2,1)S(1)}, bf16[128,256]{1,0:T(8,128)(2,1)S(1)}, u32[]{:S(2)}, u32[]{:S(2)}) collective-permute-start(bf16[128,256]{1,0:T(8,128)(2,1)S(1)} %get-tuple-element.31), channel_id=1, source_target_pairs={{0,496},{16,480},{32,464},{48,448},{64,432},{80,416},{96,400},{112... | collective-permute-start | bytes 196616 | tf_op jit(solution)/shard_map/ppermute | solution.py:269
  38.8 20.5 %collective-permute-start.6 = (bf16[256,4096]{1,0:T(8,128)(2,1)}, bf16[256,4096]{1,0:T(8,128)(2,1)}, u32[]{:S(2)}, u32[]{:S(2)}) collective-permute-start(bf16[256,4096]{1,0:T(8,128)(2,1)} %bitcast.5), channel_id=1, source_target_pairs={{0,1},{1,0},{2,3},{3,2},{4,5},{5,4},{6,7},{7,6},{8,9},{9,8},{10,11... | collective-permute-start | bytes 6291464 | tf_op jit(solution)/shard_map/ppermute | solution.py:273
  43.2 21.8 %collective-permute-start.7 = (bf16[4096,256]{1,0:T(8,128)(2,1)}, bf16[4096,256]{1,0:T(8,128)(2,1)}, u32[]{:S(2)}, u32[]{:S(2)}) collective-permute-start(bf16[4096,256]{1,0:T(8,128)(2,1)} %bitcast.7), channel_id=1, source_target_pairs={{0,1},{1,0},{2,3},{3,2},{4,5},{5,4},{6,7},{7,6},{8,9},{9,8},{10,11... | collective-permute-start | bytes 6291464 | tf_op jit(solution)/shard_map/ppermute | solution.py:273
  45.1 16.8 %collective-permute-start.5 = (bf16[64,4096]{1,0:T(8,128)(2,1)S(1)}, bf16[64,4096]{1,0:T(8,128)(2,1)S(1)}, u32[]{:S(2)}, u32[]{:S(2)}) collective-permute-start(bf16[64,4096]{1,0:T(8,128)(2,1)S(1)} %collective-permute-done.2.refs_4_.refs_3_), channel_id=1, source_target_pairs={{0,1},{1,0},{2,3},{3,2},{4,5},{5,4},{6,7},{7,6},{8,9},{9,8},{10,11... | collective-permute-start | bytes 1572872 | tf_op jit(solution)/shard_map/ppermute | solution.py:273
  55.5 3.9 %copy-start = (bf16[1,256,4096]{2,1,0:T(8,128)(2,1)S(1)}, bf16[1,256,4096]{2,1,0:T(8,128)(2,1)}, u32[]{:S(2)}) copy-start(bf16[1,256,4096]{2,1,0:T(8,128)(2,1)} %param.15) | copy-start | bytes 6291460
  55.5 6.5 %copy-start.2 = (f32[1,4096]{1,0:T(1,128)S(1)}, f32[1,4096]{1,0:T(1,128)}, u32[]{:S(2)}) copy-start(f32[1,4096]{1,0:T(1,128)} %refs_3_.1) | copy-start | bytes 49156
  55.5 6.4 %collective-permute-start.4 = (bf16[8,128,256]{2,1,0:T(8,128)(2,1)S(1)}, bf16[8,128,256]{2,1,0:T(8,128)(2,1)S(1)}, u32[]{:S(2)}, u32[]{:S(2)}) collective-permute-start(bf16[8,128,256]{2,1,0:T(8,128)(2,1)S(1)} %shard_map.106), channel_id=1, source_target_pairs={{0,1},{1,0},{2,3},{3,2},{4,5},{5,4},{6,7},{7,6},{8,9},{9,8},{10,11... | collective-permute-start | bytes 1572872 | tf_op jit(solution)/shard_map/ppermute | solution.py:273
  62.0 3.0 %copy-start.1 = (bf16[1,4096,256]{2,1,0:T(8,128)(2,1)S(1)}, bf16[1,4096,256]{2,1,0:T(8,128)(2,1)}, u32[]{:S(2)}) copy-start(bf16[1,4096,256]{2,1,0:T(8,128)(2,1)} %param.13) | copy-start | bytes 6291460
  63.0 4.7 %collective-permute-start.8 = (bf16[128,128]{1,0:T(8,128)(2,1)S(1)}, bf16[128,128]{1,0:T(8,128)(2,1)S(1)}, u32[]{:S(2)}, u32[]{:S(2)}) collective-permute-start(bf16[128,128]{1,0:T(8,128)(2,1)S(1)} %get-tuple-element.37.refs_0_), channel_id=1, source_target_pairs={{0,2},{2,0},{1,3},{3,1},{4,6},{6,4},{5,7},{7,5},{8,10},{10,8},{9,1... | collective-permute-start | bytes 98312 | tf_op jit(solution)/shard_map/ppermute | solution.py:273
  69.4 4.7 %collective-permute-start.9 = (bf16[128,128]{1,0:T(8,128)(2,1)S(1)}, bf16[128,128]{1,0:T(8,128)(2,1)S(1)}, u32[]{:S(2)}, u32[]{:S(2)}) collective-permute-start(bf16[128,128]{1,0:T(8,128)(2,1)S(1)} %get-tuple-element.44), channel_id=1, source_target_pairs={{0,2},{2,0},{1,3},{3,1},{4,6},{6,4},{5,7},{7,5},{8,10},{10,8},{9,1... | collective-permute-start | bytes 98312 | tf_op jit(solution)/shard_map/ppermute | solution.py:273
  91.6 11.2 %collective-permute-start.10 = (bf16[128,256]{1,0:T(8,128)(2,1)S(1)}, bf16[128,256]{1,0:T(8,128)(2,1)S(1)}, u32[]{:S(2)}, u32[]{:S(2)}) collective-permute-start(bf16[128,256]{1,0:T(8,128)(2,1)S(1)} %get-tuple-element.45), channel_id=1, source_target_pairs={{0,16},{1,497},{16,32},{17,1},{32,48},{33,17},{48,64},{49,33},{64,... | collective-permute-start | bytes 196616 | tf_op jit(solution)/shard_map/ppermute | solution.py:265
  97.6 9.2 %collective-permute-start.11 = (bf16[128,256]{1,0:T(8,128)(2,1)S(1)}, bf16[128,256]{1,0:T(8,128)(2,1)S(1)}, u32[]{:S(2)}, u32[]{:S(2)}) collective-permute-start(bf16[128,256]{1,0:T(8,128)(2,1)S(1)} %get-tuple-element.46), channel_id=1, source_target_pairs={{0,17},{1,496},{16,33},{17,0},{32,49},{33,16},{48,65},{49,32},{64,... | collective-permute-start | bytes 196616 | tf_op jit(solution)/shard_map/ppermute | solution.py:265

commit v7 on v6

--- a/solution.py
+++ b/solution.py
@@ -156,9 +156,13 @@
             dmixed[:, i * W : (i + 1) * W] = dot(g[...], cols[i], NT).astype(BF16)
 
 
+def stacked(x):
+    return jnp.concatenate([x[:, h * HEAD_DIM : (h + 1) * HEAD_DIM] for h in range(4)], axis=0)
+
+
 def softmax(qb, k):
-    row = lax.broadcasted_iota(jnp.int32, (T, T), 0)
-    col = lax.broadcasted_iota(jnp.int32, (T, T), 1)
+    row = lax.broadcasted_iota(jnp.int32, (4, T, T), 1).reshape(4 * T, T)
+    col = lax.broadcasted_iota(jnp.int32, (4 * T, T), 1)
     s = jnp.where(row >= col, dot(qb, k, NT) * SCALE, F32(-1e30))
     e = jnp.exp(s - jnp.max(s, axis=-1, keepdims=True))
     return e / jnp.sum(e, axis=-1, keepdims=True)
@@ -168,28 +172,27 @@
     keys = low[0] == 0
     k = jnp.where(keys, kvb[...], got[...])
     v = jnp.where(keys, got[...], kvb[...])
-
-    @pl.when(core[0] == 0)
-    def _():
+    qb = stacked(q[...]).astype(BF16)
+    p = softmax(qb, k)
+    pb = p.astype(BF16)
+
+    @pl.when(core[0] == 0)
+    def _():
+        out = dot(pb, v).astype(BF16)
         for h in range(4):
-            lanes = slice(h * HEAD_DIM, (h + 1) * HEAD_DIM)
-            p = softmax(q[:, lanes].astype(BF16), k)
-            mixed[:, lanes] = dot(p.astype(BF16), v).astype(BF16)
+            mixed[:, h * HEAD_DIM : (h + 1) * HEAD_DIM] = out[h * T : (h + 1) * T, :]
         away_out[...] = jnp.zeros((T, HEAD_DIM), BF16)
 
     @pl.when(core[0] == 1)
     def _():
-        dk, dv = 0.0, 0.0
+        dm = stacked(dmixed[...])
+        dprob = dot(dm, v, NT)
+        dscore = (p * (dprob - jnp.sum(p * dprob, axis=-1, keepdims=True))).astype(BF16)
+        out = dot(dscore, k) * SCALE
         for h in range(4):
-            lanes = slice(h * HEAD_DIM, (h + 1) * HEAD_DIM)
-            qb, dm = q[:, lanes].astype(BF16), dmixed[:, lanes]
-            p = softmax(qb, k)
-            dprob = dot(dm, v, NT)
-            dscore = (p * (dprob - jnp.sum(p * dprob, axis=-1, keepdims=True))).astype(BF16)
-            dq_out[:, lanes] = dot(dscore, k) * SCALE
-            dk += dot(dscore, qb, TN)
-            dv += dot(p.astype(BF16), dm, TN)
-        dk = dk * SCALE
+            dq_out[:, h * HEAD_DIM : (h + 1) * HEAD_DIM] = out[h * T : (h + 1) * T, :]
+        dk = dot(dscore, qb, TN) * SCALE
+        dv = dot(pb, dm, TN)
         own_out[...] = jnp.where(keys, dk, dv)
         away_out[...] = jnp.where(keys, dv, dk).astype(BF16)
 

time: 108 us -> 107 us (level)
  no operation moved by 1% of the time
where the time goes in v7:
time: 107 us
  starting transfers between devices  59.7 us (56%)
  blocking collectives  16.7 us (16%)
  waiting for transfers between devices  16.5 us (15%)
  Pallas kernels  12.3 us (11%)
  between operations  1.54 us (1%)
    ppermute x2, starting transfers between devices, mirror(): return lax.ppermute(block, SEC, [(i, 31 - i) for i in range(32)])  21.4 us
    ppermute x7, starting transfers between devices, swap(): return lax.ppermute(block, axis, [(0, 1), (1, 0)])  20.4 us
    all_to_all x1, blocking collectives, exchange(): return lax.all_to_all(parts, ('x', 'yl'), 0, 0, tiled=True)  16.7 us
    ppermute x2, starting transfers between devices, deliver(): return lax.ppermute(block, SEC + ('c',), route)  11.1 us
    pallas_call x10, Pallas kernels, call(): pl.pallas_call(ordered, out_shape=tuple((pltpu.VMEM(s, d) for s, d in out...  10.6 us
    all_to_all x1, waiting for transfers between devices, exchange(): return lax.all_to_all(parts, ('x', 'yl'), 0, 0, tiled=True)  7.93 us
    all_to_all x1, starting transfers between devices, exchange(): return lax.all_to_all(parts, ('x', 'yl'), 0, 0, tiled=True)  5.19 us
    ppermute x2, waiting for transfers between devices, deliver(): return lax.ppermute(block, SEC + ('c',), route)  4.04 us
  transfers between devices with their start and end apart: 13, of which 6 were waited for; matrix products, arithmetic and copies ran while one was open for 0% of the time, Pallas kernels for 8%

profile of v7, /device:TPU:1, one launch (start us, length us, event | category | flops | bytes accessed | tf_op | source)
XLA Modules:
  0.0 106.7 jit_solution(11438188029837875813)
XLA Ops:
  0.6 1.7 %collective-permute-start.2 = (bf16[64,4096]{1,0:T(8,128)(2,1)}, bf16[64,4096]{1,0:T(8,128)(2,1)S(1)}, u32[]{:S(2)}, u32[]{:S(2)}) collective-permute-start(bf16[64,4096]{1,0:T(8,128)(2,1)} %bitcast.9), channel_id=1, source_target_pairs={{0,0},{1,1},{2,4},{3,5},{4,8},{5,9},{6,12},{7,13},{8,2},{9,3},{10,... | collective-permute-start | bytes 1572872 | tf_op jit(solution)/shard_map/ppermute | solution.py:309
  3.0 0.9 shard_map.103
  3.9 14.6 %collective-permute-start.1 = (bf16[144,256]{1,0:T(8,128)(2,1)S(1)}, bf16[144,256]{1,0:T(8,128)(2,1)S(1)}, u32[]{:S(2)}, u32[]{:S(2)}) collective-permute-start(bf16[144,256]{1,0:T(8,128)(2,1)S(1)} %get-tuple-element.29), channel_id=1, source_target_pairs={{0,496},{16,480},{32,464},{48,448},{64,432},{80,416},{96,400},{112... | collective-permute-start | bytes 221192 | tf_op jit(solution)/shard_map/ppermute | solution.py:272
  18.5 2.9 %collective-permute-start = (bf16[128,256]{1,0:T(8,128)(2,1)S(1)}, bf16[128,256]{1,0:T(8,128)(2,1)S(1)}, u32[]{:S(2)}, u32[]{:S(2)}) collective-permute-start(bf16[128,256]{1,0:T(8,128)(2,1)S(1)} %get-tuple-element.28), channel_id=1, source_target_pairs={{0,1},{1,0},{2,3},{3,2},{4,5},{5,4},{6,7},{7,6},{8,9},{9,8},{10,11... | collective-permute-start | bytes 196616 | tf_op jit(solution)/shard_map/ppermute | solution.py:276
  21.4 0.9 collective-permute-done.refs_1_
  22.3 3.2 %collective-permute-done.1.refs_2_ = bf16[144,256]{1,0:T(8,128)(2,1)S(1)} collective-permute-done((bf16[144,256]{1,0:T(8,128)(2,1)S(1)}, bf16[144,256]{1,0:T(8,128)(2,1)S(1)}, u32[]{:S(2)}, u32[]{:S(2)}) %collective-permute-start.1) | collective-permute-done | bytes 73760 | tf_op jit(solution)/shard_map/ppermute | solution.py:272
  25.5 1.3 %shard_map.105 = (bf16[8,3,128,256]{3,2,1,0:T(8,128)(2,1)}, bf16[128,256]{1,0:T(8,128)(2,1)S(1)}) custom-call(s32[1]{0:T(128)} %bitcast.core, s32[1]{0:T(128)} %bitcast.1.low, bf16[128,256]{1,0:T(8,128)(2,1)S(1)} %get-tuple-element.27.refs_0_, bf16[128,256]{1,0:T(8,128)(2,1)S(1)} %collective-permute-done.refs_1_, ...), custom_call_target="tpu_custom_call" | custom-call | bytes 270336 | tf_op jit(solution)/shard_map/pallas_call | solution.py:36
  26.8 5.2 %all-to-all-start = ((bf16[8,3,128,256]{3,2,1,0:T(8,128)(2,1)}), bf16[8,3,128,256]{3,2,1,0:T(8,128)(2,1)S(1)}, u32[]{:S(2)}, u32[]{:S(2)}) async-start(bf16[8,3,128,256]{3,2,1,0:T(8,128)(2,1)} %get-tuple-element.30), calls=%async_computation | async-start | bytes 3145728 | tf_op jit(solution)/shard_map/all_to_all | solution.py:280
  32.0 6.8 %collective-permute-start.3 = (bf16[128,256]{1,0:T(8,128)(2,1)S(1)}, bf16[128,256]{1,0:T(8,128)(2,1)S(1)}, u32[]{:S(2)}, u32[]{:S(2)}) collective-permute-start(bf16[128,256]{1,0:T(8,128)(2,1)S(1)} %get-tuple-element.31), channel_id=1, source_target_pairs={{0,496},{16,480},{32,464},{48,448},{64,432},{80,416},{96,400},{112... | collective-permute-start | bytes 196616 | tf_op jit(solution)/shard_map/ppermute | solution.py:272
  38.8 4.3 %collective-permute-start.6 = (bf16[256,4096]{1,0:T(8,128)(2,1)}, bf16[256,4096]{1,0:T(8,128)(2,1)}, u32[]{:S(2)}, u32[]{:S(2)}) collective-permute-start(bf16[256,4096]{1,0:T(8,128)(2,1)} %bitcast.5), channel_id=1, source_target_pairs={{0,1},{1,0},{2,3},{3,2},{4,5},{5,4},{6,7},{7,6},{8,9},{9,8},{10,11... | collective-permute-start | bytes 6291464 | tf_op jit(solution)/shard_map/ppermute | solution.py:276
  43.2 1.9 %collective-permute-start.7 = (bf16[4096,256]{1,0:T(8,128)(2,1)}, bf16[4096,256]{1,0:T(8,128)(2,1)}, u32[]{:S(2)}, u32[]{:S(2)}) collective-permute-start(bf16[4096,256]{1,0:T(8,128)(2,1)} %bitcast.7), channel_id=1, source_target_pairs={{0,1},{1,0},{2,3},{3,2},{4,5},{5,4},{6,7},{7,6},{8,9},{9,8},{10,11... | collective-permute-start | bytes 6291464 | tf_op jit(solution)/shard_map/ppermute | solution.py:276
  45.1 2.4 %collective-permute-start.5 = (bf16[64,4096]{1,0:T(8,128)(2,1)S(1)}, bf16[64,4096]{1,0:T(8,128)(2,1)S(1)}, u32[]{:S(2)}, u32[]{:S(2)}) collective-permute-start(bf16[64,4096]{1,0:T(8,128)(2,1)S(1)} %collective-permute-done.2.refs_4_.refs_3_), channel_id=1, source_target_pairs={{0,1},{1,0},{2,3},{3,2},{4,5},{5,4},{6,7},{7,6},{8,9},{9,8},{10,11... | collective-permute-start | bytes 1572872 | tf_op jit(solution)/shard_map/ppermute | solution.py:276
  47.6 7.9 %all-to-all-done.refs_0_.refs_1_ = bf16[8,3,128,256]{3,2,1,0:T(8,128)(2,1)S(1)} async-done(((bf16[8,3,128,256]{3,2,1,0:T(8,128)(2,1)}), bf16[8,3,128,256]{3,2,1,0:T(8,128)(2,1)S(1)}, u32[]{:S(2)}, u32[]{:S(2)}) %all-to-all-start) | async-done | bytes 1572896 | tf_op jit(solution)/shard_map/all_to_all | solution.py:280
  55.5 0.0 copy-start.2
  55.5 3.8 %collective-permute-start.4 = (bf16[8,128,256]{2,1,0:T(8,128)(2,1)S(1)}, bf16[8,128,256]{2,1,0:T(8,128)(2,1)S(1)}, u32[]{:S(2)}, u32[]{:S(2)}) collective-permute-start(bf16[8,128,256]{2,1,0:T(8,128)(2,1)S(1)} %shard_map.106), channel_id=1, source_target_pairs={{0,1},{1,0},{2,3},{3,2},{4,5},{5,4},{6,7},{7,6},{8,9},{9,8},{10,11... | collective-permute-start | bytes 1572872 | tf_op jit(solution)/shard_map/ppermute | solution.py:276
  59.4 2.6 %shard_map.107 = (bf16[128,512]{1,0:T(8,128)(2,1)S(1)}, bf16[2,256,4096]{2,1,0:T(8,128)(2,1)S(1)}) custom-call(s32[1]{0:T(128)} %bitcast.core, s32[1]{0:T(128)} %bitcast.1.low, bf16[8,3,128,256]{3,2,1,0:T(8,128)(2,1)S(1)} %all-to-all-done.refs_0_.refs_1_, bf16[256,4096]{1,0:T(8,128)(2,1)S(1)} %bitcast.6, bf16[256,4096]{1,0:T(8,128)(2,1)} %collective-permute-done.6.refs_2_), custom_call_target="tpu_custom_call" | custom-call | flops 1000000000 | bytes 1572864 | tf_op jit(solution)/shard_map/pallas_call | solution.py:36
  62.0 0.0 copy-start.1
  62.0 1.0 shard_map.108
  63.0 1.9 %collective-permute-start.8 = (bf16[128,128]{1,0:T(8,128)(2,1)S(1)}, bf16[128,128]{1,0:T(8,128)(2,1)S(1)}, u32[]{:S(2)}, u32[]{:S(2)}) collective-permute-start(bf16[128,128]{1,0:T(8,128)(2,1)S(1)} %get-tuple-element.37.refs_0_), channel_id=1, source_target_pairs={{0,2},{2,0},{1,3},{3,1},{4,6},{6,4},{5,7},{7,5},{8,10},{10,8},{9,1... | collective-permute-start | bytes 98312 | tf_op jit(solution)/shard_map/ppermute | solution.py:276
  65.0 2.4 %shard_map.109 = (f32[128,512]{1,0:T(8,128)S(1)}, bf16[2,4096,256]{2,1,0:T(8,128)(2,1)S(1)}) custom-call(s32[1]{0:T(128)} %bitcast.core, s32[1]{0:T(128)} %bitcast.1.low, bf16[128,4096]{1,0:T(8,128)(2,1)S(1)} %get-tuple-element.33.refs_0_, f32[128,1]{1,0:T(8,128)S(1)} %get-tuple-element.34.refs_1_.refs_4_.refs_5_, bf16[4096,256]{1,0:T(8,128)(2,1)S(1)} %bitcast.8, ...), custom_call_target="tpu_custom_call" | custom-call | flops 1000000000 | bytes 1049088 | tf_op jit(solution)/shard_map/pallas_call | solution.py:36
  67.4 0.3 collective-permute-done.8.refs_1_
  67.7 0.9 shard_map.110
  68.6 3.1 %collective-permute-start.9 = (bf16[128,128]{1,0:T(8,128)(2,1)S(1)}, bf16[128,128]{1,0:T(8,128)(2,1)S(1)}, u32[]{:S(2)}, u32[]{:S(2)}) collective-permute-start(bf16[128,128]{1,0:T(8,128)(2,1)S(1)} %get-tuple-element.44), channel_id=1, source_target_pairs={{0,2},{2,0},{1,3},{3,1},{4,6},{6,4},{5,7},{7,5},{8,10},{10,8},{9,1... | collective-permute-start | bytes 98312 | tf_op jit(solution)/shard_map/ppermute | solution.py:276
  71.7 1.5 %shard_map.111.refs_0_ = f32[16,128,256]{2,1,0:T(8,128)S(1)} custom-call(s32[1]{0:T(128)} %bitcast.core, s32[1]{0:T(128)} %bitcast.1.low, bf16[2,4096,256]{2,1,0:T(8,128)(2,1)S(1)} %get-tuple-element.35.refs_0_, bf16[2,256,4096]{2,1,0:T(8,128)(2,1)S(1)} %get-tuple-element.36.refs_1_, bf16[128,512]{1,0:T(8,128)(2,1)S(1)} %get-tuple-element.39.refs_2_, ...), custom_call_target="tpu_custom_call" | custom-call | flops 1000000000 | bytes 8782336 | tf_op jit(solution)/shard_map/pallas_call | solution.py:36
  73.2 0.1 collective-permute-done.9.refs_10_
  73.3 0.7 shard_map.112
  74.0 16.7 %all_to_all.10.refs_2_ = bf16[8,2,128,256]{3,2,1,0:T(8,128)(2,1)S(1)} all-to-all(bf16[8,2,128,256]{3,2,1,0:T(8,128)(2,1)S(1)} %shard_map.112), channel_id=1, replica_groups=mesh['z'=16,'yh'=2,'x'=4,'yl'=2,'c'=2] {'x','yl'}, dimensions={0} | all-to-all | bytes 2097152 | tf_op jit(solution)/shard_map/all_to_all | solution.py:280
  90.7 0.2 shard_map.113
  90.9 5.9 %collective-permute-start.10 = (bf16[128,256]{1,0:T(8,128)(2,1)S(1)}, bf16[128,256]{1,0:T(8,128)(2,1)S(1)}, u32[]{:S(2)}, u32[]{:S(2)}) collective-permute-start(bf16[128,256]{1,0:T(8,128)(2,1)S(1)} %get-tuple-element.45), channel_id=1, source_target_pairs={{0,16},{1,497},{16,32},{17,1},{32,48},{33,17},{48,64},{49,33},{64,... | collective-permute-start | bytes 196616 | tf_op jit(solution)/shard_map/ppermute | solution.py:268
  96.8 5.1 %collective-permute-start.11 = (bf16[128,256]{1,0:T(8,128)(2,1)S(1)}, bf16[128,256]{1,0:T(8,128)(2,1)S(1)}, u32[]{:S(2)}, u32[]{:S(2)}) collective-permute-start(bf16[128,256]{1,0:T(8,128)(2,1)S(1)} %get-tuple-element.46), channel_id=1, source_target_pairs={{0,17},{1,496},{16,33},{17,0},{32,49},{33,16},{48,65},{49,32},{64,... | collective-permute-start | bytes 196616 | tf_op jit(solution)/shard_map/ppermute | solution.py:268
  102.0 4.0 %collective-permute-done.11.cross = bf16[128,256]{1,0:T(8,128)(2,1)S(1)} collective-permute-done((bf16[128,256]{1,0:T(8,128)(2,1)S(1)}, bf16[128,256]{1,0:T(8,128)(2,1)S(1)}, u32[]{:S(2)}, u32[]{:S(2)}) %collective-permute-start.11) | collective-permute-done | bytes 65568 | tf_op jit(solution)/shard_map/ppermute | solution.py:268
  106.0 0.7 shard_map.114
  (13 shorter events, 0.1 us)
Async XLA Ops:
  0.6 24.9 %collective-permute-start.2 = (bf16[64,4096]{1,0:T(8,128)(2,1)}, bf16[64,4096]{1,0:T(8,128)(2,1)S(1)}, u32[]{:S(2)}, u32[]{:S(2)}) collective-permute-start(bf16[64,4096]{1,0:T(8,128)(2,1)} %bitcast.9), channel_id=1, source_target_pairs={{0,0},{1,1},{2,4},{3,5},{4,8},{5,9},{6,12},{7,13},{8,2},{9,3},{10,... | collective-permute-start | bytes 1572872 | tf_op jit(solution)/shard_map/ppermute | solution.py:309
  3.9 21.6 %collective-permute-start.1 = (bf16[144,256]{1,0:T(8,128)(2,1)S(1)}, bf16[144,256]{1,0:T(8,128)(2,1)S(1)}, u32[]{:S(2)}, u32[]{:S(2)}) collective-permute-start(bf16[144,256]{1,0:T(8,128)(2,1)S(1)} %get-tuple-element.29), channel_id=1, source_target_pairs={{0,496},{16,480},{32,464},{48,448},{64,432},{80,416},{96,400},{112... | collective-permute-start | bytes 221192 | tf_op jit(solution)/shard_map/ppermute | solution.py:272
  18.5 3.8 %collective-permute-start = (bf16[128,256]{1,0:T(8,128)(2,1)S(1)}, bf16[128,256]{1,0:T(8,128)(2,1)S(1)}, u32[]{:S(2)}, u32[]{:S(2)}) collective-permute-start(bf16[128,256]{1,0:T(8,128)(2,1)S(1)} %get-tuple-element.28), channel_id=1, source_target_pairs={{0,1},{1,0},{2,3},{3,2},{4,5},{5,4},{6,7},{7,6},{8,9},{9,8},{10,11... | collective-permute-start | bytes 196616 | tf_op jit(solution)/shard_map/ppermute | solution.py:276
  26.8 28.6 %all-to-all-start = ((bf16[8,3,128,256]{3,2,1,0:T(8,128)(2,1)}), bf16[8,3,128,256]{3,2,1,0:T(8,128)(2,1)S(1)}, u32[]{:S(2)}, u32[]{:S(2)}) async-start(bf16[8,3,128,256]{3,2,1,0:T(8,128)(2,1)} %get-tuple-element.30), calls=%async_computation | async-start | bytes 3145728 | tf_op jit(solution)/shard_map/all_to_all | solution.py:280
  32.0 15.5 %collective-permute-start.3 = (bf16[128,256]{1,0:T(8,128)(2,1)S(1)}, bf16[128,256]{1,0:T(8,128)(2,1)S(1)}, u32[]{:S(2)}, u32[]{:S(2)}) collective-permute-start(bf16[128,256]{1,0:T(8,128)(2,1)S(1)} %get-tuple-element.31), channel_id=1, source_target_pairs={{0,496},{16,480},{32,464},{48,448},{64,432},{80,416},{96,400},{112... | collective-permute-start | bytes 196616 | tf_op jit(solution)/shard_map/ppermute | solution.py:272
  38.8 20.5 %collective-permute-start.6 = (bf16[256,4096]{1,0:T(8,128)(2,1)}, bf16[256,4096]{1,0:T(8,128)(2,1)}, u32[]{:S(2)}, u32[]{:S(2)}) collective-permute-start(bf16[256,4096]{1,0:T(8,128)(2,1)} %bitcast.5), channel_id=1, source_target_pairs={{0,1},{1,0},{2,3},{3,2},{4,5},{5,4},{6,7},{7,6},{8,9},{9,8},{10,11... | collective-permute-start | bytes 6291464 | tf_op jit(solution)/shard_map/ppermute | solution.py:276
  43.2 21.8 %collective-permute-start.7 = (bf16[4096,256]{1,0:T(8,128)(2,1)}, bf16[4096,256]{1,0:T(8,128)(2,1)}, u32[]{:S(2)}, u32[]{:S(2)}) collective-permute-start(bf16[4096,256]{1,0:T(8,128)(2,1)} %bitcast.7), channel_id=1, source_target_pairs={{0,1},{1,0},{2,3},{3,2},{4,5},{5,4},{6,7},{7,6},{8,9},{9,8},{10,11... | collective-permute-start | bytes 6291464 | tf_op jit(solution)/shard_map/ppermute | solution.py:276
  45.1 16.8 %collective-permute-start.5 = (bf16[64,4096]{1,0:T(8,128)(2,1)S(1)}, bf16[64,4096]{1,0:T(8,128)(2,1)S(1)}, u32[]{:S(2)}, u32[]{:S(2)}) collective-permute-start(bf16[64,4096]{1,0:T(8,128)(2,1)S(1)} %collective-permute-done.2.refs_4_.refs_3_), channel_id=1, source_target_pairs={{0,1},{1,0},{2,3},{3,2},{4,5},{5,4},{6,7},{7,6},{8,9},{9,8},{10,11... | collective-permute-start | bytes 1572872 | tf_op jit(solution)/shard_map/ppermute | solution.py:276
  55.5 3.9 %copy-start = (bf16[1,256,4096]{2,1,0:T(8,128)(2,1)S(1)}, bf16[1,256,4096]{2,1,0:T(8,128)(2,1)}, u32[]{:S(2)}) copy-start(bf16[1,256,4096]{2,1,0:T(8,128)(2,1)} %param.15) | copy-start | bytes 6291460
  55.5 6.5 %copy-start.2 = (f32[1,4096]{1,0:T(1,128)S(1)}, f32[1,4096]{1,0:T(1,128)}, u32[]{:S(2)}) copy-start(f32[1,4096]{1,0:T(1,128)} %refs_3_.1) | copy-start | bytes 49156
  55.5 6.4 %collective-permute-start.4 = (bf16[8,128,256]{2,1,0:T(8,128)(2,1)S(1)}, bf16[8,128,256]{2,1,0:T(8,128)(2,1)S(1)}, u32[]{:S(2)}, u32[]{:S(2)}) collective-permute-start(bf16[8,128,256]{2,1,0:T(8,128)(2,1)S(1)} %shard_map.106), channel_id=1, source_target_pairs={{0,1},{1,0},{2,3},{3,2},{4,5},{5,4},{6,7},{7,6},{8,9},{9,8},{10,11... | collective-permute-start | bytes 1572872 | tf_op jit(solution)/shard_map/ppermute | solution.py:276
  62.0 3.0 %copy-start.1 = (bf16[1,4096,256]{2,1,0:T(8,128)(2,1)S(1)}, bf16[1,4096,256]{2,1,0:T(8,128)(2,1)}, u32[]{:S(2)}) copy-start(bf16[1,4096,256]{2,1,0:T(8,128)(2,1)} %param.13) | copy-start | bytes 6291460
  63.0 4.7 %collective-permute-start.8 = (bf16[128,128]{1,0:T(8,128)(2,1)S(1)}, bf16[128,128]{1,0:T(8,128)(2,1)S(1)}, u32[]{:S(2)}, u32[]{:S(2)}) collective-permute-start(bf16[128,128]{1,0:T(8,128)(2,1)S(1)} %get-tuple-element.37.refs_0_), channel_id=1, source_target_pairs={{0,2},{2,0},{1,3},{3,1},{4,6},{6,4},{5,7},{7,5},{8,10},{10,8},{9,1... | collective-permute-start | bytes 98312 | tf_op jit(solution)/shard_map/ppermute | solution.py:276
  68.6 4.7 %collective-permute-start.9 = (bf16[128,128]{1,0:T(8,128)(2,1)S(1)}, bf16[128,128]{1,0:T(8,128)(2,1)S(1)}, u32[]{:S(2)}, u32[]{:S(2)}) collective-permute-start(bf16[128,128]{1,0:T(8,128)(2,1)S(1)} %get-tuple-element.44), channel_id=1, source_target_pairs={{0,2},{2,0},{1,3},{3,1},{4,6},{6,4},{5,7},{7,5},{8,10},{10,8},{9,1... | collective-permute-start | bytes 98312 | tf_op jit(solution)/shard_map/ppermute | solution.py:276
  90.9 11.1 %collective-permute-start.10 = (bf16[128,256]{1,0:T(8,128)(2,1)S(1)}, bf16[128,256]{1,0:T(8,128)(2,1)S(1)}, u32[]{:S(2)}, u32[]{:S(2)}) collective-permute-start(bf16[128,256]{1,0:T(8,128)(2,1)S(1)} %get-tuple-element.45), channel_id=1, source_target_pairs={{0,16},{1,497},{16,32},{17,1},{32,48},{33,17},{48,64},{49,33},{64,... | collective-permute-start | bytes 196616 | tf_op jit(solution)/shard_map/ppermute | solution.py:268
  96.8 9.2 %collective-permute-start.11 = (bf16[128,256]{1,0:T(8,128)(2,1)S(1)}, bf16[128,256]{1,0:T(8,128)(2,1)S(1)}, u32[]{:S(2)}, u32[]{:S(2)}) collective-permute-start(bf16[128,256]{1,0:T(8,128)(2,1)S(1)} %get-tuple-element.46), channel_id=1, source_target_pairs={{0,17},{1,496},{16,33},{17,0},{32,49},{33,16},{48,65},{49,32},{64,... | collective-permute-start | bytes 196616 | tf_op jit(solution)/shard_map/ppermute | solution.py:268

commit v8 on v7

--- a/solution.py
+++ b/solution.py
@@ -54,15 +54,13 @@
     return pl.ds(pl.multiple_of(index * size, size), size)
 
 
-def load_kernel(slot, store, x, g, held, x_out, g_out, sems):
+def load_kernel(x, g, x_out, g_out, sems):
     copies = [
-        pltpu.make_async_copy(store.at[0, slot[0]], held.at[:T, :], sems.at[0]),
-        pltpu.make_async_copy(x.at[0], x_out, sems.at[1]),
-        pltpu.make_async_copy(g.at[0], g_out, sems.at[2]),
+        pltpu.make_async_copy(x.at[0], x_out, sems.at[0]),
+        pltpu.make_async_copy(g.at[0], g_out, sems.at[1]),
     ]
     for copy in copies:
         copy.start()
-    held[T:, :] = jnp.zeros((PAD, W), BF16)
     for copy in copies:
         copy.wait()
 
@@ -79,12 +77,15 @@
         away[...] = x[...]
 
 
-def spread_kernel(core, low, base, twin, fetched, x, out, x_out):
+def spread_kernel(core, base, twin, fetched, x, _, out, x_out, sem):
+    copies = []
+    for j in range(8):
+        for i, ref in ((core[0], base), (1 - core[0], twin), (2, fetched.at[:T, :])):
+            copies.append(pltpu.make_async_copy(ref, out.at[j, i], sem.at[len(copies)]))
+            copies[-1].start()
     x_out[...] = x[...]
-    for j in range(8):
-        out[j, core[0]] = base[...]
-        out[j, 1 - core[0]] = twin[...]
-        out[j, 2] = fetched[:T, :]
+    for copy in copies:
+        copy.wait()
 
 
 def pick_kernel(core, low, own, out):
@@ -290,14 +291,16 @@
     vmem = pl.BlockSpec(memory_space=pltpu.VMEM)
     small = pltpu.CompilerParams(vmem_limit_bytes=6 * 2**20)
 
-    held, x, g = pl.pallas_call(
+    held = lax.dynamic_index_in_dim(mirror_store[0], fetch_slot[0], 0, keepdims=False)
+    held = jnp.pad(held, ((0, PAD), (0, 0)))
+    x, g = pl.pallas_call(
         load_kernel,
-        out_shape=tuple(pltpu.VMEM((rows, W), BF16) for rows in (T + PAD, T, T)),
-        in_specs=[smem] + [pl.BlockSpec(memory_space=pl.ANY)] * 3,
-        out_specs=(vmem,) * 3,
-        scratch_shapes=[pltpu.SemaphoreType.DMA((3,))],
+        out_shape=tuple(pltpu.VMEM((T, W), BF16) for _ in range(2)),
+        in_specs=[pl.BlockSpec(memory_space=pl.ANY)] * 2,
+        out_specs=(vmem,) * 2,
+        scratch_shapes=[pltpu.SemaphoreType.DMA((2,))],
         compiler_params=small,
-    )(fetch_slot, *(in_hbm(a) for a in (mirror_store, section_input, section_grad)))
+    )(*(in_hbm(a) for a in (section_input, section_grad)))
     fetched = mirror(held)
     base, away = call(trade_kernel, [tile, tile], place, x, g)
     base_twin = swap(away, "c")
@@ -309,16 +312,15 @@
     first = lax.ppermute(keyval_w, TEN, route)
     twin = swap(first, "c")
 
-    spread, x_late = call(
+    parts = [pltpu.with_memory_space_constraint(a, pltpu.VMEM) for a in (base, base_twin, fetched, x)]
+    spread, x_late = pl.pallas_call(
         spread_kernel,
-        [((8, 3, T, W), BF16), tile],
-        place,
-        base,
-        base_twin,
-        fetched,
-        x,
-        after=(first,),
-    )
+        out_shape=(pltpu.HBM((8, 3, T, W), BF16), pltpu.VMEM((T, W), BF16)),
+        in_specs=[smem] + [vmem] * 4 + [pl.BlockSpec(memory_space=pl.ANY)],
+        out_specs=(pl.BlockSpec(memory_space=pl.ANY), vmem),
+        scratch_shapes=[pltpu.SemaphoreType.DMA((24,))],
+        compiler_params=small,
+    )(place[0], *parts, first)
     own = exchange(spread)
     evicted = mirror(x_late)
     wq2, wo2 = swap(wq, "c"), swap(wo, "c")

time: 107 us -> 108 us (level)
  starting transfers between devices: 59.7 us -> 60.8 us
    pallas_call x10 -> x9, Pallas kernels: 10.6 us -> 9.28 us  [call(): pl.pallas_call(ordered, out_shape=tuple((pltpu.VMEM(s, d) for s, d in out...]
    pallas_call x1 -> x2, Pallas kernels: 0.93 us -> 2.28 us  [the longest x1 1.39 us: body(): pl.pallas_call(spread_kernel, out_shape=(pltpu.HBM((8, 3, T, W), BF16), p...]
where the time goes in v8:
time: 108 us; the launch traced here: 107 us
  starting transfers between devices  60.8 us (56%)
  blocking collectives  16.7 us (15%)
  waiting for transfers between devices  15.6 us (14%)
  Pallas kernels  12.3 us (11%)
  between operations  1.58 us (1%)
    ppermute x2, starting transfers between devices, mirror(): return lax.ppermute(block, SEC, [(i, 31 - i) for i in range(32)])  22.3 us
    ppermute x7, starting transfers between devices, swap(): return lax.ppermute(block, axis, [(0, 1), (1, 0)])  20.3 us
    all_to_all x1, blocking collectives, exchange(): return lax.all_to_all(parts, ('x', 'yl'), 0, 0, tiled=True)  16.7 us
    ppermute x2, starting transfers between devices, deliver(): return lax.ppermute(block, SEC + ('c',), route)  11.1 us
    pallas_call x9, Pallas kernels, call(): pl.pallas_call(ordered, out_shape=tuple((pltpu.VMEM(s, d) for s, d in out...  9.28 us
    all_to_all x1, waiting for transfers between devices, exchange(): return lax.all_to_all(parts, ('x', 'yl'), 0, 0, tiled=True)  7.07 us
    all_to_all x1, starting transfers between devices, exchange(): return lax.all_to_all(parts, ('x', 'yl'), 0, 0, tiled=True)  5.21 us
    ppermute x2, waiting for transfers between devices, deliver(): return lax.ppermute(block, SEC + ('c',), route)  4.93 us
  transfers between devices with their start and end apart: 13, of which 6 were waited for; matrix products, arithmetic and copies ran while one was open for 0% of the time, Pallas kernels for 8%

profile of v8, /device:TPU:1, one launch (start us, length us, event | category | flops | bytes accessed | tf_op | source)
XLA Modules:
  0.0 106.9 jit_solution(576580878419527543)
XLA Ops:
  0.6 0.0 copy-start
  0.6 1.8 %collective-permute-start.2 = (bf16[64,4096]{1,0:T(8,128)(2,1)}, bf16[64,4096]{1,0:T(8,128)(2,1)S(1)}, u32[]{:S(2)}, u32[]{:S(2)}) collective-permute-start(bf16[64,4096]{1,0:T(8,128)(2,1)} %bitcast.15), channel_id=1, source_target_pairs={{0,0},{1,1},{2,4},{3,5},{4,8},{5,9},{6,12},{7,13},{8,2},{9,3},{10,... | collective-permute-start | bytes 1572872 | tf_op jit(solution)/shard_map/ppermute | solution.py:312
  3.2 14.6 %collective-permute-start.1 = (bf16[144,256]{1,0:T(8,128)(2,1)S(1)}, bf16[144,256]{1,0:T(8,128)(2,1)S(1)}, u32[]{:S(2)}, u32[]{:S(2)}) collective-permute-start(bf16[144,256]{1,0:T(8,128)(2,1)S(1)} %pad.4), channel_id=1, source_target_pairs={{0,496},{16,480},{32,464},{48,448},{64,432},{80,416},{96,400},{112... | collective-permute-start | bytes 221192 | tf_op jit(solution)/shard_map/ppermute | solution.py:273
  17.8 0.9 shard_map.103
  18.7 2.9 %collective-permute-start = (bf16[128,256]{1,0:T(8,128)(2,1)S(1)}, bf16[128,256]{1,0:T(8,128)(2,1)S(1)}, u32[]{:S(2)}, u32[]{:S(2)}) collective-permute-start(bf16[128,256]{1,0:T(8,128)(2,1)S(1)} %get-tuple-element.27), channel_id=1, source_target_pairs={{0,1},{1,0},{2,3},{3,2},{4,5},{5,4},{6,7},{7,6},{8,9},{9,8},{10,11... | collective-permute-start | bytes 196616 | tf_op jit(solution)/shard_map/ppermute | solution.py:277
  21.6 0.9 collective-permute-done.twin.refs_1_
  22.5 2.3 %collective-permute-done.1.fetched = bf16[144,256]{1,0:T(8,128)(2,1)S(1)} collective-permute-done((bf16[144,256]{1,0:T(8,128)(2,1)S(1)}, bf16[144,256]{1,0:T(8,128)(2,1)S(1)}, u32[]{:S(2)}, u32[]{:S(2)}) %collective-permute-start.1) | collective-permute-done | bytes 73760 | tf_op jit(solution)/shard_map/ppermute | solution.py:273
  24.8 1.4 %shard_map.105 = (bf16[8,3,128,256]{3,2,1,0:T(8,128)(2,1)}, bf16[128,256]{1,0:T(8,128)(2,1)S(1)}) custom-call(s32[1]{0:T(128)} %bitcast.core, bf16[128,256]{1,0:T(8,128)(2,1)S(1)} %get-tuple-element.26.base.refs_0_, bf16[128,256]{1,0:T(8,128)(2,1)S(1)} %collective-permute-done.twin.refs_1_, bf16[144,256]{1,0:T(8,128)(2,1)S(1)} %collective-permute-done.1.fetched, ...), custom_call_target="tpu_custom_call" | custom-call | tf_op jit(solution)/shard_map/pallas_call | solution.py:316
  26.2 5.2 %all-to-all-start = ((bf16[8,3,128,256]{3,2,1,0:T(8,128)(2,1)}), bf16[8,3,128,256]{3,2,1,0:T(8,128)(2,1)S(1)}, u32[]{:S(2)}, u32[]{:S(2)}) async-start(bf16[8,3,128,256]{3,2,1,0:T(8,128)(2,1)} %get-tuple-element.28), calls=%async_computation | async-start | bytes 3145728 | tf_op jit(solution)/shard_map/all_to_all | solution.py:281
  31.4 7.7 %collective-permute-start.3 = (bf16[128,256]{1,0:T(8,128)(2,1)S(1)}, bf16[128,256]{1,0:T(8,128)(2,1)S(1)}, u32[]{:S(2)}, u32[]{:S(2)}) collective-permute-start(bf16[128,256]{1,0:T(8,128)(2,1)S(1)} %get-tuple-element.29), channel_id=1, source_target_pairs={{0,496},{16,480},{32,464},{48,448},{64,432},{80,416},{96,400},{112... | collective-permute-start | bytes 196616 | tf_op jit(solution)/shard_map/ppermute | solution.py:273
  39.1 4.3 %collective-permute-start.6 = (bf16[256,4096]{1,0:T(8,128)(2,1)}, bf16[256,4096]{1,0:T(8,128)(2,1)}, u32[]{:S(2)}, u32[]{:S(2)}) collective-permute-start(bf16[256,4096]{1,0:T(8,128)(2,1)} %bitcast.11), channel_id=1, source_target_pairs={{0,1},{1,0},{2,3},{3,2},{4,5},{5,4},{6,7},{7,6},{8,9},{9,8},{10,11... | collective-permute-start | bytes 6291464 | tf_op jit(solution)/shard_map/ppermute | solution.py:277
  43.4 1.9 %collective-permute-start.7 = (bf16[4096,256]{1,0:T(8,128)(2,1)}, bf16[4096,256]{1,0:T(8,128)(2,1)}, u32[]{:S(2)}, u32[]{:S(2)}) collective-permute-start(bf16[4096,256]{1,0:T(8,128)(2,1)} %bitcast.13), channel_id=1, source_target_pairs={{0,1},{1,0},{2,3},{3,2},{4,5},{5,4},{6,7},{7,6},{8,9},{9,8},{10,11... | collective-permute-start | bytes 6291464 | tf_op jit(solution)/shard_map/ppermute | solution.py:277
  45.4 2.4 %collective-permute-start.5 = (bf16[64,4096]{1,0:T(8,128)(2,1)S(1)}, bf16[64,4096]{1,0:T(8,128)(2,1)S(1)}, u32[]{:S(2)}, u32[]{:S(2)}) collective-permute-start(bf16[64,4096]{1,0:T(8,128)(2,1)S(1)} %collective-permute-done.2._.refs_3_), channel_id=1, source_target_pairs={{0,1},{1,0},{2,3},{3,2},{4,5},{5,4},{6,7},{7,6},{8,9},{9,8},{10,11... | collective-permute-start | bytes 1572872 | tf_op jit(solution)/shard_map/ppermute | solution.py:277
  47.8 7.1 %all-to-all-done.refs_0_.refs_1_ = bf16[8,3,128,256]{3,2,1,0:T(8,128)(2,1)S(1)} async-done(((bf16[8,3,128,256]{3,2,1,0:T(8,128)(2,1)}), bf16[8,3,128,256]{3,2,1,0:T(8,128)(2,1)S(1)}, u32[]{:S(2)}, u32[]{:S(2)}) %all-to-all-start) | async-done | bytes 1572896 | tf_op jit(solution)/shard_map/all_to_all | solution.py:281
  54.9 3.8 %collective-permute-start.4 = (bf16[8,128,256]{2,1,0:T(8,128)(2,1)S(1)}, bf16[8,128,256]{2,1,0:T(8,128)(2,1)S(1)}, u32[]{:S(2)}, u32[]{:S(2)}) collective-permute-start(bf16[8,128,256]{2,1,0:T(8,128)(2,1)S(1)} %shard_map.106), channel_id=1, source_target_pairs={{0,1},{1,0},{2,3},{3,2},{4,5},{5,4},{6,7},{7,6},{8,9},{9,8},{10,11... | collective-permute-start | bytes 1572872 | tf_op jit(solution)/shard_map/ppermute | solution.py:277
  58.7 2.6 %shard_map.107 = (bf16[128,512]{1,0:T(8,128)(2,1)S(1)}, bf16[2,256,4096]{2,1,0:T(8,128)(2,1)S(1)}) custom-call(s32[1]{0:T(128)} %bitcast.core, s32[1]{0:T(128)} %bitcast.1.low, bf16[8,3,128,256]{3,2,1,0:T(8,128)(2,1)S(1)} %all-to-all-done.refs_0_.refs_1_, bf16[256,4096]{1,0:T(8,128)(2,1)S(1)} %bitcast.12, bf16[256,4096]{1,0:T(8,128)(2,1)} %collective-permute-done.6.refs_2_), custom_call_target="tpu_custom_call" | custom-call | flops 1000000000 | bytes 1572864 | tf_op jit(solution)/shard_map/pallas_call | solution.py:36
  61.3 0.0 copy-start.2
  61.4 1.0 shard_map.108
  62.4 1.9 %collective-permute-start.8 = (bf16[128,128]{1,0:T(8,128)(2,1)S(1)}, bf16[128,128]{1,0:T(8,128)(2,1)S(1)}, u32[]{:S(2)}, u32[]{:S(2)}) collective-permute-start(bf16[128,128]{1,0:T(8,128)(2,1)S(1)} %get-tuple-element.35.refs_0_), channel_id=1, source_target_pairs={{0,2},{2,0},{1,3},{3,1},{4,6},{6,4},{5,7},{7,5},{8,10},{10,8},{9,1... | collective-permute-start | bytes 98312 | tf_op jit(solution)/shard_map/ppermute | solution.py:277
  64.3 2.4 %shard_map.109 = (f32[128,512]{1,0:T(8,128)S(1)}, bf16[2,4096,256]{2,1,0:T(8,128)(2,1)S(1)}) custom-call(s32[1]{0:T(128)} %bitcast.core, s32[1]{0:T(128)} %bitcast.1.low, bf16[128,4096]{1,0:T(8,128)(2,1)S(1)} %get-tuple-element.31.refs_0_, f32[128,1]{1,0:T(8,128)S(1)} %get-tuple-element.32.refs_1_.refs_4_.refs_5_, bf16[4096,256]{1,0:T(8,128)(2,1)S(1)} %bitcast.14, ...), custom_call_target="tpu_custom_call" | custom-call | flops 1000000000 | bytes 1049088 | tf_op jit(solution)/shard_map/pallas_call | solution.py:36
  66.8 0.3 collective-permute-done.8.refs_1_
  67.1 0.9 shard_map.110
  68.0 3.1 %collective-permute-start.9 = (bf16[128,128]{1,0:T(8,128)(2,1)S(1)}, bf16[128,128]{1,0:T(8,128)(2,1)S(1)}, u32[]{:S(2)}, u32[]{:S(2)}) collective-permute-start(bf16[128,128]{1,0:T(8,128)(2,1)S(1)} %get-tuple-element.42), channel_id=1, source_target_pairs={{0,2},{2,0},{1,3},{3,1},{4,6},{6,4},{5,7},{7,5},{8,10},{10,8},{9,1... | collective-permute-start | bytes 98312 | tf_op jit(solution)/shard_map/ppermute | solution.py:277
  71.1 1.5 %shard_map.111.refs_0_ = f32[16,128,256]{2,1,0:T(8,128)S(1)} custom-call(s32[1]{0:T(128)} %bitcast.core, s32[1]{0:T(128)} %bitcast.1.low, bf16[2,4096,256]{2,1,0:T(8,128)(2,1)S(1)} %get-tuple-element.33.refs_0_, bf16[2,256,4096]{2,1,0:T(8,128)(2,1)S(1)} %get-tuple-element.34.refs_1_, bf16[128,512]{1,0:T(8,128)(2,1)S(1)} %get-tuple-element.37.refs_2_, ...), custom_call_target="tpu_custom_call" | custom-call | flops 1000000000 | bytes 8782336 | tf_op jit(solution)/shard_map/pallas_call | solution.py:36
  72.6 0.1 collective-permute-done.9.refs_10_
  72.7 0.6 shard_map.112
  73.3 16.7 %all_to_all.10.refs_2_ = bf16[8,2,128,256]{3,2,1,0:T(8,128)(2,1)S(1)} all-to-all(bf16[8,2,128,256]{3,2,1,0:T(8,128)(2,1)S(1)} %shard_map.112), channel_id=1, replica_groups=mesh['z'=16,'yh'=2,'x'=4,'yl'=2,'c'=2] {'x','yl'}, dimensions={0} | all-to-all | bytes 2097152 | tf_op jit(solution)/shard_map/all_to_all | solution.py:281
  90.0 0.2 shard_map.113
  90.1 6.9 %collective-permute-start.10 = (bf16[128,256]{1,0:T(8,128)(2,1)S(1)}, bf16[128,256]{1,0:T(8,128)(2,1)S(1)}, u32[]{:S(2)}, u32[]{:S(2)}) collective-permute-start(bf16[128,256]{1,0:T(8,128)(2,1)S(1)} %get-tuple-element.43), channel_id=1, source_target_pairs={{0,16},{1,497},{16,32},{17,1},{32,48},{33,17},{48,64},{49,33},{64,... | collective-permute-start | bytes 196616 | tf_op jit(solution)/shard_map/ppermute | solution.py:269
  97.0 4.3 %collective-permute-start.11 = (bf16[128,256]{1,0:T(8,128)(2,1)S(1)}, bf16[128,256]{1,0:T(8,128)(2,1)S(1)}, u32[]{:S(2)}, u32[]{:S(2)}) collective-permute-start(bf16[128,256]{1,0:T(8,128)(2,1)S(1)} %get-tuple-element.44), channel_id=1, source_target_pairs={{0,17},{1,496},{16,33},{17,0},{32,49},{33,16},{48,65},{49,32},{64,... | collective-permute-start | bytes 196616 | tf_op jit(solution)/shard_map/ppermute | solution.py:269
  101.3 4.9 %collective-permute-done.11.cross = bf16[128,256]{1,0:T(8,128)(2,1)S(1)} collective-permute-done((bf16[128,256]{1,0:T(8,128)(2,1)S(1)}, bf16[128,256]{1,0:T(8,128)(2,1)S(1)}, u32[]{:S(2)}, u32[]{:S(2)}) %collective-permute-start.11) | collective-permute-done | bytes 65568 | tf_op jit(solution)/shard_map/ppermute | solution.py:269
  106.2 0.7 shard_map.114
  (17 shorter events, 0.1 us)
Async XLA Ops:
  0.6 2.5 %copy-start = (bf16[1,2,128,256]{3,2,1,0:T(8,128)(2,1)S(1)}, bf16[1,2,128,256]{3,2,1,0:T(8,128)(2,1)}, u32[]{:S(2)}) copy-start(bf16[1,2,128,256]{3,2,1,0:T(8,128)(2,1)} %param.10) | copy-start | bytes 393220
  0.6 24.2 %collective-permute-start.2 = (bf16[64,4096]{1,0:T(8,128)(2,1)}, bf16[64,4096]{1,0:T(8,128)(2,1)S(1)}, u32[]{:S(2)}, u32[]{:S(2)}) collective-permute-start(bf16[64,4096]{1,0:T(8,128)(2,1)} %bitcast.15), channel_id=1, source_target_pairs={{0,0},{1,1},{2,4},{3,5},{4,8},{5,9},{6,12},{7,13},{8,2},{9,3},{10,... | collective-permute-start | bytes 1572872 | tf_op jit(solution)/shard_map/ppermute | solution.py:312
  3.2 21.6 %collective-permute-start.1 = (bf16[144,256]{1,0:T(8,128)(2,1)S(1)}, bf16[144,256]{1,0:T(8,128)(2,1)S(1)}, u32[]{:S(2)}, u32[]{:S(2)}) collective-permute-start(bf16[144,256]{1,0:T(8,128)(2,1)S(1)} %pad.4), channel_id=1, source_target_pairs={{0,496},{16,480},{32,464},{48,448},{64,432},{80,416},{96,400},{112... | collective-permute-start | bytes 221192 | tf_op jit(solution)/shard_map/ppermute | solution.py:273
  18.7 3.8 %collective-permute-start = (bf16[128,256]{1,0:T(8,128)(2,1)S(1)}, bf16[128,256]{1,0:T(8,128)(2,1)S(1)}, u32[]{:S(2)}, u32[]{:S(2)}) collective-permute-start(bf16[128,256]{1,0:T(8,128)(2,1)S(1)} %get-tuple-element.27), channel_id=1, source_target_pairs={{0,1},{1,0},{2,3},{3,2},{4,5},{5,4},{6,7},{7,6},{8,9},{9,8},{10,11... | collective-permute-start | bytes 196616 | tf_op jit(solution)/shard_map/ppermute | solution.py:277
  26.2 28.7 %all-to-all-start = ((bf16[8,3,128,256]{3,2,1,0:T(8,128)(2,1)}), bf16[8,3,128,256]{3,2,1,0:T(8,128)(2,1)S(1)}, u32[]{:S(2)}, u32[]{:S(2)}) async-start(bf16[8,3,128,256]{3,2,1,0:T(8,128)(2,1)} %get-tuple-element.28), calls=%async_computation | async-start | bytes 3145728 | tf_op jit(solution)/shard_map/all_to_all | solution.py:281
  31.4 16.4 %collective-permute-start.3 = (bf16[128,256]{1,0:T(8,128)(2,1)S(1)}, bf16[128,256]{1,0:T(8,128)(2,1)S(1)}, u32[]{:S(2)}, u32[]{:S(2)}) collective-permute-start(bf16[128,256]{1,0:T(8,128)(2,1)S(1)} %get-tuple-element.29), channel_id=1, source_target_pairs={{0,496},{16,480},{32,464},{48,448},{64,432},{80,416},{96,400},{112... | collective-permute-start | bytes 196616 | tf_op jit(solution)/shard_map/ppermute | solution.py:273
  39.1 19.6 %collective-permute-start.6 = (bf16[256,4096]{1,0:T(8,128)(2,1)}, bf16[256,4096]{1,0:T(8,128)(2,1)}, u32[]{:S(2)}, u32[]{:S(2)}) collective-permute-start(bf16[256,4096]{1,0:T(8,128)(2,1)} %bitcast.11), channel_id=1, source_target_pairs={{0,1},{1,0},{2,3},{3,2},{4,5},{5,4},{6,7},{7,6},{8,9},{9,8},{10,11... | collective-permute-start | bytes 6291464 | tf_op jit(solution)/shard_map/ppermute | solution.py:277
  43.4 20.9 %collective-permute-start.7 = (bf16[4096,256]{1,0:T(8,128)(2,1)}, bf16[4096,256]{1,0:T(8,128)(2,1)}, u32[]{:S(2)}, u32[]{:S(2)}) collective-permute-start(bf16[4096,256]{1,0:T(8,128)(2,1)} %bitcast.13), channel_id=1, source_target_pairs={{0,1},{1,0},{2,3},{3,2},{4,5},{5,4},{6,7},{7,6},{8,9},{9,8},{10,11... | collective-permute-start | bytes 6291464 | tf_op jit(solution)/shard_map/ppermute | solution.py:277
  45.4 16.0 %collective-permute-start.5 = (bf16[64,4096]{1,0:T(8,128)(2,1)S(1)}, bf16[64,4096]{1,0:T(8,128)(2,1)S(1)}, u32[]{:S(2)}, u32[]{:S(2)}) collective-permute-start(bf16[64,4096]{1,0:T(8,128)(2,1)S(1)} %collective-permute-done.2._.refs_3_), channel_id=1, source_target_pairs={{0,1},{1,0},{2,3},{3,2},{4,5},{5,4},{6,7},{7,6},{8,9},{9,8},{10,11... | collective-permute-start | bytes 1572872 | tf_op jit(solution)/shard_map/ppermute | solution.py:277
  54.9 3.9 %copy-start.1 = (bf16[1,256,4096]{2,1,0:T(8,128)(2,1)S(1)}, bf16[1,256,4096]{2,1,0:T(8,128)(2,1)}, u32[]{:S(2)}) copy-start(bf16[1,256,4096]{2,1,0:T(8,128)(2,1)} %param.15) | copy-start | bytes 6291460
  54.9 6.5 %copy-start.3 = (f32[1,4096]{1,0:T(1,128)S(1)}, f32[1,4096]{1,0:T(1,128)}, u32[]{:S(2)}) copy-start(f32[1,4096]{1,0:T(1,128)} %refs_3_.1) | copy-start | bytes 49156
  54.9 6.4 %collective-permute-start.4 = (bf16[8,128,256]{2,1,0:T(8,128)(2,1)S(1)}, bf16[8,128,256]{2,1,0:T(8,128)(2,1)S(1)}, u32[]{:S(2)}, u32[]{:S(2)}) collective-permute-start(bf16[8,128,256]{2,1,0:T(8,128)(2,1)S(1)} %shard_map.106), channel_id=1, source_target_pairs={{0,1},{1,0},{2,3},{3,2},{4,5},{5,4},{6,7},{7,6},{8,9},{9,8},{10,11... | collective-permute-start | bytes 1572872 | tf_op jit(solution)/shard_map/ppermute | solution.py:277
  61.3 3.0 %copy-start.2 = (bf16[1,4096,256]{2,1,0:T(8,128)(2,1)S(1)}, bf16[1,4096,256]{2,1,0:T(8,128)(2,1)}, u32[]{:S(2)}) copy-start(bf16[1,4096,256]{2,1,0:T(8,128)(2,1)} %param.13) | copy-start | bytes 6291460
  62.4 4.7 %collective-permute-start.8 = (bf16[128,128]{1,0:T(8,128)(2,1)S(1)}, bf16[128,128]{1,0:T(8,128)(2,1)S(1)}, u32[]{:S(2)}, u32[]{:S(2)}) collective-permute-start(bf16[128,128]{1,0:T(8,128)(2,1)S(1)} %get-tuple-element.35.refs_0_), channel_id=1, source_target_pairs={{0,2},{2,0},{1,3},{3,1},{4,6},{6,4},{5,7},{7,5},{8,10},{10,8},{9,1... | collective-permute-start | bytes 98312 | tf_op jit(solution)/shard_map/ppermute | solution.py:277
  68.0 4.7 %collective-permute-start.9 = (bf16[128,128]{1,0:T(8,128)(2,1)S(1)}, bf16[128,128]{1,0:T(8,128)(2,1)S(1)}, u32[]{:S(2)}, u32[]{:S(2)}) collective-permute-start(bf16[128,128]{1,0:T(8,128)(2,1)S(1)} %get-tuple-element.42), channel_id=1, source_target_pairs={{0,2},{2,0},{1,3},{3,1},{4,6},{6,4},{5,7},{7,5},{8,10},{10,8},{9,1... | collective-permute-start | bytes 98312 | tf_op jit(solution)/shard_map/ppermute | solution.py:277
  90.1 11.1 %collective-permute-start.10 = (bf16[128,256]{1,0:T(8,128)(2,1)S(1)}, bf16[128,256]{1,0:T(8,128)(2,1)S(1)}, u32[]{:S(2)}, u32[]{:S(2)}) collective-permute-start(bf16[128,256]{1,0:T(8,128)(2,1)S(1)} %get-tuple-element.43), channel_id=1, source_target_pairs={{0,16},{1,497},{16,32},{17,1},{32,48},{33,17},{48,64},{49,33},{64,... | collective-permute-start | bytes 196616 | tf_op jit(solution)/shard_map/ppermute | solution.py:269
  97.0 9.2 %collective-permute-start.11 = (bf16[128,256]{1,0:T(8,128)(2,1)S(1)}, bf16[128,256]{1,0:T(8,128)(2,1)S(1)}, u32[]{:S(2)}, u32[]{:S(2)}) collective-permute-start(bf16[128,256]{1,0:T(8,128)(2,1)S(1)} %get-tuple-element.44), channel_id=1, source_target_pairs={{0,17},{1,496},{16,33},{17,0},{32,49},{33,16},{48,65},{49,32},{64,... | collective-permute-start | bytes 196616 | tf_op jit(solution)/shard_map/ppermute | solution.py:269
